TPU v7x, 32 devices: a whole 2x2x4 slice. The times are simulated.
32 devices in a mesh: expert: 8 (over z, x), replica: 4 (over y, core).
Axes of the slice: x: 2, y: 2, z: 4, core: 2. Of those that a mesh axis runs over, the one named last changes fastest.
Arguments:
- tokens: bfloat16 [8192, 1024], P(('expert', 'replica')), may hold values from -6 to 6
- route: int32 [32, 256], P(('expert', 'replica')), may hold values from 0 to 255, each once within a row
- w_qkv: bfloat16 [1024, 3072], P(('expert', 'replica')), may hold values from -0.1875 to 0.1875
- w_attn_out: bfloat16 [1024, 1024], P(('expert', 'replica')), may hold values from -1 to 1
- w_up: bfloat16 [1024, 4096], P(('expert', 'replica')), may hold values from -0.1875 to 0.1875
- w_down: bfloat16 [4096, 1024], P(('expert', 'replica')), may hold values from -0.09375 to 0.09375
- gain_attn: bfloat16 [1024], P(('expert', 'replica')), may hold values from 0.25 to 1.75
- gain_ffn: bfloat16 [1024], P(('expert', 'replica')), may hold values from 0.25 to 1.75
- expert_in: bfloat16 [8, 1024, 4096], P('expert'), may hold values from -0.1875 to 0.1875
- expert_out: bfloat16 [8, 4096, 1024], P('expert'), may hold values from -0.09375 to 0.09375
- centroids: bfloat16 [8, 1024], P('expert'), may hold values from -0.09375 to 0.09375
- expert_gain: bfloat16 [8, 1024], P('expert'), may hold values from 0.25 to 1.75
- cotangent: bfloat16 [8192, 1024], P(('expert', 'replica')), may hold values from -6 to 6
Outputs:
- mixed: bfloat16 [8192, 1024], P(('expert', 'replica'))
- grad_tokens: float32 [8192, 1024], P(('expert', 'replica'))
- grad_qkv: float32 [1024, 3072], P(('expert', 'replica'))
- grad_attn_out: float32 [1024, 1024], P(('expert', 'replica'))
- grad_up: float32 [1024, 4096], P(('expert', 'replica'))
- grad_down: float32 [4096, 1024], P(('expert', 'replica'))
- grad_gain_attn: float32 [1024], P(('expert', 'replica'))
- grad_gain_ffn: float32 [1024], P(('expert', 'replica'))
- grad_expert_in: float32 [8, 1024, 4096], P('expert', 'replica')
- grad_expert_out: float32 [8, 4096, 1024], P('expert', 'replica')
- grad_centroids: float32 [8, 1024], P('expert', 'replica')
- grad_expert_gain: float32 [8, 1024], P('expert', 'replica')
Inputs may be any that keep to these rules, and one draw needn't show every extreme that they name: `route`: each row is a permutation of 0 to 255.
All inputs are finite; a program needn't handle non-finite values.
Results may differ from a plain program's by a relative error of at most 0.015.
Values may be sent and summed in bfloat16 or wider, within the bound.
No kernel may reach another device: no remote copies, remote signals or barrier semaphores. Data moves between devices by JAX's collectives and lax.ppermute only.
A program may use at most 256 MiB of HBM per device.

v0:
```python
import functools
import math

import jax
import jax.numpy as jnp
from jax import lax
from jax.experimental import pallas as pl
from jax.experimental.pallas import tpu as pltpu
from jax.sharding import PartitionSpec as P

HEADS = 16
EPSILON = 1e-05
ALL_AXES = ("expert", "replica")
VMEM_LIMIT = 58 * 2**20
GELU_SCALE = math.sqrt(2.0 / math.pi)
BF16, F32 = jnp.bfloat16, jnp.float32


def permuted(values, target):
    n_dev = lax.axis_size("expert") * lax.axis_size("replica")
    return lax.ppermute(values, ALL_AXES, [(d, target(d, n_dev)) for d in range(n_dev)])


def swap_core(values):
    return permuted(values, lambda d, n: d ^ 1)


def swap_first(values):
    return permuted(values, lambda d, n: d ^ (2 if d % 2 else 4))


def swap_second(values):
    return permuted(values, lambda d, n: d ^ (4 if d % 2 else 2))


def swap_x(values):
    return permuted(values, lambda d, n: d ^ 4)


def swap_y(values):
    return permuted(values, lambda d, n: d ^ 2)


def swap_plane(values, bit):
    return permuted(values, lambda d, n: d ^ (8 * bit))


def after(values, *earlier):
    return lax.optimization_barrier((values,) + earlier)[0]


HINT = 30


def body_name(body):
    return getattr(body, "func", body).__name__


def run_kernel(body, args, spaces, outs, scratch=(), flops=0, out_spaces=None):
    place = {
        "v": pl.BlockSpec(memory_space=pltpu.VMEM),
        "h": pl.BlockSpec(memory_space=pl.ANY),
        "s": pl.BlockSpec(memory_space=pltpu.SMEM),
    }
    moved = sum(a.size * a.dtype.itemsize for a in args)
    moved += sum(o.size * o.dtype.itemsize for o in outs)
    return pl.pallas_call(
        body,
        name=body_name(body),
        out_shape=list(outs),
        in_specs=[place[s] for s in spaces],
        out_specs=[place[s] for s in (out_spaces or "v" * len(outs))],
        scratch_shapes=list(scratch),
        cost_estimate=pl.CostEstimate(flops=int(flops * HINT), bytes_accessed=int(moved * HINT), transcendentals=0),
        compiler_params=pltpu.CompilerParams(vmem_limit_bytes=VMEM_LIMIT),
    )(*args)


def shaped(*shape, dtype=BF16):
    return jax.ShapeDtypeStruct(shape, dtype)


def dot_nn(left, right):
    return jnp.dot(left, right, preferred_element_type=F32)


def dot_nt(left, right):
    return lax.dot_general(left, right, (((1,), (1,)), ((), ())), preferred_element_type=F32)


def dot_tn(left, right):
    return lax.dot_general(left, right, (((0,), (0,)), ((), ())), preferred_element_type=F32)


def normed(values):
    centered = values - jnp.mean(values, axis=-1, keepdims=True)
    inverse = lax.rsqrt(jnp.mean(centered * centered, axis=-1, keepdims=True) + EPSILON)
    return centered * inverse, inverse


def norm_back(grad_normed, norm, inverse):
    return inverse * (
        grad_normed
        - jnp.mean(grad_normed, axis=-1, keepdims=True)
        - norm * jnp.mean(grad_normed * norm, axis=-1, keepdims=True)
    )


def gelu_both(values):
    square = values * values
    bent = jnp.tanh(GELU_SCALE * values * (1.0 + 0.044715 * square))
    half = 0.5 * (1.0 + bent)
    slope = half + 0.5 * values * (1.0 - bent * bent) * (
        GELU_SCALE * (1.0 + 3.0 * 0.044715 * square)
    )
    return values * half, slope


def row_start(pos, core, first, second, step, n_planes, block):
    x, y = pos[1], pos[2]
    flip = lambda v, on: 1 - v if on else v
    across = jnp.where(core == 0, flip(x, first), flip(x, second))
    along = jnp.where(core == 0, flip(y, second), flip(y, first))
    plane = pos[0] ^ step
    return pl.multiple_of(((plane * 2 + across) * 2 + along) * block, block)


PIECE_ORDER = ((0, 0), (1, 0), (0, 1), (1, 1))


def load_weight(pos, sides, target, sems, n_planes, by_plane):
    block = target.shape[0] // (4 * n_planes)
    part = n_planes // 2
    order = [(far, *chip) for far in range(2) for chip in PIECE_ORDER]
    copies = []
    for side, pieces in enumerate(sides):
        half = pieces[0].shape[1]
        core = pos[3] if side == 0 else 1 - pos[3]
        lanes = pl.ds(pl.multiple_of(core * half, 128), half)
        spots = [(piece, at) for piece in pieces for at in range(0, piece.shape[0], block * part)]
        for (far, first, second), (piece, at) in zip(order, spots, strict=True):
            for step in range(part):
                row = row_start(pos, core, first, second, far * part + step, n_planes, block)
                copies.append(
                    (
                        far * part + step if by_plane else side,
                        pltpu.make_async_copy(
                            piece.at[pl.ds(at + step * block, block), :],
                            target.at[pl.ds(row, block), lanes],
                            sems.at[far * part + step] if by_plane else sems.at[core],
                        ),
                    )
                )
    for _, copy in sorted(copies, key=lambda pair: pair[0]):
        copy.start()


def wait_half(target, core, sems):
    half = target.at[:, : target.shape[1] // 2]
    pltpu.make_async_copy(half, half, sems.at[core]).wait()


def wait_step(pos, target, sems, step, n_planes):
    rows = target.shape[0] // n_planes
    part = target.at[:rows, :]
    pltpu.make_async_copy(part, part, sems.at[step]).wait()
    return pl.multiple_of((pos[0] ^ step) * rows, rows)


def wait_whole(target, sem):
    pltpu.make_async_copy(target, target, sem).wait()


def causal_mask(length):
    return lax.broadcasted_iota(jnp.int32, (length, length), 0) >= lax.broadcasted_iota(
        jnp.int32, (length, length), 1
    )


def take_sides(refs, split):
    mine, both = split[0], sum(split)
    return (refs[:mine], refs[mine:both]), refs[both:]


def attend_kernel(n_planes, split, pos, tokens, *refs):
    sides, refs = take_sides(refs, split)
    hidden, ffn_in, attn_in, qkv, heads, gains, weight, sem = refs
    length, width = tokens.shape
    load_weight(pos, sides, weight, sem, n_planes, False)
    inputs = tokens[...].astype(F32)
    norm, _ = normed(inputs)
    wait_half(weight, 1, sem)
    columns = weight[:, 4 * width : 4 * width + 128].astype(F32)
    gains[...] = columns.T[:8]
    attn_in[...] = (norm * gains[0:1, :]).astype(BF16)
    wait_half(weight, 0, sem)
    for part in range(3):
        lanes = slice(part * width, (part + 1) * width)
        qkv[:, lanes] = dot_nn(attn_in[...], weight[:, lanes]).astype(BF16)
    head_size = width // HEADS
    causal = causal_mask(length)
    lane = lax.broadcasted_iota(jnp.int32, (1, 2 * head_size), 1)

    def pair(i, _):
        at = pl.multiple_of(i * 2 * head_size, 2 * head_size)
        query = qkv[:, pl.ds(at, 2 * head_size)] * (head_size**-0.5)
        key_rows = qkv[:, pl.ds(width + at, 2 * head_size)]
        value_rows = qkv[:, pl.ds(2 * width + at, 2 * head_size)]
        mixed = []
        for head in range(2):
            own = (lane // head_size) == head
            scores = dot_nt(jnp.where(own, query, 0).astype(BF16), key_rows)
            scores = jnp.where(causal, scores, -1e30)
            shifted = jnp.exp(scores - jnp.max(scores, axis=-1, keepdims=True))
            probs = shifted / jnp.sum(shifted, axis=-1, keepdims=True)
            mixed.append(dot_nn(probs.astype(BF16), value_rows))
        heads[:, pl.ds(at, 2 * head_size)] = jnp.where(lane < head_size, mixed[0], mixed[1]).astype(
            BF16
        )
        return 0

    lax.fori_loop(0, HEADS // 2, pair, 0)
    hidden[...] = inputs + dot_nn(heads[...], weight[:, 3 * width : 4 * width])
    norm_two, _ = normed(hidden[...])
    ffn_in[...] = (norm_two * gains[1:2, :]).astype(BF16)


def up_kernel(n_planes, split, pos, ffn_in, *refs):
    sides, (act, slope, weight, sem) = take_sides(refs, split)
    load_weight(pos, sides, weight, sem, n_planes, False)
    chunk = 512
    half = weight.shape[1] // 2
    for side in range(2):
        core = pos[3] if side == 0 else 1 - pos[3]
        wait_half(weight, core, sem)
        for i in range(half // chunk):
            lanes = pl.ds(pl.multiple_of(core * half + i * chunk, chunk), chunk)
            value, grad = gelu_both(dot_nn(ffn_in[...], weight[:, lanes]))
            act[:, lanes] = value.astype(BF16)
            slope[:, lanes] = grad


def down_kernel(n_planes, split, pos, act, hidden, pick, *refs):
    sides, (dense_out, sent, weight, sem) = take_sides(refs, split)
    load_weight(pos, sides, weight, sem, n_planes, True)
    rows = weight.shape[0] // n_planes
    total = hidden[...]
    for step in range(n_planes):
        at = pl.ds(wait_step(pos, weight, sem, step, n_planes), rows)
        total = total + dot_nn(act[:, at], weight[at, :])
    dense_out[...] = total
    sent[...] = dot_nn(pick[...], total.astype(BF16)).astype(BF16)


def expert_kernel(
    pos,
    arrived,
    grad_delta,
    centroid,
    norm_gain,
    weight_in,
    weight_out,
    delta,
    grad_rows,
    norm_low,
    kept,
    sent_low,
    sent_high,
    whole_low,
    grad_pre,
    vectors,
    w_in,
    w_out,
    act,
    slope,
    sems,
):
    chunk = 512
    n_chunks = w_in.shape[1] // chunk
    spans = [pl.ds(i * chunk, chunk) for i in range(n_chunks)]
    copies_in = [
        pltpu.make_async_copy(weight_in.at[0, :, span], w_in.at[:, span], sems.at[0, i])
        for i, span in enumerate(spans)
    ]
    copies_out = [
        pltpu.make_async_copy(weight_out.at[0, span, :], w_out.at[span, :], sems.at[1, i])
        for i, span in enumerate(spans)
    ]
    for copy in copies_in + copies_out:
        copy.start()
    rows = arrived[...].astype(F32)
    center = centroid[...].astype(F32)
    gain = norm_gain[...].astype(F32)
    gate = jax.nn.sigmoid(jnp.sum(rows * center, axis=-1, keepdims=True))
    norm, inverse = normed(rows)
    norm_low[...] = (norm * gain).astype(BF16)
    grad_out = grad_delta[...].astype(F32)
    grad_whole = gate * grad_out
    whole_low[...] = grad_whole.astype(BF16)
    for copy, span in zip(copies_in, spans):
        copy.wait()
        value, grad = gelu_both(dot_nn(norm_low[...], w_in[:, span]))
        act[:, span] = value.astype(BF16)
        slope[:, span] = grad
    half = act.shape[1] // 2
    kept[:, :half] = act[:, pl.ds(pl.multiple_of(pos[2] * half, 128), half)]
    other = pl.multiple_of((1 - pos[2]) * half, 128)
    sent_low[...] = act[:, pl.ds(other, half // 2)]
    sent_high[...] = act[:, pl.ds(pl.multiple_of(other + half // 2, 128), half // 2)]
    kept[:, half:] = whole_low[...]
    for copy in copies_out:
        copy.wait()
    whole = rows + dot_nn(act[...], w_out[...])
    delta[...] = (gate * whole).astype(BF16)
    grad_gate = jnp.sum(grad_out * whole, axis=-1, keepdims=True)
    grad_logit = grad_gate * gate * (1.0 - gate)

    for span in spans:
        grad_act = dot_nt(whole_low[...], w_out[span, :])
        grad_pre[:, span] = (grad_act * slope[:, span]).astype(BF16)
    grad_norm = dot_nt(grad_pre[...], w_in[...])
    vectors[...] = jnp.zeros_like(vectors)
    vectors[0:1, :] = jnp.sum(grad_logit * rows, axis=0, keepdims=True)
    vectors[1:2, :] = jnp.sum(grad_norm * norm, axis=0, keepdims=True)
    back = norm_back(grad_norm * gain, norm, inverse)
    grad_rows[...] = (grad_whole + grad_logit * center + back).astype(BF16)


VECTOR_ROWS = 16


def put_vectors(target, at, one, two):
    width = one.shape[1]
    row = lax.broadcasted_iota(jnp.int32, (VECTOR_ROWS, width), 0)
    both = jnp.where(row == 0, one, jnp.where(row == 1, two, 0.0))
    target[at : at + VECTOR_ROWS, :] = jnp.zeros((VECTOR_ROWS, target.shape[1]), BF16)
    target[at : at + VECTOR_ROWS, :width] = both.astype(BF16)


def copies_send_kernel(pos, left, right, vectors, sent):
    block = left.shape[1] // 4
    other = 1 - pos[3]
    tile = 256

    def step(i, _):
        outer, inner = lax.div(i, block // tile), lax.rem(i, block // tile)
        at = pl.multiple_of((2 * outer + other) * block + inner * tile, tile)
        sent[pl.ds(pl.multiple_of(i * tile, tile), tile), :] = dot_tn(
            left[:, pl.ds(at, tile)], right[...]
        ).astype(BF16)
        return 0

    lax.fori_loop(0, 2 * block // tile, step, 0)
    put_vectors(sent, 2 * block, vectors[:1, :], vectors[1:2, :])


def copies_keep_kernel(pos, left, right, vectors, received, sent, kept, vector_sums):
    block = left.shape[1] // 4
    core, y = pos[3], pos[2]
    tile = 256

    def step(i, _):
        rows = pl.ds(pl.multiple_of(i * tile, tile), tile)
        for turn, target in ((0, kept), (1, sent)):
            outer = 1 - y if turn else y
            at = pl.multiple_of((2 * outer + core) * block + i * tile, tile)
            there = pl.ds(pl.multiple_of(outer * block + i * tile, tile), tile)
            target[rows, :] = (
                dot_tn(left[:, pl.ds(at, tile)], right[...]) + received[there, :].astype(F32)
            ).astype(BF16)
        return 0

    lax.fori_loop(0, block // tile, step, 0)
    width = vectors.shape[1]
    got = received[2 * block : 2 * block + VECTOR_ROWS, :width].astype(F32)
    vector_sums[...] = vectors[...] + got[:8]
    put_vectors(sent, block, vector_sums[:1, :], vector_sums[1:2, :])


def copies_whole_kernel(pos, kept, low, high, whole, core_kept, core_rest, result):
    tile = 512
    rows = kept.shape[0]
    width = kept.shape[1] - result.shape[1]
    start = pos[3] * (width // 2)

    def step(i, _):
        at = pl.ds(pl.multiple_of(i * tile, tile), tile)
        mine = jnp.where(pos[3] == 0, low[:, at], high[:, at])
        other = jnp.where(pos[3] == 0, core_rest[:rows, at], core_rest[rows : 2 * rows, at])
        both = pl.ds(pl.multiple_of(start + i * tile, tile), tile)
        result[at, :] = (
            dot_tn(kept[:, both], kept[:, width:])
            + dot_tn(mine, whole[...])
            + dot_tn(core_kept[:, both], core_kept[:, width:])
            + dot_tn(other, core_rest[2 * rows :, :])
        )
        return 0

    lax.fori_loop(0, result.shape[0] // tile, step, 0)


def dense_grad_kernel(pos, returned, cotangent, pick, act, grad_dense, grad_low, sent):
    grad_dense[...] = cotangent[...].astype(F32) + dot_tn(pick[...], returned[...])
    grad_low[...] = grad_dense[...].astype(BF16)
    sum_send_kernel(pos, act, grad_low, sent)


def sum_send_kernel(pos, left, right, sent):
    half = right.shape[1] // 2
    lanes = pl.ds(pl.multiple_of((1 - pos[3]) * half, 128), half)
    tile = min(1024, left.shape[1] // 2)

    def step(i, _):
        rows = pl.ds(pl.multiple_of(i * tile, tile), tile)
        sent[rows, :] = dot_tn(left[:, rows], right[:, lanes]).astype(BF16)
        return 0

    lax.fori_loop(0, left.shape[1] // tile, step, 0)


def lay_out(pos, total, far, near, kept, sems, n_planes, vector=None):
    block = total.shape[0] // (4 * n_planes)
    for second in (1, 0):
        for step in range(n_planes):
            for first in (1, 0):
                row = row_start(pos, pos[3], second, first, step, n_planes, block)
                if first:
                    target, at, sem = (far if second else near), step, sems.at[1 + second]
                else:
                    target, at, sem = kept, second * n_planes + step, sems.at[0]
                pltpu.make_async_copy(
                    total.at[pl.ds(row, block), :], target.at[pl.ds(at * block, block), :], sem
                ).start()
    if vector is not None:
        pltpu.make_async_copy(
            vector, far.at[pl.ds(total.shape[0] // 4, VECTOR_ROWS), :], sems.at[2]
        ).start()
    for target, sem in ((kept, 0), (near, 1), (far, 2)):
        wait_whole(target, sems.at[sem])


def sum_keep_kernel(
    n_planes, pos, left, right, received, far, near, kept, total, sems, vector=None
):
    half = right.shape[1] // 2
    lanes = pl.ds(pl.multiple_of(pos[3] * half, 128), half)
    tile = min(1024, left.shape[1] // 2)

    def step(i, _):
        rows = pl.ds(pl.multiple_of(i * tile, tile), tile)
        total[rows, :] = (
            dot_tn(left[:, rows], right[:, lanes]) + received[rows, :].astype(F32)
        ).astype(BF16)
        return 0

    lax.fori_loop(0, left.shape[1] // tile, step, 0)
    lay_out(pos, total, far, near, kept, sems, n_planes, vector)


def pre_back_kernel(n_planes, split, pos, grad_low, slope, *refs):
    sides, (grad_pre, weight, sem) = take_sides(refs, split)
    load_weight(pos, sides, weight, sem, n_planes, True)
    rows = weight.shape[0] // n_planes
    chunk = min(512, rows)
    for step in range(n_planes):
        start = wait_step(pos, weight, sem, step, n_planes)
        for i in range(rows // chunk):
            at = pl.ds(pl.multiple_of(start + i * chunk, chunk), chunk)
            grad_pre[:, at] = (dot_nt(grad_low[...], weight[at, :]) * slope[:, at]).astype(BF16)


def hidden_back_kernel(n_planes, split, pos, grad_pre, hidden, grad_dense, gains, *refs):
    sides, (ffn_in, heads, grad_hidden, grad_low, grad_gain, send, weight, sem) = take_sides(refs, split)
    load_weight(pos, sides, weight, sem, n_planes, False)
    norm, inverse = normed(hidden[...])
    half = weight.shape[1] // 2
    grad_in = 0.0
    for side in range(2):
        core = pos[3] if side == 0 else 1 - pos[3]
        wait_half(weight, core, sem)
        lanes = pl.ds(pl.multiple_of(core * half, 128), half)
        grad_in = grad_in + dot_nt(grad_pre[:, lanes], weight[:, lanes])
    grad_gain[...] = jnp.zeros_like(grad_gain)
    grad_gain[0:1, :] = jnp.sum(grad_in * norm, axis=0, keepdims=True)
    grad_hidden[...] = grad_dense[...] + norm_back(grad_in * gains[1:2, :], norm, inverse)
    grad_low[...] = grad_hidden[...].astype(BF16)
    wide_columns(1 - pos[3], ffn_in, heads, grad_pre, grad_low, send, None)


def attend_back_kernel(n_planes, split, pos, grad_low, qkv, tokens, grad_hidden, gains, *refs):
    sides, refs = take_sides(refs, split)
    grad_qkv, grad_tokens, grad_gain, grad_heads, weight, sem = refs
    length, width = tokens.shape
    head_size = width // HEADS
    load_weight(pos, sides, weight, sem, n_planes, False)
    inputs = tokens[...].astype(F32)
    norm, inverse = normed(inputs)
    causal = causal_mask(length)
    lane = lax.broadcasted_iota(jnp.int32, (1, 2 * head_size), 1)
    wait_half(weight, 1, sem)
    grad_heads[...] = dot_nt(grad_low[...], weight[:, 3 * width : 4 * width]).astype(BF16)
    factor = head_size**-0.5

    def pair(i, _):
        at = pl.multiple_of(i * 2 * head_size, 2 * head_size)
        query = qkv[:, pl.ds(at, 2 * head_size)]
        key_rows = qkv[:, pl.ds(width + at, 2 * head_size)]
        value_rows = qkv[:, pl.ds(2 * width + at, 2 * head_size)]
        grad_out = grad_heads[:, pl.ds(at, 2 * head_size)]
        sums = [0.0, 0.0, 0.0]
        for head in range(2):
            own = (lane // head_size) == head
            masked = lambda v: jnp.where(own, v, 0).astype(BF16)
            own_query, own_grad = masked(query), masked(grad_out)
            scores = dot_nt(own_query, key_rows) * factor
            scores = jnp.where(causal, scores, -1e30)
            shifted = jnp.exp(scores - jnp.max(scores, axis=-1, keepdims=True))
            probs = shifted / jnp.sum(shifted, axis=-1, keepdims=True)
            grad_probs = dot_nt(own_grad, value_rows)
            row_terms = jnp.sum(probs * grad_probs, axis=-1, keepdims=True)
            grad_scores = (probs * (grad_probs - row_terms)).astype(BF16)
            sums[0] = sums[0] + dot_nn(grad_scores, masked(key_rows)) * factor
            sums[1] = sums[1] + dot_tn(grad_scores, own_query) * factor
            sums[2] = sums[2] + dot_tn(probs.astype(BF16), own_grad)
        for part in range(3):
            grad_qkv[:, pl.ds(part * width + at, 2 * head_size)] = sums[part].astype(BF16)
        return 0

    lax.fori_loop(0, HEADS // 2, pair, 0)
    wait_half(weight, 0, sem)
    grad_in = dot_nt(grad_qkv[...], weight[:, : 3 * width])
    grad_gain[...] = jnp.zeros_like(grad_gain)
    grad_gain[0:1, :] = jnp.sum(grad_in * norm, axis=0, keepdims=True)
    grad_tokens[...] = grad_hidden[...] + norm_back(grad_in * gains[0:1, :], norm, inverse)


def wide_columns(half, ffn_in, heads, grad_pre, grad_low, target, received):
    width = ffn_in.shape[1]
    columns = target.shape[1]
    rest = grad_pre.shape[1] - columns
    tile = 512

    def fill(lanes, left, right):
        def step(i, _):
            rows = pl.ds(pl.multiple_of(i * tile, tile), tile)
            value = dot_tn(left[:, rows], right())
            if received is not None:
                value = value + received[rows, lanes].astype(F32)
            target[rows, lanes] = value.astype(BF16)
            return 0

        lax.fori_loop(0, width // tile, step, 0)

    @pl.when(half == 0)
    def _():
        fill(slice(0, columns), ffn_in, lambda: grad_pre[:, :columns])

    @pl.when(half == 1)
    def _():
        fill(slice(0, rest), ffn_in, lambda: grad_pre[:, columns:])
        fill(slice(rest, columns), heads, lambda: grad_low[...])


def wide_keep_kernel(
    n_planes,
    pos,
    ffn_in,
    heads,
    grad_pre,
    grad_low,
    received,
    attn_in,
    grad_qkv,
    gain_one,
    gain_two,
    far,
    near,
    kept,
    send,
    total,
    sems,
):
    wide_columns(pos[3], ffn_in, heads, grad_pre, grad_low, total, received)
    lay_out(pos, total, far, near, kept, sems, n_planes)
    last_send_kernel(pos, attn_in, grad_qkv, gain_one, gain_two, send)


def last_send_kernel(pos, left, right, gain_one, gain_two, sent):
    put_vectors(sent, left.shape[1], gain_one[:1, :], gain_two[:1, :])
    sum_send_kernel(pos, left, right, sent)


def last_keep_kernel(
    n_planes,
    pos,
    left,
    right,
    gain_one,
    gain_two,
    received,
    far,
    near,
    kept,
    vector,
    total,
    vector_low,
    sems,
):
    at = received.shape[0] - VECTOR_ROWS
    width = gain_one.shape[1]
    vector[...] = jnp.zeros_like(vector)
    vector_low[...] = jnp.zeros_like(vector_low)
    for i, gain in enumerate((gain_one, gain_two)):
        row = slice(at, at + VECTOR_ROWS)
        summed = gain[:1, :] + received[row, :width].astype(F32)[i : i + 1]
        vector[i : i + 1, :width] = summed
    vector_low[:8, :] = vector[...].astype(BF16)
    sum_keep_kernel(
        n_planes, pos, left, right, received, far, near, kept, total, sems, vector_low
    )


def own_columns(values, core):
    half = values.shape[1] // 2
    mine = lax.dynamic_slice_in_dim(values, core * half, half, 1)
    other = lax.dynamic_slice_in_dim(values, (1 - core) * half, half, 1)
    got = swap_core(other)
    return jnp.where(
        core == 0, jnp.concatenate([mine, got], axis=0), jnp.concatenate([got, mine], axis=0)
    )


def exchange_rows(total, vector, swap):
    half = total.shape[0] // 2
    send = total[half:].astype(BF16)
    if vector is not None:
        send = jnp.concatenate(
            [send, jnp.pad(vector, ((0, VECTOR_ROWS - vector.shape[0]), (0, 0))).astype(BF16)], axis=0
        )
    got = swap(send).astype(F32)
    if vector is not None:
        vector = vector + got[half : half + vector.shape[0]]
    return total[:half] + got[:half], vector


def start_sum(got, kept):
    return kept.astype(F32) + got[: kept.shape[0]].astype(F32)


def second_sum(got_far, got_near, kept, vector=None, gate=()):
    half = kept.shape[0] // 2
    send = (kept[half:].astype(F32) + got_far[:half].astype(F32)).astype(BF16)
    if vector is not None:
        vector = vector + got_far[half : half + vector.shape[0]].astype(F32)
        low = jnp.pad(vector, ((0, VECTOR_ROWS - vector.shape[0]), (0, 0))).astype(BF16)
        send = jnp.concatenate([send, low], axis=0)
    got = swap_first(after(send, *gate) if gate else send).astype(F32)
    if vector is not None:
        vector = vector + got[half : half + vector.shape[0]]
    return kept[:half].astype(F32) + got_near.astype(F32) + got[:half], vector, (send,)


def whole_rows(total, core):
    shard = total.shape[0] // 2
    mine = lax.dynamic_slice_in_dim(total, core * shard, shard, 0)
    other = lax.dynamic_slice_in_dim(total, (1 - core) * shard, shard, 0)
    got = swap_core(other.astype(BF16)).astype(F32)
    return jnp.where(
        core == 0, jnp.concatenate([mine, got], axis=1), jnp.concatenate([got, mine], axis=1)
    )


def on_device(
    tokens,
    route,
    w_qkv,
    w_attn_out,
    w_up,
    w_down,
    gain_attn,
    gain_ffn,
    expert_in,
    expert_out,
    centroids,
    expert_gain,
    cotangent,
):
    length, features = tokens.shape
    n_expert = lax.axis_size("expert")
    n_replica = lax.axis_size("replica")
    n_dev = n_expert * n_replica
    n_planes = n_dev // 8
    per_dest = length // n_expert
    hidden_size = w_up.shape[1]
    replica = lax.axis_index("replica")
    me = lax.axis_index("expert") * n_replica + replica
    core = me % 2
    pos = jnp.stack([me // 8, (me // 4) % 2, (me // 2) % 2, core]).astype(jnp.int32)
    route_pick = (route[0][:, None] == lax.iota(jnp.int32, length)[None]).astype(BF16)

    def to_expert(picked):
        return lax.all_to_all(
            picked.reshape(n_expert, per_dest, features),
            "expert",
            split_axis=0,
            concat_axis=0,
            tiled=True,
        ).reshape(length, features)

    padded_gains = jnp.pad(jnp.stack([gain_attn, gain_ffn], axis=1), ((0, 0), (0, 254)))
    first = jnp.concatenate([w_qkv, w_attn_out, padded_gains], axis=1)
    owned = [own_columns(v, core) for v in (first, w_up, w_down)]
    join = lambda *v: jnp.concatenate(v, axis=0)
    far_bit = n_planes // 2

    def near_planes(own, *earlier):
        stack = after(own, *earlier) if earlier else own
        bit = 1
        while bit < far_bit:
            stack = join(stack, swap_plane(stack, bit))
            bit *= 2
        return stack

    own_a, own_b, own_c = owned
    near_a = near_planes(own_a)
    gate = (near_a,)
    far_a = swap_plane(near_a, far_bit)
    near_one_a = swap_first(near_a)
    near_b, near_c = near_planes(own_b, *gate), near_planes(own_c, *gate)
    gate = (far_a, near_one_a, near_b, near_c)
    far_b = swap_plane(after(near_b, *gate), far_bit)
    near_two_a = swap_second(after(join(near_a, near_one_a), *gate))
    one_a = swap_first(after(far_a, *gate))
    near_one_b = swap_first(after(near_b, *gate))
    gate = (far_b, near_two_a, one_a, near_one_b)
    far_c = swap_plane(after(near_c, *gate), far_bit)
    two_a = swap_second(after(join(far_a, one_a), *gate))
    near_two_b = swap_second(after(join(near_b, near_one_b), *gate))
    one_b = swap_first(after(far_b, *gate))
    core_near_a = swap_core(after(join(near_a, near_one_a, near_two_a), *gate))
    gate = (far_c, two_a, near_two_b, one_b, core_near_a)
    two_b = swap_second(after(join(far_b, one_b), *gate))
    near_one_c = swap_first(after(near_c, *gate))
    one_c = swap_first(after(far_c, *gate))
    core_far_a = swap_core(after(join(far_a, one_a, two_a), *gate))
    core_near_b = swap_core(after(join(near_b, near_one_b, near_two_b), *gate))
    first_pieces = [near_a, near_one_a, near_two_a, far_a, one_a, two_a, core_near_a, core_far_a]
    gate = (two_b, near_one_c, one_c, core_far_a, core_near_b)
    near_two_c = swap_second(after(join(near_c, near_one_c), *gate))
    two_c = swap_second(after(join(far_c, one_c), *gate))
    core_far_b = swap_core(after(join(far_b, one_b, two_b), *gate))
    up_pieces = [near_b, near_one_b, near_two_b, far_b, one_b, two_b, core_near_b, core_far_b]
    grad_delta = to_expert(jnp.dot(route_pick, cotangent, preferred_element_type=F32).astype(BF16))

    wide = first.shape[1]
    planes = functools.partial
    weight_first = pltpu.VMEM((features, wide), BF16)
    weight_up = pltpu.VMEM((features, hidden_size), BF16)
    weight_down = pltpu.VMEM((hidden_size, features), BF16)
    two_sems, three_sems, plane_sems = (pltpu.SemaphoreType.DMA((n,)) for n in (2, 3, n_planes))
    unit = 2 * length * features * features

    hidden, ffn_in, attn_in, qkv, heads, gains = run_kernel(
        planes(attend_kernel, n_planes, (6, 2)),
        [after(pos, grad_delta), tokens, *first_pieces],
        "sv" + "h" * 8,
        [
            shaped(length, features, dtype=F32),
            shaped(length, features),
            shaped(length, features),
            shaped(length, 3 * features),
            shaped(length, features),
            shaped(8, features, dtype=F32),
        ],
        [weight_first, two_sems],
        flops=5 * unit,
    )
    gate = (near_two_c, two_c, core_far_b, hidden)
    core_near_c = swap_core(after(join(near_c, near_one_c, near_two_c), *gate))
    core_far_c = swap_core(after(join(far_c, one_c, two_c), *gate))
    act, slope = run_kernel(
        planes(up_kernel, n_planes, (6, 2)),
        [pos, ffn_in, *up_pieces],
        "sv" + "h" * 8,
        [shaped(length, hidden_size), shaped(length, hidden_size, dtype=F32)],
        [weight_up, two_sems],
        flops=4 * unit,
    )
    down_pieces = [near_c, near_one_c, near_two_c, far_c, one_c, two_c, core_near_c, core_far_c]
    dense_out, sent = run_kernel(
        planes(down_kernel, n_planes, (6, 2)),
        [pos, act, hidden, route_pick, *down_pieces],
        "svvv" + "h" * 8,
        [shaped(length, features, dtype=F32), shaped(length, features)],
        [weight_down, plane_sems],
        flops=4 * unit,
    )
    arrived = to_expert(after(sent, grad_delta))
    inner = expert_in.shape[2]
    (
        delta,
        grad_rows,
        expert_norm,
        pair,
        sent_low,
        sent_high,
        whole_low,
        expert_grad_pre,
        vectors,
    ) = run_kernel(
        expert_kernel,
        [pos, arrived, grad_delta, centroids, expert_gain, expert_in, expert_out],
        "svvvvhh",
        [
            shaped(length, features),
            shaped(length, features),
            shaped(length, features),
            shaped(length, inner // 2 + features),
            shaped(length, inner // 4),
            shaped(length, inner // 4),
            shaped(length, features),
            shaped(length, inner),
            shaped(8, features, dtype=F32),
        ],
        [
            pltpu.VMEM((features, inner), BF16),
            pltpu.VMEM((inner, features), BF16),
            pltpu.VMEM((length, inner), BF16),
            pltpu.VMEM((length, inner), F32),
            pltpu.SemaphoreType.DMA((2, inner // 512)),
        ],
        flops=16 * unit,
    )
    returned = to_expert(grad_rows)
    got_low = swap_y(sent_low)
    got_high = swap_y(after(sent_high, got_low))
    got_whole = swap_y(after(whole_low, got_high))

    (send_in,) = run_kernel(
        copies_send_kernel,
        [pos, expert_norm, expert_grad_pre, vectors],
        "svvv",
        [shaped(features // 2 + VECTOR_ROWS, inner)],
        flops=2 * unit,
    )
    got_in = swap_core(send_in)

    grad_dense, grad_dense_low, send_down = run_kernel(
        dense_grad_kernel,
        [after(pos, send_in, got_low), returned, cotangent, route_pick, act],
        "svvvv",
        [
            shaped(length, features, dtype=F32),
            shaped(length, features),
            shaped(hidden_size, features // 2),
        ],
        flops=4 * unit,
    )
    got_down = swap_core(send_down)
    (grad_pre,) = run_kernel(
        planes(pre_back_kernel, n_planes, (6, 2)),
        [after(pos, send_down, got_in, got_high), grad_dense_low, slope, *down_pieces],
        "svv" + "h" * 8,
        [shaped(length, hidden_size)],
        [weight_down, plane_sems],
        flops=4 * unit,
    )
    core_kept = swap_core(pair)
    far_down, near_down, kept_down = run_kernel(
        planes(sum_keep_kernel, n_planes),
        [after(pos, grad_pre, got_whole, core_kept), act, grad_dense_low, got_down],
        "svvv",
        [shaped(hidden_size // 4, features // 2)] * 2 + [shaped(hidden_size // 2, features // 2)],
        [pltpu.VMEM((hidden_size, features // 2), BF16), three_sems],
        flops=4 * unit,
        out_spaces="hhh",
    )
    got_far_down, got_near_down = swap_second(far_down), swap_second(near_down)
    send_in, kept_in, vectors = run_kernel(
        copies_keep_kernel,
        [after(pos, kept_down), expert_norm, expert_grad_pre, vectors, got_in],
        "svvvv",
        [
            shaped(features // 4 + VECTOR_ROWS, inner),
            shaped(features // 4, inner),
            shaped(8, features, dtype=F32),
        ],
        flops=2 * unit,
    )
    core_rest = swap_core(join(got_low, got_high, got_whole))
    wide_half = (hidden_size + features) // 2
    grad_hidden, grad_hidden_low, grad_gain_two, send_up = run_kernel(
        planes(hidden_back_kernel, n_planes, (6, 2)),
        [
            after(pos, send_in),
            grad_pre,
            hidden,
            grad_dense,
            gains,
            *up_pieces,
            ffn_in,
            heads,
        ],
        "svvvv" + "h" * 8 + "vv",
        [
            shaped(length, features, dtype=F32),
            shaped(length, features),
            shaped(8, features, dtype=F32),
            shaped(features, wide_half),
        ],
        [weight_up, two_sems],
        flops=7 * unit,
    )
    got_up = swap_core(send_up)
    grad_qkv, grad_tokens, grad_gain_one = run_kernel(
        planes(attend_back_kernel, n_planes, (6, 2)),
        [
            after(pos, got_far_down, got_near_down, send_up, core_rest),
            grad_hidden_low,
            qkv,
            tokens,
            grad_hidden,
            gains,
            *first_pieces,
        ],
        "svvvvv" + "h" * 8,
        [
            shaped(length, 3 * features),
            shaped(length, features, dtype=F32),
            shaped(8, features, dtype=F32),
        ],
        [pltpu.VMEM((length, features), BF16), weight_first, two_sems],
        flops=8 * unit,
    )
    in_low = swap_y(after(send_in[: features // 16], grad_qkv))
    down_2 = second_sum(got_far_down, got_near_down, kept_down)
    last_half = 3 * features // 2
    far_up, near_up, kept_up, send_last = run_kernel(
        planes(wide_keep_kernel, n_planes),
        [
            after(pos, grad_qkv, down_2[0]),
            ffn_in,
            heads,
            grad_pre,
            grad_hidden_low,
            got_up,
            attn_in,
            grad_qkv,
            grad_gain_one,
            grad_gain_two,
        ],
        "s" + "v" * 9,
        [shaped(features // 4, wide_half)] * 2
        + [shaped(features // 2, wide_half), shaped(features + VECTOR_ROWS, last_half)],
        [pltpu.VMEM((features, wide_half), BF16), three_sems],
        flops=5 * unit,
        out_spaces="hhhv",
    )
    swaps = [
        functools.partial(swap_plane, bit=bit)
        for bit in (1 << i for i in reversed(range(n_planes.bit_length() - 1)))
    ]
    got_far_up = swap_second(far_up)
    down_3, _ = exchange_rows(after(down_2[0], kept_up), None, swaps[0])
    got_near_up = swap_second(after(near_up, got_far_up))
    got_last = swap_core(send_last)
    delta_home = to_expert(after(delta, send_last))
    (sum_expert_out,) = run_kernel(
        copies_whole_kernel,
        [
            after(pos, send_last, delta_home, in_low),
            pair,
            got_low,
            got_high,
            got_whole,
            core_kept,
            core_rest,
        ],
        "s" + "v" * 6,
        [shaped(inner // n_replica, features, dtype=F32)],
        flops=4 * unit,
    )
    far, near, kept, vector = run_kernel(
        planes(last_keep_kernel, n_planes),
        [
            after(pos, sum_expert_out, got_far_up, down_3),
            attn_in,
            grad_qkv,
            grad_gain_one,
            grad_gain_two,
            got_last,
        ],
        "s" + "v" * 5,
        [
            shaped(features // 4 + VECTOR_ROWS, last_half),
            shaped(features // 4, last_half),
            shaped(features // 2, last_half),
            shaped(8, last_half, dtype=F32),
        ],
        [
            pltpu.VMEM((features, last_half), BF16),
            pltpu.VMEM((VECTOR_ROWS, last_half), BF16),
            three_sems,
        ],
        flops=2 * unit,
        out_spaces="hhhv",
    )
    up_2 = second_sum(got_far_up, got_near_up, kept_up, gate=(kept,))
    last_2 = second_sum(swap_second(far), swap_second(near), kept, vector)
    in_high = swap_y(after(send_in[features // 16 :], up_2[0]))
    sums = []
    for total, vector, left in (
        (after(down_3, up_2[0]), None, swaps[1:]),
        (*up_2[:2], swaps),
        (*last_2[:2], swaps),
    ):
        for swap in left:
            total, vector = exchange_rows(total, vector, swap)
        sums.append(whole_rows(total, core))
    sum_down, sum_up, sum_last = sums
    mixed = (
        dense_out
        + lax.dot_general(
            route_pick, delta_home, (((0,), (0,)), ((), ())), preferred_element_type=F32
        )
    ).astype(BF16)
    part = features // n_replica
    sum_expert_in = kept_in.astype(F32) + join(in_low, in_high[: 3 * features // 16]).astype(F32)
    vectors = vectors[:2] + in_high[3 * features // 16 : 3 * features // 16 + 2, :features].astype(F32)
    vectors = lax.dynamic_slice_in_dim(vectors, replica * part, part, 1)
    shard = features // n_dev
    gain_grads = lax.dynamic_slice_in_dim(vector[:2, :features], me * shard, shard, 1)
    return (
        mixed,
        grad_tokens,
        sum_last,
        sum_up[:, hidden_size:],
        sum_up[:, :hidden_size],
        sum_down,
        gain_grads[0],
        gain_grads[1],
        sum_expert_in[None],
        sum_expert_out[None],
        vectors[:1],
        vectors[1:],
    )


def solution(mesh):
    placed = (
        P(("expert", "replica"), None),
        P(("expert", "replica"), None),
        P(("expert", "replica"), None),
        P(("expert", "replica"), None),
        P(("expert", "replica"), None),
        P(("expert", "replica"), None),
        P(("expert", "replica")),
        P(("expert", "replica")),
        P("expert", None, None),
        P("expert", None, None),
        P("expert", None),
        P("expert", None),
        P(("expert", "replica"), None),
    )
    return jax.shard_map(
        on_device,
        mesh=mesh,
        in_specs=placed,
        out_specs=(
            P(("expert", "replica"), None),
            P(("expert", "replica"), None),
            P(("expert", "replica"), None),
            P(("expert", "replica"), None),
            P(("expert", "replica"), None),
            P(("expert", "replica"), None),
            P(("expert", "replica")),
            P(("expert", "replica")),
            P("expert", "replica", None),
            P("expert", "replica", None),
            P("expert", "replica"),
            P("expert", "replica"),
        ),
        check_vma=False,
    )
```

profile of v0, /device:TPU:0, one launch (start us, length us, event | category | flops | bytes accessed | tf_op | source)
XLA Modules:
  0.0 509.5 jit_solution(2543931419993153371)
XLA Ops:
  5.7 2.7 collective-permute-start.1
  8.5 7.2 %collective-permute-done.1 = bf16[64,2176]{1,0:T(8,128)(2,1)S(1)} collective-permute-done((bf16[64,2176]{1,0:T(8,128)(2,1)S(1)}, bf16[64,2176]{1,0:T(8,128)(2,1)S(1)}, u32[]{:S(2)}, u32[]{:S(2)}) %collective-permute-start.1) | collective-permute-done | bytes 278560 | tf_op jit(solution)/shard_map/ppermute | solution.py:21
  17.4 2.6 collective-permute-start.3
  22.8 20.0 %collective-permute-done.7 = bf16[256,512]{1,0:T(8,128)(2,1)S(1)} collective-permute-done((bf16[256,512]{1,0:T(8,128)(2,1)S(1)}, bf16[256,512]{1,0:T(8,128)(2,1)S(1)}, u32[]{:S(2)}, u32[]{:S(2)}) %collective-permute-start.7) | collective-permute-done | bytes 262176 | tf_op jit(solution)/shard_map/ppermute | solution.py:21
  48.7 22.7 %collective-permute-done.8.refs_2_ = bf16[256,2176]{1,0:T(8,128)(2,1)S(1)} collective-permute-done((bf16[256,2176]{1,0:T(8,128)(2,1)S(1)}, bf16[256,2176]{1,0:T(8,128)(2,1)S(1)}, u32[]{:S(2)}, u32[]{:S(2)}) %collective-permute-start.8) | collective-permute-done | bytes 1114144 | tf_op jit(solution)/shard_map/ppermute | solution.py:21
  76.9 16.9 %collective-permute-done.12.refs_5_ = bf16[256,2176]{1,0:T(8,128)(2,1)S(1)} collective-permute-done((bf16[256,2176]{1,0:T(8,128)(2,1)S(1)}, bf16[256,2176]{1,0:T(8,128)(2,1)S(1)}, u32[]{:S(2)}, u32[]{:S(2)}) %collective-permute-start.12) | collective-permute-done | bytes 1114144 | tf_op jit(solution)/shard_map/ppermute | solution.py:21
  95.5 5.5 %collective-permute-done.14.refs_3_ = bf16[512,512]{1,0:T(8,128)(2,1)} collective-permute-done((bf16[512,512]{1,0:T(8,128)(2,1)}, bf16[512,512]{1,0:T(8,128)(2,1)}, u32[]{:S(2)}, u32[]{:S(2)}) %collective-permute-start.14) | collective-permute-done | bytes 524320 | tf_op jit(solution)/shard_map/ppermute | solution.py:21
  101.0 3.9 collective-permute-done.15.refs_2_
  107.8 5.6 %all-to-all-start = ((bf16[8,32,1024]{2,1,0:T(8,128)(2,1)}), bf16[8,32,1024]{2,1,0:T(8,128)(2,1)}, u32[]{:S(2)}, u32[]{:S(2)}) async-start(bf16[8,32,1024]{2,1,0:T(8,128)(2,1)} %bitcast.5), calls=%async_computation | async-start | bytes 1048576 | tf_op jit(solution)/shard_map/all_to_all | solution.py:702
  113.4 2.1 pad_maximum_fusion.10
  119.5 8.2 %all-to-all-done = bf16[8,32,1024]{2,1,0:T(8,128)(2,1)} async-done(((bf16[8,32,1024]{2,1,0:T(8,128)(2,1)}), bf16[8,32,1024]{2,1,0:T(8,128)(2,1)}, u32[]{:S(2)}, u32[]{:S(2)}) %all-to-all-start) | async-done | bytes 524320 | tf_op jit(solution)/shard_map/all_to_all | solution.py:702
  127.7 6.2 %collective-permute-done.20.refs_1_ = bf16[512,512]{1,0:T(8,128)(2,1)} collective-permute-done((bf16[512,512]{1,0:T(8,128)(2,1)}, bf16[512,512]{1,0:T(8,128)(2,1)}, u32[]{:S(2)}, u32[]{:S(2)}) %collective-permute-start.20) | collective-permute-done | bytes 524320 | tf_op jit(solution)/shard_map/ppermute | solution.py:21
  136.0 8.6 %collective-permute-done.21.refs_4_ = bf16[512,512]{1,0:T(8,128)(2,1)} collective-permute-done((bf16[512,512]{1,0:T(8,128)(2,1)}, bf16[512,512]{1,0:T(8,128)(2,1)}, u32[]{:S(2)}, u32[]{:S(2)}) %collective-permute-start.21) | collective-permute-done | bytes 524320 | tf_op jit(solution)/shard_map/ppermute | solution.py:21
  144.5 2.2 pad_maximum_fusion.12
  150.4 16.0 %attend_kernel.1 = (f32[256,1024]{1,0:T(8,128)}, bf16[256,1024]{1,0:T(8,128)(2,1)}, bf16[256,1024]{1,0:T(8,128)(2,1)}, bf16[256,3072]{1,0:T(8,128)(2,1)}, bf16[256,1024]{1,0:T(8,128)(2,1)}, /*index=5*/f32[8,1024]{1,0:T(8,128)}) custom-call(s32[4]{0:T(128)} %pad_add_fusion.pos, bf16[256,1024]{1,0:T(8,128)(2,1)} %tokens.3, bf16[128,2176]{1,0:T(8,128)(2,1)} %copy-done.16, ...), custom_call_target="tpu_custom_call" | custom-call | flops 80530636800 | bytes 409928160 | tf_op jit(solution)/shard_map/attend_kernel/pallas_call | solution.py:67
  168.0 6.8 %collective-permute-done.24.refs_5_ = bf16[1024,512]{1,0:T(8,128)(2,1)} collective-permute-done((bf16[1024,512]{1,0:T(8,128)(2,1)}, bf16[1024,512]{1,0:T(8,128)(2,1)}, u32[]{:S(2)}, u32[]{:S(2)}) %collective-permute-start.24) | collective-permute-done | bytes 1048608 | tf_op jit(solution)/shard_map/ppermute | solution.py:21
  174.8 3.0 pad_maximum_fusion.5
  178.2 10.7 %up_kernel.1 = (bf16[256,4096]{1,0:T(8,128)(2,1)}, f32[256,4096]{1,0:T(8,128)}) custom-call(s32[4]{0:T(128)} %pad_add_fusion.pos, bf16[256,1024]{1,0:T(8,128)(2,1)} %get-tuple-element.107.ffn_in.refs_8_, bf16[128,2048]{1,0:T(8,128)(2,1)} %copy-done.23, bf16[128,2048]{1,0:T(8,128)(2,1)} %copy-done.7, bf16[256,2048]{1,0:T(8,128)(2,1)} %copy-done.15, ...), custom_call_target="tpu_custom_call" | custom-call | flops 64424509440 | bytes 456131040 | tf_op jit(solution)/shard_map/up_kernel/pallas_call | solution.py:67
  190.2 7.2 %down_kernel.1 = (f32[256,1024]{1,0:T(8,128)}, bf16[256,1024]{1,0:T(8,128)(2,1)}) custom-call(s32[4]{0:T(128)} %pad_add_fusion.pos, bf16[256,4096]{1,0:T(8,128)(2,1)} %get-tuple-element.113.act.left, f32[256,1024]{1,0:T(8,128)} %get-tuple-element.114.hidden, bf16[256,256]{1,0:T(8,128)(2,1)} %fusion.8.pick, ...), custom_call_target="tpu_custom_call" | custom-call | flops 64424509440 | bytes 397148640 | tf_op jit(solution)/shard_map/down_kernel/pallas_call | solution.py:67
  197.4 19.3 %all_to_all.20 = bf16[8,32,1024]{2,1,0:T(8,128)(2,1)} all-to-all(bf16[8,32,1024]{2,1,0:T(8,128)(2,1)} %bitcast.27), channel_id=1, replica_groups=mesh['expert'=8,'replica'=4] {'expert'}, dimensions={0} | all-to-all | bytes 1048576 | tf_op jit(solution)/shard_map/all_to_all | solution.py:702
  216.7 16.4 %expert_kernel.1 = (bf16[256,1024]{1,0:T(8,128)(2,1)}, bf16[256,1024]{1,0:T(8,128)(2,1)}, bf16[256,1024]{1,0:T(8,128)(2,1)}, bf16[256,3072]{1,0:T(8,128)(2,1)}, ...) custom-call(s32[4]{0:T(128)} %pad_add_fusion.pos, ...), custom_call_target="tpu_custom_call" | custom-call | flops 257698037760 | bytes 740352512 | tf_op jit(solution)/shard_map/expert_kernel/pallas_call | solution.py:67
  233.7 3.9 all-to-all-start.2
  237.6 8.4 %collective-permute-done.27.low = bf16[256,1024]{1,0:T(8,128)(2,1)S(1)} collective-permute-done((bf16[256,1024]{1,0:T(8,128)(2,1)}, bf16[256,1024]{1,0:T(8,128)(2,1)S(1)}, u32[]{:S(2)}, u32[]{:S(2)}) %collective-permute-start.27) | collective-permute-done | bytes 524320 | tf_op jit(solution)/shard_map/ppermute | solution.py:21
  246.5 5.3 %copies_send_kernel.1 = bf16[528,4096]{1,0:T(8,128)(2,1)} custom-call(s32[4]{0:T(128)} %pad_add_fusion.pos, bf16[256,1024]{1,0:T(8,128)(2,1)} %get-tuple-element.123.left, bf16[256,4096]{1,0:T(8,128)(2,1)} %get-tuple-element.124.right, f32[8,1024]{1,0:T(8,128)} %get-tuple-element.125.vectors), custom_call_target="tpu_custom_call" | custom-call | flops 32212254720 | bytes 209388000 | tf_op jit(solution)/shard_map/copies_send_kernel/pallas_call | solution.py:67
  252.4 5.9 %collective-permute-done.29.high = bf16[256,1024]{1,0:T(8,128)(2,1)S(1)} collective-permute-done((bf16[256,1024]{1,0:T(8,128)(2,1)}, bf16[256,1024]{1,0:T(8,128)(2,1)S(1)}, u32[]{:S(2)}, u32[]{:S(2)}) %collective-permute-start.29) | collective-permute-done | bytes 524320 | tf_op jit(solution)/shard_map/ppermute | solution.py:21
  259.6 6.3 %dense_grad_kernel.1 = (f32[256,1024]{1,0:T(8,128)}, bf16[256,1024]{1,0:T(8,128)(2,1)}, bf16[4096,512]{1,0:T(8,128)(2,1)}) custom-call(s32[4]{0:T(128)} %pad_add_fusion.pos, bf16[256,1024]{1,0:T(8,128)(2,1)} %bitcast.25, bf16[256,1024]{1,0:T(8,128)(2,1)} %cotangent.1, bf16[256,256]{1,0:T(8,128)(2,1)} %fusion.8.pick, ...), custom_call_target="tpu_custom_call" | custom-call | flops 64424509440 | bytes 271319520 | tf_op jit(solution)/shard_map/dense_grad_kernel/pallas_call | solution.py:67
  265.9 3.2 collective-permute-done.30.whole
  270.4 8.3 %pre_back_kernel.1.grad_pre = bf16[256,4096]{1,0:T(8,128)(2,1)} custom-call(s32[4]{0:T(128)} %pad_add_fusion.pos, bf16[256,1024]{1,0:T(8,128)(2,1)} %get-tuple-element.133.grad_low.right, f32[256,4096]{1,0:T(8,128)} %get-tuple-element.134.slope, bf16[512,512]{1,0:T(8,128)(2,1)} %constant_dynamic-update-slice_fusion.2.refs_0_, ...), custom_call_target="tpu_custom_call" | custom-call | flops 64424509440 | bytes 456131040 | tf_op jit(solution)/shard_map/pre_back_kernel/pallas_call | solution.py:67
  278.8 7.0 %sum_keep_kernel.1 = (bf16[1024,512]{1,0:T(8,128)(2,1)}, bf16[1024,512]{1,0:T(8,128)(2,1)}, bf16[2048,512]{1,0:T(8,128)(2,1)}) custom-call(s32[4]{0:T(128)} %pad_add_fusion.pos, bf16[256,4096]{1,0:T(8,128)(2,1)} %get-tuple-element.113.act.left, bf16[256,1024]{1,0:T(8,128)(2,1)} %get-tuple-element.133.grad_low.right, ...), custom_call_target="tpu_custom_call" | custom-call | flops 64424509440 | bytes 330301920 | tf_op jit(solution)/shard_map/sum_keep_kernel/pallas_call | solution.py:67
  287.8 5.9 %copies_keep_kernel.1 = (bf16[272,4096]{1,0:T(8,128)(2,1)}, bf16[256,4096]{1,0:T(8,128)(2,1)}, f32[8,1024]{1,0:T(8,128)}) custom-call(s32[4]{0:T(128)} %pad_add_fusion.pos, bf16[256,1024]{1,0:T(8,128)(2,1)} %get-tuple-element.123.left, bf16[256,4096]{1,0:T(8,128)(2,1)} %get-tuple-element.124.right, f32[8,1024]{1,0:T(8,128)} %get-tuple-element.125.vectors, ...), custom_call_target="tpu_custom_call" | custom-call | flops 32212254720 | bytes 340132320 | tf_op jit(solution)/shard_map/copies_keep_kernel/pallas_call | solution.py:67
  293.7 14.2 %hidden_back_kernel.1 = (f32[256,1024]{1,0:T(8,128)}, bf16[256,1024]{1,0:T(8,128)(2,1)}, f32[8,1024]{1,0:T(8,128)}, bf16[1024,2560]{1,0:T(8,128)(2,1)}) custom-call(s32[4]{0:T(128)} %pad_add_fusion.pos, bf16[256,4096]{1,0:T(8,128)(2,1)} %pre_back_kernel.1.grad_pre, f32[256,1024]{1,0:T(8,128)} %get-tuple-element.114.hidden, ...), custom_call_target="tpu_custom_call" | custom-call | flops 112742891520 | bytes 615383552 | tf_op jit(solution)/shard_map/hidden_back_kernel/pallas_call | solution.py:67
  307.9 4.2 collective-permute-done.34
  315.2 19.4 %attend_back_kernel.1 = (bf16[256,3072]{1,0:T(8,128)(2,1)}, f32[256,1024]{1,0:T(8,128)}, f32[8,1024]{1,0:T(8,128)}) custom-call(s32[4]{0:T(128)} %pad_add_fusion.pos, bf16[256,1024]{1,0:T(8,128)(2,1)} %get-tuple-element.150.grad_low, bf16[256,3072]{1,0:T(8,128)(2,1)} %get-tuple-element.151.qkv, bf16[256,1024]{1,0:T(8,128)(2,1)} %tokens.3, ...), custom_call_target="tpu_custom_call" | custom-call | flops 128849018880 | bytes 458097120 | tf_op jit(solution)/shard_map/attend_back_kernel/pallas_call | solution.py:67
  336.3 11.3 %wide_keep_kernel.1 = (bf16[256,2560]{1,0:T(8,128)(2,1)}, bf16[256,2560]{1,0:T(8,128)(2,1)}, bf16[512,2560]{1,0:T(8,128)(2,1)}, bf16[1040,1536]{1,0:T(8,128)(2,1)}) custom-call(s32[4]{0:T(128)} %pad_add_fusion.pos, bf16[256,1024]{1,0:T(8,128)(2,1)} %get-tuple-element.107.ffn_in.refs_8_, bf16[256,1024]{1,0:T(8,128)(2,1)} %get-tuple-element.147.refs_9_.heads, ...), custom_call_target="tpu_custom_call" | custom-call | flops 80530636800 | bytes 585400832 | tf_op jit(solution)/shard_map/wide_keep_kernel/pallas_call | solution.py:67
  347.5 4.6 all-to-all-start.3
  352.2 3.0 collective-permute-start.40
  357.6 2.8 slice.152
  362.7 25.0 %collective-permute-done.40 = bf16[512,512]{1,0:T(8,128)(2,1)} collective-permute-done((bf16[512,512]{1,0:T(8,128)(2,1)S(1)}, bf16[512,512]{1,0:T(8,128)(2,1)}, u32[]{:S(2)}, u32[]{:S(2)}) %collective-permute-start.40) | collective-permute-done | bytes 524320 | tf_op jit(solution)/shard_map/ppermute | solution.py:21
  389.0 7.5 %copies_whole_kernel.1 = f32[1024,1024]{1,0:T(8,128)} custom-call(s32[4]{0:T(128)} %pad_add_fusion.pos, bf16[256,3072]{1,0:T(8,128)(2,1)} %get-tuple-element.137.kept, bf16[256,1024]{1,0:T(8,128)(2,1)} %copy-done.19, bf16[256,1024]{1,0:T(8,128)(2,1)} %copy-done.20, bf16[256,1024]{1,0:T(8,128)(2,1)} %copy-done.21, ...), custom_call_target="tpu_custom_call" | custom-call | flops 64424509440 | bytes 314573280 | tf_op jit(solution)/shard_map/copies_whole_kernel/pallas_call | solution.py:67
  398.1 6.1 %last_keep_kernel.1 = (bf16[272,1536]{1,0:T(8,128)(2,1)}, bf16[256,1536]{1,0:T(8,128)(2,1)}, bf16[512,1536]{1,0:T(8,128)(2,1)}, f32[8,1536]{1,0:T(8,128)}) custom-call(s32[4]{0:T(128)} %pad_add_fusion.pos, bf16[256,1024]{1,0:T(8,128)(2,1)} %get-tuple-element.155.attn_in.left, bf16[256,3072]{1,0:T(8,128)(2,1)} %get-tuple-element.153.grad_qkv.right, ...), custom_call_target="tpu_custom_call" | custom-call | flops 32212254720 | bytes 258048480 | tf_op jit(solution)/shard_map/last_keep_kernel/pallas_call | solution.py:67
  411.0 28.2 %collective-permute-done.43 = bf16[272,1536]{1,0:T(8,128)(2,1)S(1)} collective-permute-done((bf16[272,1536]{1,0:T(8,128)(2,1)}, bf16[272,1536]{1,0:T(8,128)(2,1)S(1)}, u32[]{:S(2)}, u32[]{:S(2)}) %collective-permute-start.43) | collective-permute-done | bytes 835616 | tf_op jit(solution)/shard_map/ppermute | solution.py:21
  446.0 5.6 %collective-permute-done.53 = bf16[256,512]{1,0:T(8,128)(2,1)S(1)} collective-permute-done((bf16[256,512]{1,0:T(8,128)(2,1)S(1)}, bf16[256,512]{1,0:T(8,128)(2,1)S(1)}, u32[]{:S(2)}, u32[]{:S(2)}) %collective-permute-start.53) | collective-permute-done | bytes 262176 | tf_op jit(solution)/shard_map/ppermute | solution.py:21
  452.3 3.8 collective-permute-done.42
  457.4 25.2 %collective-permute-done.50 = bf16[128,2560]{1,0:T(8,128)(2,1)S(1)} collective-permute-done((bf16[128,2560]{1,0:T(8,128)(2,1)S(1)}, bf16[128,2560]{1,0:T(8,128)(2,1)S(1)}, u32[]{:S(2)}, u32[]{:S(2)}) %collective-permute-start.50) | collective-permute-done | bytes 655392 | tf_op jit(solution)/shard_map/ppermute | solution.py:21
  482.9 6.3 %collective-permute-done.45 = bf16[144,1536]{1,0:T(8,128)(2,1)S(1)} collective-permute-done((bf16[144,1536]{1,0:T(8,128)(2,1)S(1)}, bf16[144,1536]{1,0:T(8,128)(2,1)S(1)}, u32[]{:S(2)}, u32[]{:S(2)}) %collective-permute-start.45) | collective-permute-done | bytes 442400 | tf_op jit(solution)/shard_map/ppermute | solution.py:21
  489.6 6.6 %collective-permute-done.51 = bf16[64,2560]{1,0:T(8,128)(2,1)S(1)} collective-permute-done((bf16[64,2560]{1,0:T(8,128)(2,1)S(1)}, bf16[64,2560]{1,0:T(8,128)(2,1)S(1)}, u32[]{:S(2)}, u32[]{:S(2)}) %collective-permute-start.51) | collective-permute-done | bytes 327712 | tf_op jit(solution)/shard_map/ppermute | solution.py:21
  496.5 4.9 collective-permute-done.46
  505.6 3.8 add_bitcast_fusion
  (230 shorter events, 77.4 us)
Async XLA Ops:
  15.7 27.8 %collective-permute-start.2 = (bf16[128,2176]{1,0:T(8,128)(2,1)S(1)}, bf16[128,2176]{1,0:T(8,128)(2,1)S(1)}, u32[]{:S(2)}, u32[]{:S(2)}) collective-permute-start(bf16[128,2176]{1,0:T(8,128)(2,1)S(1)} %pad_maximum_fusion.13.refs_0_), channel_id=1, source_target_pairs={{0,4},{1,3},{2,6},{3,1},{4,0},{5,7},{6,2},{7,5},{8,12},{9,11},{10,... | collective-permute-start | bytes 1671176 | tf_op jit(solution)/shard_map/ppermute | solution.py:21
  17.4 26.8 %collective-permute-start.3 = (bf16[128,2176]{1,0:T(8,128)(2,1)S(1)}, bf16[128,2176]{1,0:T(8,128)(2,1)S(1)}, u32[]{:S(2)}, u32[]{:S(2)}) collective-permute-start(bf16[128,2176]{1,0:T(8,128)(2,1)S(1)} %pad_maximum_fusion.13.refs_0_), channel_id=1, source_target_pairs={{0,16},{1,17},{2,18},{3,19},{4,20},{5,21},{6,22},{7,23},{8,24},{9,... | collective-permute-start | bytes 1671176 | tf_op jit(solution)/shard_map/ppermute | solution.py:21
  20.0 23.5 %collective-permute-start.5 = (bf16[64,2048]{1,0:T(8,128)(2,1)S(1)}, bf16[64,2048]{1,0:T(8,128)(2,1)S(1)}, u32[]{:S(2)}, u32[]{:S(2)}) collective-permute-start(bf16[64,2048]{1,0:T(8,128)(2,1)S(1)} %maximum_select_fusion.4), channel_id=1, source_target_pairs={{0,8},{1,9},{2,10},{3,11},{4,12},{5,13},{6,14},{7,15},{8,0},{9,1},... | collective-permute-start | bytes 786440 | tf_op jit(solution)/shard_map/ppermute | solution.py:21
  21.6 21.2 %collective-permute-start.7 = (bf16[256,512]{1,0:T(8,128)(2,1)S(1)}, bf16[256,512]{1,0:T(8,128)(2,1)S(1)}, u32[]{:S(2)}, u32[]{:S(2)}) collective-permute-start(bf16[256,512]{1,0:T(8,128)(2,1)S(1)} %maximum_select_fusion.5), channel_id=1, source_target_pairs={{0,8},{1,9},{2,10},{3,11},{4,12},{5,13},{6,14},{7,15},{8,0},{9,1},... | collective-permute-start | bytes 786440 | tf_op jit(solution)/shard_map/ppermute | solution.py:21
  44.2 27.1 %collective-permute-start.8 = (bf16[256,2176]{1,0:T(8,128)(2,1)S(1)}, bf16[256,2176]{1,0:T(8,128)(2,1)S(1)}, u32[]{:S(2)}, u32[]{:S(2)}) collective-permute-start(bf16[256,2176]{1,0:T(8,128)(2,1)S(1)} %pad_maximum_fusion.7), channel_id=1, source_target_pairs={{0,2},{1,5},{2,0},{3,7},{4,6},{5,1},{6,4},{7,3},{8,10},{9,13},{10,... | collective-permute-start | bytes 3342344 | tf_op jit(solution)/shard_map/ppermute | solution.py:21
  44.8 27.6 %collective-permute-start.9 = (bf16[128,2176]{1,0:T(8,128)(2,1)S(1)}, bf16[128,2176]{1,0:T(8,128)(2,1)S(1)}, u32[]{:S(2)}, u32[]{:S(2)}) collective-permute-start(bf16[128,2176]{1,0:T(8,128)(2,1)S(1)} %collective-permute-done.3.refs_3_), channel_id=1, source_target_pairs={{0,4},{1,3},{2,6},{3,1},{4,0},{5,7},{6,2},{7,5},{8,12},{9,11},{10,... | collective-permute-start | bytes 1671176 | tf_op jit(solution)/shard_map/ppermute | solution.py:21
  46.2 26.1 %collective-permute-start.10 = (bf16[128,2048]{1,0:T(8,128)(2,1)S(1)}, bf16[128,2048]{1,0:T(8,128)(2,1)S(1)}, u32[]{:S(2)}, u32[]{:S(2)}) collective-permute-start(bf16[128,2048]{1,0:T(8,128)(2,1)S(1)} %constant_dynamic-update-slice_fusion.refs_0_), channel_id=1, source_target_pairs={{0,16},{1,17},{2,18},{3,19},{4,20},{5,21},{6,22},{7,23},{8,24},{9,... | collective-permute-start | bytes 1572872 | tf_op jit(solution)/shard_map/ppermute | solution.py:21
  48.1 24.2 %collective-permute-start.11 = (bf16[128,2048]{1,0:T(8,128)(2,1)S(1)}, bf16[128,2048]{1,0:T(8,128)(2,1)S(1)}, u32[]{:S(2)}, u32[]{:S(2)}) collective-permute-start(bf16[128,2048]{1,0:T(8,128)(2,1)S(1)} %constant_dynamic-update-slice_fusion.refs_0_), channel_id=1, source_target_pairs={{0,4},{1,3},{2,6},{3,1},{4,0},{5,7},{6,2},{7,5},{8,12},{9,11},{10,... | collective-permute-start | bytes 1572872 | tf_op jit(solution)/shard_map/ppermute | solution.py:21
  72.4 32.6 %collective-permute-start.13 = (bf16[512,2176]{1,0:T(8,128)(2,1)S(1)}, bf16[512,2176]{1,0:T(8,128)(2,1)S(1)}, u32[]{:S(2)}, u32[]{:S(2)}) collective-permute-start(bf16[512,2176]{1,0:T(8,128)(2,1)S(1)} %pad_maximum_fusion), channel_id=1, source_target_pairs={{0,1},{1,0},{2,3},{3,2},{4,5},{5,4},{6,7},{7,6},{8,9},{9,8},{10,11... | collective-permute-start | bytes 6684680 | tf_op jit(solution)/shard_map/ppermute | solution.py:21
  72.6 21.2 %collective-permute-start.12 = (bf16[256,2176]{1,0:T(8,128)(2,1)S(1)}, bf16[256,2176]{1,0:T(8,128)(2,1)S(1)}, u32[]{:S(2)}, u32[]{:S(2)}) collective-permute-start(bf16[256,2176]{1,0:T(8,128)(2,1)S(1)} %pad_maximum_fusion.8), channel_id=1, source_target_pairs={{0,2},{1,5},{2,0},{3,7},{4,6},{5,1},{6,4},{7,3},{8,10},{9,13},{10,... | collective-permute-start | bytes 3342344 | tf_op jit(solution)/shard_map/ppermute | solution.py:21
  73.3 31.7 %collective-permute-start.15 = (bf16[256,2048]{1,0:T(8,128)(2,1)S(1)}, bf16[256,2048]{1,0:T(8,128)(2,1)S(1)}, u32[]{:S(2)}, u32[]{:S(2)}) collective-permute-start(bf16[256,2048]{1,0:T(8,128)(2,1)S(1)} %pad_maximum_fusion.9), channel_id=1, source_target_pairs={{0,2},{1,5},{2,0},{3,7},{4,6},{5,1},{6,4},{7,3},{8,10},{9,13},{10,... | collective-permute-start | bytes 3145736 | tf_op jit(solution)/shard_map/ppermute | solution.py:21
  74.8 26.2 %collective-permute-start.14 = (bf16[512,512]{1,0:T(8,128)(2,1)}, bf16[512,512]{1,0:T(8,128)(2,1)}, u32[]{:S(2)}, u32[]{:S(2)}) collective-permute-start(bf16[512,512]{1,0:T(8,128)(2,1)} %constant_dynamic-update-slice_fusion.2.refs_0_), channel_id=1, source_target_pairs={{0,16},{1,17},{2,18},{3,19},{4,20},{5,21},{6,22},{7,23},{8,24},{9,... | collective-permute-start | bytes 1572872 | tf_op jit(solution)/shard_map/ppermute | solution.py:21
  76.5 24.5 %collective-permute-start.16 = (bf16[128,2048]{1,0:T(8,128)(2,1)S(1)}, bf16[128,2048]{1,0:T(8,128)(2,1)S(1)}, u32[]{:S(2)}, u32[]{:S(2)}) collective-permute-start(bf16[128,2048]{1,0:T(8,128)(2,1)S(1)} %collective-permute-done.10.refs_3_), channel_id=1, source_target_pairs={{0,4},{1,3},{2,6},{3,1},{4,0},{5,7},{6,2},{7,5},{8,12},{9,11},{10,... | collective-permute-start | bytes 1572872 | tf_op jit(solution)/shard_map/ppermute | solution.py:21
  105.0 43.3 %collective-permute-start.17 = (bf16[512,2176]{1,0:T(8,128)(2,1)}, bf16[512,2176]{1,0:T(8,128)(2,1)}, u32[]{:S(2)}, u32[]{:S(2)}) collective-permute-start(bf16[512,2176]{1,0:T(8,128)(2,1)} %pad_maximum_fusion.1), channel_id=1, source_target_pairs={{0,1},{1,0},{2,3},{3,2},{4,5},{5,4},{6,7},{7,6},{8,9},{9,8},{10,11... | collective-permute-start | bytes 6684680 | tf_op jit(solution)/shard_map/ppermute | solution.py:21
  105.3 42.9 %collective-permute-start.19 = (bf16[512,2048]{1,0:T(8,128)(2,1)S(1)}, bf16[512,2048]{1,0:T(8,128)(2,1)}, u32[]{:S(2)}, u32[]{:S(2)}) collective-permute-start(bf16[512,2048]{1,0:T(8,128)(2,1)S(1)} %pad_maximum_fusion.2), channel_id=1, source_target_pairs={{0,1},{1,0},{2,3},{3,2},{4,5},{5,4},{6,7},{7,6},{8,9},{9,8},{10,11... | collective-permute-start | bytes 6291464 | tf_op jit(solution)/shard_map/ppermute | solution.py:21
  107.8 19.9 %all-to-all-start = ((bf16[8,32,1024]{2,1,0:T(8,128)(2,1)}), bf16[8,32,1024]{2,1,0:T(8,128)(2,1)}, u32[]{:S(2)}, u32[]{:S(2)}) async-start(bf16[8,32,1024]{2,1,0:T(8,128)(2,1)} %bitcast.5), calls=%async_computation | async-start | bytes 1048576 | tf_op jit(solution)/shard_map/all_to_all | solution.py:702
  115.5 31.3 %collective-permute-start.18 = (bf16[256,2048]{1,0:T(8,128)(2,1)}, bf16[256,2048]{1,0:T(8,128)(2,1)}, u32[]{:S(2)}, u32[]{:S(2)}) collective-permute-start(bf16[256,2048]{1,0:T(8,128)(2,1)} %pad_maximum_fusion.10), channel_id=1, source_target_pairs={{0,2},{1,5},{2,0},{3,7},{4,6},{5,1},{6,4},{7,3},{8,10},{9,13},{10,... | collective-permute-start | bytes 3145736 | tf_op jit(solution)/shard_map/ppermute | solution.py:21
  116.0 17.9 %collective-permute-start.20 = (bf16[512,512]{1,0:T(8,128)(2,1)}, bf16[512,512]{1,0:T(8,128)(2,1)}, u32[]{:S(2)}, u32[]{:S(2)}) collective-permute-start(bf16[512,512]{1,0:T(8,128)(2,1)} %constant_dynamic-update-slice_fusion.2.refs_0_), channel_id=1, source_target_pairs={{0,4},{1,3},{2,6},{3,1},{4,0},{5,7},{6,2},{7,5},{8,12},{9,11},{10,... | collective-permute-start | bytes 1572872 | tf_op jit(solution)/shard_map/ppermute | solution.py:21
  118.0 26.5 %collective-permute-start.21 = (bf16[512,512]{1,0:T(8,128)(2,1)}, bf16[512,512]{1,0:T(8,128)(2,1)}, u32[]{:S(2)}, u32[]{:S(2)}) collective-permute-start(bf16[512,512]{1,0:T(8,128)(2,1)} %collective-permute-done.14.refs_3_), channel_id=1, source_target_pairs={{0,4},{1,3},{2,6},{3,1},{4,0},{5,7},{6,2},{7,5},{8,12},{9,11},{10,... | collective-permute-start | bytes 1572872 | tf_op jit(solution)/shard_map/ppermute | solution.py:21
  148.3 29.5 %collective-permute-start.22 = (bf16[512,2048]{1,0:T(8,128)(2,1)S(1)}, bf16[512,2048]{1,0:T(8,128)(2,1)}, u32[]{:S(2)}, u32[]{:S(2)}) collective-permute-start(bf16[512,2048]{1,0:T(8,128)(2,1)S(1)} %pad_maximum_fusion.3), channel_id=1, source_target_pairs={{0,1},{1,0},{2,3},{3,2},{4,5},{5,4},{6,7},{7,6},{8,9},{9,8},{10,11... | collective-permute-start | bytes 6291464 | tf_op jit(solution)/shard_map/ppermute | solution.py:21
  148.3 18.1 %collective-permute-start.23 = (bf16[1024,512]{1,0:T(8,128)(2,1)}, bf16[1024,512]{1,0:T(8,128)(2,1)}, u32[]{:S(2)}, u32[]{:S(2)}) collective-permute-start(bf16[1024,512]{1,0:T(8,128)(2,1)} %pad_maximum_fusion.11), channel_id=1, source_target_pairs={{0,2},{1,5},{2,0},{3,7},{4,6},{5,1},{6,4},{7,3},{8,10},{9,13},{10,... | collective-permute-start | bytes 3145736 | tf_op jit(solution)/shard_map/ppermute | solution.py:21
  148.9 25.8 %collective-permute-start.24 = (bf16[1024,512]{1,0:T(8,128)(2,1)}, bf16[1024,512]{1,0:T(8,128)(2,1)}, u32[]{:S(2)}, u32[]{:S(2)}) collective-permute-start(bf16[1024,512]{1,0:T(8,128)(2,1)} %pad_maximum_fusion.12), channel_id=1, source_target_pairs={{0,2},{1,5},{2,0},{3,7},{4,6},{5,1},{6,4},{7,3},{8,10},{9,13},{10,... | collective-permute-start | bytes 3145736 | tf_op jit(solution)/shard_map/ppermute | solution.py:21
  233.1 12.9 %collective-permute-start.27 = (bf16[256,1024]{1,0:T(8,128)(2,1)}, bf16[256,1024]{1,0:T(8,128)(2,1)S(1)}, u32[]{:S(2)}, u32[]{:S(2)}) collective-permute-start(bf16[256,1024]{1,0:T(8,128)(2,1)} %get-tuple-element.126), channel_id=1, source_target_pairs={{0,2},{1,3},{2,0},{3,1},{4,6},{5,7},{6,4},{7,5},{8,10},{9,11},{10,... | collective-permute-start | bytes 1572872 | tf_op jit(solution)/shard_map/ppermute | solution.py:21
  233.7 25.1 %all-to-all-start.2 = ((bf16[8,32,1024]{2,1,0:T(8,128)(2,1)}), bf16[8,32,1024]{2,1,0:T(8,128)(2,1)S(1)}, u32[]{:S(2)}, u32[]{:S(2)}) async-start(bf16[8,32,1024]{2,1,0:T(8,128)(2,1)} %bitcast.24), calls=%async_computation.2 | async-start | bytes 1048576 | tf_op jit(solution)/shard_map/all_to_all | solution.py:702
  246.0 12.3 %collective-permute-start.29 = (bf16[256,1024]{1,0:T(8,128)(2,1)}, bf16[256,1024]{1,0:T(8,128)(2,1)S(1)}, u32[]{:S(2)}, u32[]{:S(2)}) collective-permute-start(bf16[256,1024]{1,0:T(8,128)(2,1)} %get-tuple-element.131), channel_id=1, source_target_pairs={{0,2},{1,3},{2,0},{3,1},{4,6},{5,7},{6,4},{7,5},{8,10},{9,11},{10,... | collective-permute-start | bytes 1572872 | tf_op jit(solution)/shard_map/ppermute | solution.py:21
  251.8 18.6 %collective-permute-start.28 = (bf16[528,4096]{1,0:T(8,128)(2,1)}, bf16[528,4096]{1,0:T(8,128)(2,1)}, u32[]{:S(2)}, u32[]{:S(2)}) collective-permute-start(bf16[528,4096]{1,0:T(8,128)(2,1)} %copies_send_kernel.1), channel_id=1, source_target_pairs={{0,1},{1,0},{2,3},{3,2},{4,5},{5,4},{6,7},{7,6},{8,9},{9,8},{10,11... | collective-permute-start | bytes 12976136 | tf_op jit(solution)/shard_map/ppermute | solution.py:21
  251.9 26.9 %collective-permute-start.31 = (bf16[256,3072]{1,0:T(8,128)(2,1)}, bf16[256,3072]{1,0:T(8,128)(2,1)}, u32[]{:S(2)}, u32[]{:S(2)}) collective-permute-start(bf16[256,3072]{1,0:T(8,128)(2,1)} %get-tuple-element.137.kept), channel_id=1, source_target_pairs={{0,1},{1,0},{2,3},{3,2},{4,5},{5,4},{6,7},{7,6},{8,9},{9,8},{10,11... | collective-permute-start | bytes 4718600 | tf_op jit(solution)/shard_map/ppermute | solution.py:21
  265.9 12.8 %collective-permute-start.32 = (bf16[4096,512]{1,0:T(8,128)(2,1)}, bf16[4096,512]{1,0:T(8,128)(2,1)}, u32[]{:S(2)}, u32[]{:S(2)}) collective-permute-start(bf16[4096,512]{1,0:T(8,128)(2,1)} %get-tuple-element.129), channel_id=1, source_target_pairs={{0,1},{1,0},{2,3},{3,2},{4,5},{5,4},{6,7},{7,6},{8,9},{9,8},{10,11... | collective-permute-start | bytes 12582920 | tf_op jit(solution)/shard_map/ppermute | solution.py:21
  270.4 37.5 %collective-permute-start.35 = (bf16[768,1024]{1,0:T(8,128)(2,1)}, bf16[768,1024]{1,0:T(8,128)(2,1)}, u32[]{:S(2)}, u32[]{:S(2)}) collective-permute-start(bf16[768,1024]{1,0:T(8,128)(2,1)} %pad_maximum_fusion.6), channel_id=1, source_target_pairs={{0,1},{1,0},{2,3},{3,2},{4,5},{5,4},{6,7},{7,6},{8,9},{9,8},{10,11... | collective-permute-start | bytes 4718600 | tf_op jit(solution)/shard_map/ppermute | solution.py:21
  285.7 22.2 %collective-permute-start.33 = (bf16[1024,512]{1,0:T(8,128)(2,1)}, bf16[1024,512]{1,0:T(8,128)(2,1)}, u32[]{:S(2)}, u32[]{:S(2)}) collective-permute-start(bf16[1024,512]{1,0:T(8,128)(2,1)} %get-tuple-element.139), channel_id=1, source_target_pairs={{0,2},{1,5},{2,0},{3,7},{4,6},{5,1},{6,4},{7,3},{8,10},{9,13},{10,... | collective-permute-start | bytes 3145736 | tf_op jit(solution)/shard_map/ppermute | solution.py:21
  286.3 25.8 %collective-permute-start.34 = (bf16[1024,512]{1,0:T(8,128)(2,1)}, bf16[1024,512]{1,0:T(8,128)(2,1)}, u32[]{:S(2)}, u32[]{:S(2)}) collective-permute-start(bf16[1024,512]{1,0:T(8,128)(2,1)} %get-tuple-element.140), channel_id=1, source_target_pairs={{0,2},{1,5},{2,0},{3,7},{4,6},{5,1},{6,4},{7,3},{8,10},{9,13},{10,... | collective-permute-start | bytes 3145736 | tf_op jit(solution)/shard_map/ppermute | solution.py:21
  307.8 28.4 %collective-permute-start.37 = (bf16[1024,2560]{1,0:T(8,128)(2,1)}, bf16[1024,2560]{1,0:T(8,128)(2,1)}, u32[]{:S(2)}, u32[]{:S(2)}) collective-permute-start(bf16[1024,2560]{1,0:T(8,128)(2,1)} %get-tuple-element.148), channel_id=1, source_target_pairs={{0,1},{1,0},{2,3},{3,2},{4,5},{5,4},{6,7},{7,6},{8,9},{9,8},{10,11... | collective-permute-start | bytes 15728648 | tf_op jit(solution)/shard_map/ppermute | solution.py:21
  313.6 21.0 %collective-permute-start.36 = (bf16[1024,512]{1,0:T(8,128)(2,1)S(1)}, bf16[1024,512]{1,0:T(8,128)(2,1)S(1)}, u32[]{:S(2)}, u32[]{:S(2)}) collective-permute-start(bf16[1024,512]{1,0:T(8,128)(2,1)S(1)} %add_convert_fusion.1), channel_id=1, source_target_pairs={{0,4},{1,3},{2,6},{3,1},{4,0},{5,7},{6,2},{7,5},{8,12},{9,11},{10,... | collective-permute-start | bytes 3145736 | tf_op jit(solution)/shard_map/ppermute | solution.py:21
  347.5 41.4 %all-to-all-start.3 = ((bf16[8,32,1024]{2,1,0:T(8,128)(2,1)}), bf16[8,32,1024]{2,1,0:T(8,128)(2,1)}, u32[]{:S(2)}, u32[]{:S(2)}) async-start(bf16[8,32,1024]{2,1,0:T(8,128)(2,1)} %bitcast.13), calls=%async_computation.3 | async-start | bytes 1048576 | tf_op jit(solution)/shard_map/all_to_all | solution.py:702
  352.2 35.5 %collective-permute-start.40 = (bf16[512,512]{1,0:T(8,128)(2,1)S(1)}, bf16[512,512]{1,0:T(8,128)(2,1)}, u32[]{:S(2)}, u32[]{:S(2)}) collective-permute-start(bf16[512,512]{1,0:T(8,128)(2,1)S(1)} %slice.222), channel_id=1, source_target_pairs={{0,16},{1,17},{2,18},{3,19},{4,20},{5,21},{6,22},{7,23},{8,24},{9,... | collective-permute-start | bytes 1572872 | tf_op jit(solution)/shard_map/ppermute | solution.py:21
  357.1 31.8 %collective-permute-start.38 = (bf16[64,4096]{1,0:T(8,128)(2,1)}, bf16[64,4096]{1,0:T(8,128)(2,1)}, u32[]{:S(2)}, u32[]{:S(2)}) collective-permute-start(bf16[64,4096]{1,0:T(8,128)(2,1)} %slice.122), channel_id=1, source_target_pairs={{0,2},{1,3},{2,0},{3,1},{4,6},{5,7},{6,4},{7,5},{8,10},{9,11},{10,... | collective-permute-start | bytes 1572872 | tf_op jit(solution)/shard_map/ppermute | solution.py:21
  361.2 36.9 %collective-permute-start.41 = (bf16[1040,1536]{1,0:T(8,128)(2,1)}, bf16[1040,1536]{1,0:T(8,128)(2,1)}, u32[]{:S(2)}, u32[]{:S(2)}) collective-permute-start(bf16[1040,1536]{1,0:T(8,128)(2,1)} %get-tuple-element.158), channel_id=1, source_target_pairs={{0,1},{1,0},{2,3},{3,2},{4,5},{5,4},{6,7},{7,6},{8,9},{9,8},{10,11... | collective-permute-start | bytes 9584648 | tf_op jit(solution)/shard_map/ppermute | solution.py:21
  361.2 35.3 %collective-permute-start.39 = (bf16[256,2560]{1,0:T(8,128)(2,1)}, bf16[256,2560]{1,0:T(8,128)(2,1)}, u32[]{:S(2)}, u32[]{:S(2)}) collective-permute-start(bf16[256,2560]{1,0:T(8,128)(2,1)} %get-tuple-element.163), channel_id=1, source_target_pairs={{0,2},{1,5},{2,0},{3,7},{4,6},{5,1},{6,4},{7,3},{8,10},{9,13},{10,... | collective-permute-start | bytes 3932168 | tf_op jit(solution)/shard_map/ppermute | solution.py:21
  396.5 44.7 %collective-permute-start.48 = (bf16[256,2560]{1,0:T(8,128)(2,1)}, bf16[256,2560]{1,0:T(8,128)(2,1)}, u32[]{:S(2)}, u32[]{:S(2)}) collective-permute-start(bf16[256,2560]{1,0:T(8,128)(2,1)} %get-tuple-element.172), channel_id=1, source_target_pairs={{0,2},{1,5},{2,0},{3,7},{4,6},{5,1},{6,4},{7,3},{8,10},{9,13},{10,... | collective-permute-start | bytes 3932168 | tf_op jit(solution)/shard_map/ppermute | solution.py:21
  404.3 35.0 %collective-permute-start.43 = (bf16[272,1536]{1,0:T(8,128)(2,1)}, bf16[272,1536]{1,0:T(8,128)(2,1)S(1)}, u32[]{:S(2)}, u32[]{:S(2)}) collective-permute-start(bf16[272,1536]{1,0:T(8,128)(2,1)} %get-tuple-element.169), channel_id=1, source_target_pairs={{0,2},{1,5},{2,0},{3,7},{4,6},{5,1},{6,4},{7,3},{8,10},{9,13},{10,... | collective-permute-start | bytes 2506760 | tf_op jit(solution)/shard_map/ppermute | solution.py:21
  406.7 34.5 %collective-permute-start.49 = (bf16[256,2560]{1,0:T(8,128)(2,1)S(1)}, bf16[256,2560]{1,0:T(8,128)(2,1)S(1)}, u32[]{:S(2)}, u32[]{:S(2)}) collective-permute-start(bf16[256,2560]{1,0:T(8,128)(2,1)S(1)} %add_convert_fusion), channel_id=1, source_target_pairs={{0,4},{1,3},{2,6},{3,1},{4,0},{5,7},{6,2},{7,5},{8,12},{9,11},{10,... | collective-permute-start | bytes 3932168 | tf_op jit(solution)/shard_map/ppermute | solution.py:21
  409.6 46.5 %collective-permute-start.42 = (bf16[256,1536]{1,0:T(8,128)(2,1)S(1)}, bf16[256,1536]{1,0:T(8,128)(2,1)S(1)}, u32[]{:S(2)}, u32[]{:S(2)}) collective-permute-start(bf16[256,1536]{1,0:T(8,128)(2,1)S(1)} %copy-done.28), channel_id=1, source_target_pairs={{0,2},{1,5},{2,0},{3,7},{4,6},{5,1},{6,4},{7,3},{8,10},{9,13},{10,... | collective-permute-start | bytes 2359304 | tf_op jit(solution)/shard_map/ppermute | solution.py:21
  439.5 12.6 %collective-permute-start.44 = (bf16[272,1536]{1,0:T(8,128)(2,1)S(1)}, bf16[272,1536]{1,0:T(8,128)(2,1)S(1)}, u32[]{:S(2)}, u32[]{:S(2)}) collective-permute-start(bf16[272,1536]{1,0:T(8,128)(2,1)S(1)} %fusion.2), channel_id=1, source_target_pairs={{0,4},{1,3},{2,6},{3,1},{4,0},{5,7},{6,2},{7,5},{8,12},{9,11},{10,... | collective-permute-start | bytes 2506760 | tf_op jit(solution)/shard_map/ppermute | solution.py:21
  444.0 38.6 %collective-permute-start.50 = (bf16[128,2560]{1,0:T(8,128)(2,1)S(1)}, bf16[128,2560]{1,0:T(8,128)(2,1)S(1)}, u32[]{:S(2)}, u32[]{:S(2)}) collective-permute-start(bf16[128,2560]{1,0:T(8,128)(2,1)S(1)} %slice.221), channel_id=1, source_target_pairs={{0,16},{1,17},{2,18},{3,19},{4,20},{5,21},{6,22},{7,23},{8,24},{9,... | collective-permute-start | bytes 1966088 | tf_op jit(solution)/shard_map/ppermute | solution.py:21
  444.7 59.9 %collective-permute-start.55 = (bf16[208,4096]{1,0:T(8,128)(2,1)S(1)}, bf16[208,4096]{1,0:T(8,128)(2,1)S(1)}, u32[]{:S(2)}, u32[]{:S(2)}) collective-permute-start(bf16[208,4096]{1,0:T(8,128)(2,1)S(1)} %copy-done.10), channel_id=1, source_target_pairs={{0,2},{1,3},{2,0},{3,1},{4,6},{5,7},{6,4},{7,5},{8,10},{9,11},{10,... | collective-permute-start | bytes 5111816 | tf_op jit(solution)/shard_map/ppermute | solution.py:21
  456.5 32.7 %collective-permute-start.45 = (bf16[144,1536]{1,0:T(8,128)(2,1)S(1)}, bf16[144,1536]{1,0:T(8,128)(2,1)S(1)}, u32[]{:S(2)}, u32[]{:S(2)}) collective-permute-start(bf16[144,1536]{1,0:T(8,128)(2,1)S(1)} %fusion.5), channel_id=1, source_target_pairs={{0,16},{1,17},{2,18},{3,19},{4,20},{5,21},{6,22},{7,23},{8,24},{9,... | collective-permute-start | bytes 1327112 | tf_op jit(solution)/shard_map/ppermute | solution.py:21
  482.8 13.4 %collective-permute-start.51 = (bf16[64,2560]{1,0:T(8,128)(2,1)S(1)}, bf16[64,2560]{1,0:T(8,128)(2,1)S(1)}, u32[]{:S(2)}, u32[]{:S(2)}) collective-permute-start(bf16[64,2560]{1,0:T(8,128)(2,1)S(1)} %slice.224), channel_id=1, source_target_pairs={{0,8},{1,9},{2,10},{3,11},{4,12},{5,13},{6,14},{7,15},{8,0},{9,1},... | collective-permute-start | bytes 983048 | tf_op jit(solution)/shard_map/ppermute | solution.py:21
  489.5 11.9 %collective-permute-start.46 = (bf16[80,1536]{1,0:T(8,128)(2,1)S(1)}, bf16[80,1536]{1,0:T(8,128)(2,1)S(1)}, u32[]{:S(2)}, u32[]{:S(2)}) collective-permute-start(bf16[80,1536]{1,0:T(8,128)(2,1)S(1)} %fusion.9), channel_id=1, source_target_pairs={{0,8},{1,9},{2,10},{3,11},{4,12},{5,13},{6,14},{7,15},{8,0},{9,1},... | collective-permute-start | bytes 737288 | tf_op jit(solution)/shard_map/ppermute | solution.py:21
  (41 other events, 560.0 us)
where the time goes:
time: 514 us; the launch traced here: 510 us
  waiting for transfers between devices  234 us (46%)
  Pallas kernels  141 us (27%)
  starting transfers between devices  59 us (11%)
  other arithmetic  34.9 us (7%)
  blocking collectives  19.3 us (4%)
  local copies, waits for them, and re-layouts  16.3 us (3%)
    ppermute x56, waiting for transfers between devices, permuted(): lax.ppermute(values, ALL_AXES, [(d, target(d, n_dev)) for d in range(n_de...  226 us
    pallas_call x14, Pallas kernels, run_kernel(): pl.pallas_call(body, name=body_name(body), out_shape=list(outs), in_specs...  141 us
    ppermute x56, starting transfers between devices, permuted(): lax.ppermute(values, ALL_AXES, [(d, target(d, n_dev)) for d in range(n_de...  44.9 us
    all_to_all x1, blocking collectives, to_expert(): lax.all_to_all(picked.reshape(n_expert, per_dest, features), 'expert', sp...  19.3 us
    concatenate x14, other arithmetic, on_device(): join = lambda *v: jnp.concatenate(v, axis=0)  16 us
    all_to_all x3, starting transfers between devices, to_expert(): lax.all_to_all(picked.reshape(n_expert, per_dest, features), 'expert', sp...  14.1 us
  transfers between devices with their start and end apart: 59, of which 24 were waited for; matrix products, arithmetic and copies ran while one was open for 8% of the time, Pallas kernels for 21%

commit v1 on v0

--- a/solution.py
+++ b/solution.py
@@ -219,7 +219,7 @@
         )
         return 0
 
-    lax.fori_loop(0, HEADS // 2, pair, 0)
+    lax.fori_loop(0, HEADS // 2, pair, 0, unroll=True)
     hidden[...] = inputs + dot_nn(heads[...], weight[:, 3 * width : 4 * width])
     norm_two, _ = normed(hidden[...])
     ffn_in[...] = (norm_two * gains[1:2, :]).astype(BF16)
@@ -354,27 +354,26 @@
     put_vectors(sent, 2 * block, vectors[:1, :], vectors[1:2, :])
 
 
-def copies_keep_kernel(pos, left, right, vectors, received, sent, kept, vector_sums):
+def copies_keep_kernel(
+    pos, left, right, vectors, received, sent_first, sent, kept, vector_sums
+):
     block = left.shape[1] // 4
     core, y = pos[3], pos[2]
-    tile = 256
-
-    def step(i, _):
-        rows = pl.ds(pl.multiple_of(i * tile, tile), tile)
-        for turn, target in ((0, kept), (1, sent)):
-            outer = 1 - y if turn else y
-            at = pl.multiple_of((2 * outer + core) * block + i * tile, tile)
-            there = pl.ds(pl.multiple_of(outer * block + i * tile, tile), tile)
-            target[rows, :] = (
-                dot_tn(left[:, pl.ds(at, tile)], right[...]) + received[there, :].astype(F32)
-            ).astype(BF16)
-        return 0
-
-    lax.fori_loop(0, block // tile, step, 0)
+    early = sent_first.shape[0]
+    for turn in range(2):
+        outer = 1 - y if turn else y
+        at = pl.ds(pl.multiple_of((2 * outer + core) * block, 128), block)
+        there = pl.ds(pl.multiple_of(outer * block, 16), block)
+        value = dot_tn(left[:, at], right[...]) + received[there, :].astype(F32)
+        if turn:
+            sent_first[...] = value[:early].astype(BF16)
+            sent[: block - early, :] = value[early:].astype(BF16)
+        else:
+            kept[...] = value.astype(BF16)
     width = vectors.shape[1]
     got = received[2 * block : 2 * block + VECTOR_ROWS, :width].astype(F32)
     vector_sums[...] = vectors[...] + got[:8]
-    put_vectors(sent, block, vector_sums[:1, :], vector_sums[1:2, :])
+    put_vectors(sent, block - early, vector_sums[:1, :], vector_sums[1:2, :])
 
 
 def copies_whole_kernel(pos, kept, low, high, whole, core_kept, core_rest, result):
@@ -526,7 +525,7 @@
             grad_qkv[:, pl.ds(part * width + at, 2 * head_size)] = sums[part].astype(BF16)
         return 0
 
-    lax.fori_loop(0, HEADS // 2, pair, 0)
+    lax.fori_loop(0, HEADS // 2, pair, 0, unroll=True)
     wait_half(weight, 0, sem)
     grad_in = dot_nt(grad_qkv[...], weight[:, : 3 * width])
     grad_gain[...] = jnp.zeros_like(grad_gain)
@@ -645,6 +644,21 @@
 
 def start_sum(got, kept):
     return kept.astype(F32) + got[: kept.shape[0]].astype(F32)
+
+
+def plane_sum(total, vector, n_planes):
+    block = total.shape[0] // n_planes
+    result, sums = total[:block], vector
+    for step in range(1, n_planes):
+        send = total[step * block : (step + 1) * block].astype(BF16)
+        if vector is not None:
+            low = jnp.pad(vector, ((0, VECTOR_ROWS - vector.shape[0]), (0, 0))).astype(BF16)
+            send = jnp.concatenate([send, low], axis=0)
+        got = swap_plane(send, step).astype(F32)
+        result = result + got[:block]
+        if vector is not None:
+            sums = sums + got[block : block + vector.shape[0]]
+    return result, sums
 
 
 def second_sum(got_far, got_near, kept, vector=None, gate=()):
@@ -749,8 +763,8 @@
     near_two_c = swap_second(after(join(near_c, near_one_c), *gate))
     two_c = swap_second(after(join(far_c, one_c), *gate))
     core_far_b = swap_core(after(join(far_b, one_b, two_b), *gate))
+    core_one_c = swap_core(after(join(far_c, one_c), *gate))
     up_pieces = [near_b, near_one_b, near_two_b, far_b, one_b, two_b, core_near_b, core_far_b]
-    grad_delta = to_expert(jnp.dot(route_pick, cotangent, preferred_element_type=F32).astype(BF16))
 
     wide = first.shape[1]
     planes = functools.partial
@@ -762,7 +776,7 @@
 
     hidden, ffn_in, attn_in, qkv, heads, gains = run_kernel(
         planes(attend_kernel, n_planes, (6, 2)),
-        [after(pos, grad_delta), tokens, *first_pieces],
+        [pos, tokens, *first_pieces],
         "sv" + "h" * 8,
         [
             shaped(length, features, dtype=F32),
@@ -777,7 +791,12 @@
     )
     gate = (near_two_c, two_c, core_far_b, hidden)
     core_near_c = swap_core(after(join(near_c, near_one_c, near_two_c), *gate))
-    core_far_c = swap_core(after(join(far_c, one_c, two_c), *gate))
+    core_two_c = swap_core(after(two_c, *gate))
+    grad_delta = to_expert(
+        after(
+            jnp.dot(route_pick, cotangent, preferred_element_type=F32).astype(BF16), hidden
+        )
+    )
     act, slope = run_kernel(
         planes(up_kernel, n_planes, (6, 2)),
         [pos, ffn_in, *up_pieces],
@@ -786,11 +805,11 @@
         [weight_up, two_sems],
         flops=4 * unit,
     )
-    down_pieces = [near_c, near_one_c, near_two_c, far_c, one_c, two_c, core_near_c, core_far_c]
+    down_pieces = [near_c, near_one_c, near_two_c, far_c, one_c, two_c, core_near_c, core_one_c, core_two_c]
     dense_out, sent = run_kernel(
-        planes(down_kernel, n_planes, (6, 2)),
+        planes(down_kernel, n_planes, (6, 3)),
         [pos, act, hidden, route_pick, *down_pieces],
-        "svvv" + "h" * 8,
+        "svvv" + "h" * 9,
         [shaped(length, features, dtype=F32), shaped(length, features)],
         [weight_down, plane_sems],
         flops=4 * unit,
@@ -833,8 +852,6 @@
     )
     returned = to_expert(grad_rows)
     got_low = swap_y(sent_low)
-    got_high = swap_y(after(sent_high, got_low))
-    got_whole = swap_y(after(whole_low, got_high))
 
     (send_in,) = run_kernel(
         copies_send_kernel,
@@ -847,7 +864,7 @@
 
     grad_dense, grad_dense_low, send_down = run_kernel(
         dense_grad_kernel,
-        [after(pos, send_in, got_low), returned, cotangent, route_pick, act],
+        [after(pos, send_in), returned, cotangent, route_pick, act],
         "svvvv",
         [
             shaped(length, features, dtype=F32),
@@ -857,42 +874,45 @@
         flops=4 * unit,
     )
     got_down = swap_core(send_down)
+    got_high = swap_y(after(sent_high, send_down))
     (grad_pre,) = run_kernel(
-        planes(pre_back_kernel, n_planes, (6, 2)),
-        [after(pos, send_down, got_in, got_high), grad_dense_low, slope, *down_pieces],
-        "svv" + "h" * 8,
+        planes(pre_back_kernel, n_planes, (6, 3)),
+        [after(pos, send_down, got_in, got_low), grad_dense_low, slope, *down_pieces],
+        "svv" + "h" * 9,
         [shaped(length, hidden_size)],
         [weight_down, plane_sems],
         flops=4 * unit,
     )
     core_kept = swap_core(pair)
+    got_whole = swap_y(after(whole_low, grad_pre))
     far_down, near_down, kept_down = run_kernel(
         planes(sum_keep_kernel, n_planes),
-        [after(pos, grad_pre, got_whole, core_kept), act, grad_dense_low, got_down],
+        [after(pos, grad_pre, got_high, core_kept), act, grad_dense_low, got_down],
         "svvv",
         [shaped(hidden_size // 4, features // 2)] * 2 + [shaped(hidden_size // 2, features // 2)],
         [pltpu.VMEM((hidden_size, features // 2), BF16), three_sems],
         flops=4 * unit,
         out_spaces="hhh",
     )
-    got_far_down, got_near_down = swap_second(far_down), swap_second(near_down)
-    send_in, kept_in, vectors = run_kernel(
+    got_far_down = swap_second(far_down)
+    got_near_down = swap_second(after(near_down, got_far_down))
+    first_in, send_in, kept_in, vectors = run_kernel(
         copies_keep_kernel,
         [after(pos, kept_down), expert_norm, expert_grad_pre, vectors, got_in],
         "svvvv",
         [
-            shaped(features // 4 + VECTOR_ROWS, inner),
+            shaped(features // 16, inner),
+            shaped(3 * features // 16 + VECTOR_ROWS, inner),
             shaped(features // 4, inner),
             shaped(8, features, dtype=F32),
         ],
         flops=2 * unit,
     )
-    core_rest = swap_core(join(got_low, got_high, got_whole))
     wide_half = (hidden_size + features) // 2
     grad_hidden, grad_hidden_low, grad_gain_two, send_up = run_kernel(
         planes(hidden_back_kernel, n_planes, (6, 2)),
         [
-            after(pos, send_in),
+            after(pos, send_in, got_whole),
             grad_pre,
             hidden,
             grad_dense,
@@ -912,10 +932,11 @@
         flops=7 * unit,
     )
     got_up = swap_core(send_up)
+    core_rest = swap_core(join(*(after(v, send_up) for v in (got_low, got_high, got_whole))))
     grad_qkv, grad_tokens, grad_gain_one = run_kernel(
         planes(attend_back_kernel, n_planes, (6, 2)),
         [
-            after(pos, got_far_down, got_near_down, send_up, core_rest),
+            after(pos, got_far_down, send_up),
             grad_hidden_low,
             qkv,
             tokens,
@@ -932,13 +953,13 @@
         [pltpu.VMEM((length, features), BF16), weight_first, two_sems],
         flops=8 * unit,
     )
-    in_low = swap_y(after(send_in[: features // 16], grad_qkv))
-    down_2 = second_sum(got_far_down, got_near_down, kept_down)
+    in_low = swap_y(after(first_in, grad_qkv))
+    down_2 = second_sum(got_far_down, got_near_down, kept_down, gate=(send_up,))
     last_half = 3 * features // 2
     far_up, near_up, kept_up, send_last = run_kernel(
         planes(wide_keep_kernel, n_planes),
         [
-            after(pos, grad_qkv, down_2[0]),
+            after(pos, grad_qkv, down_2[0], core_rest),
             ffn_in,
             heads,
             grad_pre,
@@ -961,14 +982,12 @@
         for bit in (1 << i for i in reversed(range(n_planes.bit_length() - 1)))
     ]
     got_far_up = swap_second(far_up)
-    down_3, _ = exchange_rows(after(down_2[0], kept_up), None, swaps[0])
     got_near_up = swap_second(after(near_up, got_far_up))
     got_last = swap_core(send_last)
-    delta_home = to_expert(after(delta, send_last))
     (sum_expert_out,) = run_kernel(
         copies_whole_kernel,
         [
-            after(pos, send_last, delta_home, in_low),
+            after(pos, send_last, in_low),
             pair,
             got_low,
             got_high,
@@ -983,7 +1002,7 @@
     far, near, kept, vector = run_kernel(
         planes(last_keep_kernel, n_planes),
         [
-            after(pos, sum_expert_out, got_far_up, down_3),
+            after(pos, sum_expert_out, got_far_up),
             attn_in,
             grad_qkv,
             grad_gain_one,
@@ -1006,18 +1025,16 @@
         out_spaces="hhhv",
     )
     up_2 = second_sum(got_far_up, got_near_up, kept_up, gate=(kept,))
-    last_2 = second_sum(swap_second(far), swap_second(near), kept, vector)
-    in_high = swap_y(after(send_in[features // 16 :], up_2[0]))
-    sums = []
-    for total, vector, left in (
-        (after(down_3, up_2[0]), None, swaps[1:]),
-        (*up_2[:2], swaps),
-        (*last_2[:2], swaps),
-    ):
-        for swap in left:
-            total, vector = exchange_rows(total, vector, swap)
-        sums.append(whole_rows(total, core))
-    sum_down, sum_up, sum_last = sums
+    last_2 = second_sum(swap_second(far), swap_second(after(near, up_2[0])), kept, vector)
+    in_high = swap_y(after(send_in, up_2[0]))
+    down_3, _ = exchange_rows(after(down_2[0], kept), None, swaps[0])
+    delta_home = to_expert(after(delta, down_3))
+    down_3 = after(down_3, last_2[0])
+    for swap in swaps[1:]:
+        down_3, _ = exchange_rows(down_3, None, swap)
+    up_3, _ = plane_sum(after(up_2[0], *last_2[2]), None, n_planes)
+    last_3, vector = plane_sum(*last_2[:2], n_planes)
+    sum_down, sum_up, sum_last = (whole_rows(v, core) for v in (down_3, up_3, last_3))
     mixed = (
         dense_out
         + lax.dot_general(

time: 514 us -> 488 us (0.949)
  blocking collectives: 19.3 us -> 0 us
  waiting for transfers between devices: 234 us -> 221 us
  starting transfers between devices: 59 us -> 64.7 us
    ppermute x56 -> x59, waiting for transfers between devices: 226 us -> 198 us  [permuted(): lax.ppermute(values, ALL_AXES, [(d, target(d, n_dev)) for d in range(n_de...]
    all_to_all x1 -> x0, blocking collectives: 19.3 us -> none  [to_expert(): lax.all_to_all(picked.reshape(n_expert, per_dest, features), 'expert', sp...]
    all_to_all x3 -> x4, waiting for transfers between devices: 8.25 us -> 23.7 us  [to_expert(): lax.all_to_all(picked.reshape(n_expert, per_dest, features), 'expert', sp...]
    pallas_call x14, Pallas kernels: 141 us -> 136 us  [run_kernel(): pl.pallas_call(body, name=body_name(body), out_shape=list(outs), in_specs...]
    all_to_all x3 -> x4, starting transfers between devices: 14.1 us -> 18.2 us  [to_expert(): lax.all_to_all(picked.reshape(n_expert, per_dest, features), 'expert', sp...]
    concatenate x14 -> x13, other arithmetic: 16 us -> 13.2 us  [on_device(): join = lambda *v: jnp.concatenate(v, axis=0)]
    ppermute x56 -> x59, starting transfers between devices: 44.9 us -> 46.5 us  [permuted(): lax.ppermute(values, ALL_AXES, [(d, target(d, n_dev)) for d in range(n_de...]
  transfers between devices with their start and end apart: 59 -> 63, of which waited for: 24 -> 26; matrix products, arithmetic and copies ran while one was open for 8% -> 9% of each run, Pallas kernels for 21% -> 25%
where the time goes in v1:
time: 488 us; the launch traced here: 480 us
  waiting for transfers between devices  221 us (45%)
  Pallas kernels  136 us (28%)
  starting transfers between devices  64.7 us (13%)
  other arithmetic  39.7 us (8%)
  local copies, waits for them, and re-layouts  14.7 us (3%)
    ppermute x59, waiting for transfers between devices, permuted(): lax.ppermute(values, ALL_AXES, [(d, target(d, n_dev)) for d in range(n_de...  198 us
    pallas_call x14, Pallas kernels, run_kernel(): pl.pallas_call(body, name=body_name(body), out_shape=list(outs), in_specs...  136 us
    ppermute x59, starting transfers between devices, permuted(): lax.ppermute(values, ALL_AXES, [(d, target(d, n_dev)) for d in range(n_de...  46.5 us
    all_to_all x4, waiting for transfers between devices, to_expert(): lax.all_to_all(picked.reshape(n_expert, per_dest, features), 'expert', sp...  23.7 us
    all_to_all x4, starting transfers between devices, to_expert(): lax.all_to_all(picked.reshape(n_expert, per_dest, features), 'expert', sp...  18.2 us
    concatenate x13, other arithmetic, on_device(): join = lambda *v: jnp.concatenate(v, axis=0)  13.2 us
  transfers between devices with their start and end apart: 63, of which 26 were waited for; matrix products, arithmetic and copies ran while one was open for 9% of the time, Pallas kernels for 25%

profile of v1, /device:TPU:0, one launch (start us, length us, event | category | flops | bytes accessed | tf_op | source)
XLA Modules:
  0.0 480.1 jit_solution(10328453543715076831)
XLA Ops:
  5.7 2.7 collective-permute-start.1
  8.5 7.2 %collective-permute-done.1 = bf16[64,2176]{1,0:T(8,128)(2,1)S(1)} collective-permute-done((bf16[64,2176]{1,0:T(8,128)(2,1)S(1)}, bf16[64,2176]{1,0:T(8,128)(2,1)S(1)}, u32[]{:S(2)}, u32[]{:S(2)}) %collective-permute-start.1) | collective-permute-done | bytes 278560 | tf_op jit(solution)/shard_map/ppermute | solution.py:21
  19.5 2.7 collective-permute-start.3
  22.8 18.7 %collective-permute-done.7 = bf16[256,512]{1,0:T(8,128)(2,1)S(1)} collective-permute-done((bf16[256,512]{1,0:T(8,128)(2,1)S(1)}, bf16[256,512]{1,0:T(8,128)(2,1)S(1)}, u32[]{:S(2)}, u32[]{:S(2)}) %collective-permute-start.7) | collective-permute-done | bytes 262176 | tf_op jit(solution)/shard_map/ppermute | solution.py:21
  42.4 3.4 collective-permute-done.3.refs_3_
  48.4 23.9 %collective-permute-done.8.refs_2_ = bf16[256,2176]{1,0:T(8,128)(2,1)S(1)} collective-permute-done((bf16[256,2176]{1,0:T(8,128)(2,1)S(1)}, bf16[256,2176]{1,0:T(8,128)(2,1)S(1)}, u32[]{:S(2)}, u32[]{:S(2)}) %collective-permute-start.8) | collective-permute-done | bytes 1114144 | tf_op jit(solution)/shard_map/ppermute | solution.py:21
  76.4 18.6 %collective-permute-done.12.refs_5_ = bf16[256,2176]{1,0:T(8,128)(2,1)S(1)} collective-permute-done((bf16[256,2176]{1,0:T(8,128)(2,1)S(1)}, bf16[256,2176]{1,0:T(8,128)(2,1)S(1)}, u32[]{:S(2)}, u32[]{:S(2)}) %collective-permute-start.12) | collective-permute-done | bytes 1114144 | tf_op jit(solution)/shard_map/ppermute | solution.py:21
  96.7 5.6 %collective-permute-done.14.refs_3_ = bf16[512,512]{1,0:T(8,128)(2,1)} collective-permute-done((bf16[512,512]{1,0:T(8,128)(2,1)}, bf16[512,512]{1,0:T(8,128)(2,1)}, u32[]{:S(2)}, u32[]{:S(2)}) %collective-permute-start.14) | collective-permute-done | bytes 524320 | tf_op jit(solution)/shard_map/ppermute | solution.py:21
  102.3 3.9 collective-permute-done.15.refs_2_
  113.2 20.4 %collective-permute-done.21.refs_4_ = bf16[512,512]{1,0:T(8,128)(2,1)} collective-permute-done((bf16[512,512]{1,0:T(8,128)(2,1)}, bf16[512,512]{1,0:T(8,128)(2,1)}, u32[]{:S(2)}, u32[]{:S(2)}) %collective-permute-start.21) | collective-permute-done | bytes 524320 | tf_op jit(solution)/shard_map/ppermute | solution.py:21
  133.6 2.2 pad_maximum_fusion.11
  138.0 2.8 pad_maximum_fusion.3
  142.9 10.8 %attend_kernel.1 = (f32[256,1024]{1,0:T(8,128)}, bf16[256,1024]{1,0:T(8,128)(2,1)}, bf16[256,1024]{1,0:T(8,128)(2,1)}, bf16[256,3072]{1,0:T(8,128)(2,1)}, bf16[256,1024]{1,0:T(8,128)(2,1)}, /*index=5*/f32[8,1024]{1,0:T(8,128)}) custom-call(s32[4]{0:T(128)} %pad_add_fusion.pos, bf16[256,1024]{1,0:T(8,128)(2,1)} %tokens.3, bf16[128,2176]{1,0:T(8,128)(2,1)} %copy-done.21, ...), custom_call_target="tpu_custom_call" | custom-call | flops 80530636800 | bytes 409928160 | tf_op jit(solution)/shard_map/attend_kernel/pallas_call | solution.py:67
  153.7 5.2 %all-to-all-start = ((bf16[8,32,1024]{2,1,0:T(8,128)(2,1)}), bf16[8,32,1024]{2,1,0:T(8,128)(2,1)S(1)}, u32[]{:S(2)}, u32[]{:S(2)}) async-start(bf16[8,32,1024]{2,1,0:T(8,128)(2,1)} %bitcast.7), calls=%async_computation | async-start | bytes 1048576 | tf_op jit(solution)/shard_map/all_to_all | solution.py:716
  158.9 8.2 %collective-permute-done.23.refs_2_ = bf16[1024,512]{1,0:T(8,128)(2,1)S(1)} collective-permute-done((bf16[1024,512]{1,0:T(8,128)(2,1)}, bf16[1024,512]{1,0:T(8,128)(2,1)S(1)}, u32[]{:S(2)}, u32[]{:S(2)}) %collective-permute-start.23) | collective-permute-done | bytes 1048608 | tf_op jit(solution)/shard_map/ppermute | solution.py:21
  168.7 3.9 collective-permute-start.27
  172.6 10.7 %up_kernel.1 = (bf16[256,4096]{1,0:T(8,128)(2,1)}, f32[256,4096]{1,0:T(8,128)}) custom-call(s32[4]{0:T(128)} %pad_add_fusion.pos, bf16[256,1024]{1,0:T(8,128)(2,1)} %get-tuple-element.114.ffn_in.refs_8_, bf16[128,2048]{1,0:T(8,128)(2,1)} %copy-done.32, bf16[128,2048]{1,0:T(8,128)(2,1)} %copy-done.9, bf16[256,2048]{1,0:T(8,128)(2,1)} %copy-done.19, ...), custom_call_target="tpu_custom_call" | custom-call | flops 64424509440 | bytes 456131040 | tf_op jit(solution)/shard_map/up_kernel/pallas_call | solution.py:67
  185.0 7.2 %down_kernel.1 = (f32[256,1024]{1,0:T(8,128)}, bf16[256,1024]{1,0:T(8,128)(2,1)}) custom-call(s32[4]{0:T(128)} %pad_add_fusion.pos, bf16[256,4096]{1,0:T(8,128)(2,1)} %get-tuple-element.120.act.left, f32[256,1024]{1,0:T(8,128)} %get-tuple-element.121.hidden, bf16[256,256]{1,0:T(8,128)(2,1)} %fusion.6.pick, ...), custom_call_target="tpu_custom_call" | custom-call | flops 64424509440 | bytes 397148640 | tf_op jit(solution)/shard_map/down_kernel/pallas_call | solution.py:67
  192.2 5.6 %all-to-all-start.1 = ((bf16[8,32,1024]{2,1,0:T(8,128)(2,1)}), bf16[8,32,1024]{2,1,0:T(8,128)(2,1)S(1)}, u32[]{:S(2)}, u32[]{:S(2)}) async-start(bf16[8,32,1024]{2,1,0:T(8,128)(2,1)} %bitcast.27), calls=%async_computation.1 | async-start | bytes 1048576 | tf_op jit(solution)/shard_map/all_to_all | solution.py:716
  197.9 15.0 %all-to-all-done.1 = bf16[8,32,1024]{2,1,0:T(8,128)(2,1)S(1)} async-done(((bf16[8,32,1024]{2,1,0:T(8,128)(2,1)}), bf16[8,32,1024]{2,1,0:T(8,128)(2,1)S(1)}, u32[]{:S(2)}, u32[]{:S(2)}) %all-to-all-start.1) | async-done | bytes 524320 | tf_op jit(solution)/shard_map/all_to_all | solution.py:716
  213.7 16.5 %expert_kernel.1 = (bf16[256,1024]{1,0:T(8,128)(2,1)}, bf16[256,1024]{1,0:T(8,128)(2,1)}, bf16[256,1024]{1,0:T(8,128)(2,1)}, bf16[256,3072]{1,0:T(8,128)(2,1)}, ...) custom-call(s32[4]{0:T(128)} %pad_add_fusion.pos, ...), custom_call_target="tpu_custom_call" | custom-call | flops 257698037760 | bytes 740352512 | tf_op jit(solution)/shard_map/expert_kernel/pallas_call | solution.py:67
  230.1 3.8 all-to-all-start.2
  234.0 5.4 %copies_send_kernel.1 = bf16[528,4096]{1,0:T(8,128)(2,1)} custom-call(s32[4]{0:T(128)} %pad_add_fusion.pos, bf16[256,1024]{1,0:T(8,128)(2,1)} %get-tuple-element.131.left, bf16[256,4096]{1,0:T(8,128)(2,1)} %get-tuple-element.132.right, f32[8,1024]{1,0:T(8,128)} %get-tuple-element.133.vectors), custom_call_target="tpu_custom_call" | custom-call | flops 32212254720 | bytes 209388000 | tf_op jit(solution)/shard_map/copies_send_kernel/pallas_call | solution.py:67
  240.1 8.6 %all-to-all-done.2 = bf16[8,32,1024]{2,1,0:T(8,128)(2,1)S(1)} async-done(((bf16[8,32,1024]{2,1,0:T(8,128)(2,1)}), bf16[8,32,1024]{2,1,0:T(8,128)(2,1)S(1)}, u32[]{:S(2)}, u32[]{:S(2)}) %all-to-all-start.2) | async-done | bytes 524320 | tf_op jit(solution)/shard_map/all_to_all | solution.py:716
  249.5 6.4 %dense_grad_kernel.1 = (f32[256,1024]{1,0:T(8,128)}, bf16[256,1024]{1,0:T(8,128)(2,1)}, bf16[4096,512]{1,0:T(8,128)(2,1)}) custom-call(s32[4]{0:T(128)} %pad_add_fusion.pos, bf16[256,1024]{1,0:T(8,128)(2,1)} %bitcast.29, bf16[256,1024]{1,0:T(8,128)(2,1)} %cotangent.1, bf16[256,256]{1,0:T(8,128)(2,1)} %fusion.6.pick, ...), custom_call_target="tpu_custom_call" | custom-call | flops 64424509440 | bytes 271319520 | tf_op jit(solution)/shard_map/dense_grad_kernel/pallas_call | solution.py:67
  256.2 8.5 %pre_back_kernel.1.grad_pre = bf16[256,4096]{1,0:T(8,128)(2,1)} custom-call(s32[4]{0:T(128)} %pad_add_fusion.pos, bf16[256,1024]{1,0:T(8,128)(2,1)} %get-tuple-element.139.grad_low.right, f32[256,4096]{1,0:T(8,128)} %get-tuple-element.140.slope, bf16[512,512]{1,0:T(8,128)(2,1)} %constant_dynamic-update-slice_fusion.2.refs_0_, ...), custom_call_target="tpu_custom_call" | custom-call | flops 64424509440 | bytes 456131040 | tf_op jit(solution)/shard_map/pre_back_kernel/pallas_call | solution.py:67
  266.6 4.1 collective-permute-done.30.high
  270.7 7.1 %sum_keep_kernel.1 = (bf16[1024,512]{1,0:T(8,128)(2,1)}, bf16[1024,512]{1,0:T(8,128)(2,1)}, bf16[2048,512]{1,0:T(8,128)(2,1)}) custom-call(s32[4]{0:T(128)} %pad_add_fusion.pos, bf16[256,4096]{1,0:T(8,128)(2,1)} %get-tuple-element.120.act.left, bf16[256,1024]{1,0:T(8,128)(2,1)} %get-tuple-element.139.grad_low.right, ...), custom_call_target="tpu_custom_call" | custom-call | flops 64424509440 | bytes 330301920 | tf_op jit(solution)/shard_map/sum_keep_kernel/pallas_call | solution.py:67
  277.8 6.4 %copies_keep_kernel.1 = (bf16[64,4096]{1,0:T(8,128)(2,1)}, bf16[208,4096]{1,0:T(8,128)(2,1)}, bf16[256,4096]{1,0:T(8,128)(2,1)}, f32[8,1024]{1,0:T(8,128)}) custom-call(s32[4]{0:T(128)} %pad_add_fusion.pos, bf16[256,1024]{1,0:T(8,128)(2,1)} %get-tuple-element.131.left, bf16[256,4096]{1,0:T(8,128)(2,1)} %get-tuple-element.132.right, ...), custom_call_target="tpu_custom_call" | custom-call | flops 32212254720 | bytes 340132320 | tf_op jit(solution)/shard_map/copies_keep_kernel/pallas_call | solution.py:67
  285.0 13.9 %hidden_back_kernel.1 = (f32[256,1024]{1,0:T(8,128)}, bf16[256,1024]{1,0:T(8,128)(2,1)}, f32[8,1024]{1,0:T(8,128)}, bf16[1024,2560]{1,0:T(8,128)(2,1)}) custom-call(s32[4]{0:T(128)} %pad_add_fusion.pos, bf16[256,4096]{1,0:T(8,128)(2,1)} %pre_back_kernel.1.grad_pre, f32[256,1024]{1,0:T(8,128)} %get-tuple-element.121.hidden, ...), custom_call_target="tpu_custom_call" | custom-call | flops 112742891520 | bytes 615383552 | tf_op jit(solution)/shard_map/hidden_back_kernel/pallas_call | solution.py:67
  306.1 17.8 %attend_back_kernel.1 = (bf16[256,3072]{1,0:T(8,128)(2,1)}, f32[256,1024]{1,0:T(8,128)}, f32[8,1024]{1,0:T(8,128)}) custom-call(s32[4]{0:T(128)} %pad_add_fusion.pos, bf16[256,1024]{1,0:T(8,128)(2,1)} %get-tuple-element.160.grad_low, bf16[256,3072]{1,0:T(8,128)(2,1)} %get-tuple-element.161.qkv, bf16[256,1024]{1,0:T(8,128)(2,1)} %tokens.3, ...), custom_call_target="tpu_custom_call" | custom-call | flops 128849018880 | bytes 458097120 | tf_op jit(solution)/shard_map/attend_back_kernel/pallas_call | solution.py:67
  324.7 4.7 collective-permute-done.36
  332.9 11.6 %wide_keep_kernel.1 = (bf16[256,2560]{1,0:T(8,128)(2,1)}, bf16[256,2560]{1,0:T(8,128)(2,1)}, bf16[512,2560]{1,0:T(8,128)(2,1)}, bf16[1040,1536]{1,0:T(8,128)(2,1)}) custom-call(s32[4]{0:T(128)} %pad_add_fusion.pos, bf16[256,1024]{1,0:T(8,128)(2,1)} %get-tuple-element.114.ffn_in.refs_8_, bf16[256,1024]{1,0:T(8,128)(2,1)} %get-tuple-element.156.refs_9_.heads, ...), custom_call_target="tpu_custom_call" | custom-call | flops 80530636800 | bytes 585400832 | tf_op jit(solution)/shard_map/wide_keep_kernel/pallas_call | solution.py:67
  345.9 7.5 %copies_whole_kernel.1 = f32[1024,1024]{1,0:T(8,128)} custom-call(s32[4]{0:T(128)} %pad_add_fusion.pos, bf16[256,3072]{1,0:T(8,128)(2,1)} %get-tuple-element.143.kept, bf16[256,1024]{1,0:T(8,128)(2,1)} %copy-done.26, bf16[256,1024]{1,0:T(8,128)(2,1)} %copy-done.28, bf16[256,1024]{1,0:T(8,128)(2,1)} %copy-done.30, ...), custom_call_target="tpu_custom_call" | custom-call | flops 64424509440 | bytes 314573280 | tf_op jit(solution)/shard_map/copies_whole_kernel/pallas_call | solution.py:67
  353.4 9.0 %collective-permute-done.40 = bf16[256,2560]{1,0:T(8,128)(2,1)S(1)} collective-permute-done((bf16[256,2560]{1,0:T(8,128)(2,1)}, bf16[256,2560]{1,0:T(8,128)(2,1)S(1)}, u32[]{:S(2)}, u32[]{:S(2)}) %collective-permute-start.40) | collective-permute-done | bytes 1310752 | tf_op jit(solution)/shard_map/ppermute | solution.py:21
  363.7 6.2 %last_keep_kernel.1 = (bf16[272,1536]{1,0:T(8,128)(2,1)}, bf16[256,1536]{1,0:T(8,128)(2,1)}, bf16[512,1536]{1,0:T(8,128)(2,1)}, f32[8,1536]{1,0:T(8,128)}) custom-call(s32[4]{0:T(128)} %pad_add_fusion.pos, bf16[256,1024]{1,0:T(8,128)(2,1)} %get-tuple-element.168.attn_in.left, bf16[256,3072]{1,0:T(8,128)(2,1)} %get-tuple-element.163.grad_qkv.right, ...), custom_call_target="tpu_custom_call" | custom-call | flops 32212254720 | bytes 258048480 | tf_op jit(solution)/shard_map/last_keep_kernel/pallas_call | solution.py:67
  373.2 21.4 %collective-permute-done.42 = bf16[512,512]{1,0:T(8,128)(2,1)S(1)} collective-permute-done((bf16[512,512]{1,0:T(8,128)(2,1)S(1)}, bf16[512,512]{1,0:T(8,128)(2,1)S(1)}, u32[]{:S(2)}, u32[]{:S(2)}) %collective-permute-start.42) | collective-permute-done | bytes 524320 | tf_op jit(solution)/shard_map/ppermute | solution.py:21
  395.8 3.5 all-to-all-start.3
  399.3 4.0 collective-permute-done.46
  407.0 2.2 convert_add_fusion
  417.3 8.6 %collective-permute-done.52 = bf16[64,2560]{1,0:T(8,128)(2,1)S(1)} collective-permute-done((bf16[64,2560]{1,0:T(8,128)(2,1)}, bf16[64,2560]{1,0:T(8,128)(2,1)S(1)}, u32[]{:S(2)}, u32[]{:S(2)}) %collective-permute-start.52) | collective-permute-done | bytes 327712 | tf_op jit(solution)/shard_map/ppermute | solution.py:21
  426.3 2.7 collective-permute-done.54
  429.0 13.3 %collective-permute-done.53 = bf16[64,2560]{1,0:T(8,128)(2,1)} collective-permute-done((bf16[64,2560]{1,0:T(8,128)(2,1)}, bf16[64,2560]{1,0:T(8,128)(2,1)}, u32[]{:S(2)}, u32[]{:S(2)}) %collective-permute-start.53) | collective-permute-done | bytes 327712 | tf_op jit(solution)/shard_map/ppermute | solution.py:21
  449.4 2.6 collective-permute-start.50
  453.6 6.5 %collective-permute-done.48 = bf16[80,1536]{1,0:T(8,128)(2,1)S(1)} collective-permute-done((bf16[80,1536]{1,0:T(8,128)(2,1)S(1)}, bf16[80,1536]{1,0:T(8,128)(2,1)S(1)}, u32[]{:S(2)}, u32[]{:S(2)}) %collective-permute-start.48) | collective-permute-done | bytes 245792 | tf_op jit(solution)/shard_map/ppermute | solution.py:21
  460.2 7.8 %collective-permute-done.49 = bf16[80,1536]{1,0:T(8,128)(2,1)S(1)} collective-permute-done((bf16[80,1536]{1,0:T(8,128)(2,1)S(1)}, bf16[80,1536]{1,0:T(8,128)(2,1)S(1)}, u32[]{:S(2)}, u32[]{:S(2)}) %collective-permute-start.49) | collective-permute-done | bytes 245792 | tf_op jit(solution)/shard_map/ppermute | solution.py:21
  468.8 3.2 collective-permute-done.56
  475.8 3.8 add_bitcast_fusion
  (258 shorter events, 82.4 us)
Async XLA Ops:
  15.7 26.6 %collective-permute-start.2 = (bf16[128,2176]{1,0:T(8,128)(2,1)S(1)}, bf16[128,2176]{1,0:T(8,128)(2,1)S(1)}, u32[]{:S(2)}, u32[]{:S(2)}) collective-permute-start(bf16[128,2176]{1,0:T(8,128)(2,1)S(1)} %pad_maximum_fusion.12.refs_0_), channel_id=1, source_target_pairs={{0,4},{1,3},{2,6},{3,1},{4,0},{5,7},{6,2},{7,5},{8,12},{9,11},{10,... | collective-permute-start | bytes 1671176 | tf_op jit(solution)/shard_map/ppermute | solution.py:21
  17.4 24.8 %collective-permute-start.5 = (bf16[64,2048]{1,0:T(8,128)(2,1)S(1)}, bf16[64,2048]{1,0:T(8,128)(2,1)S(1)}, u32[]{:S(2)}, u32[]{:S(2)}) collective-permute-start(bf16[64,2048]{1,0:T(8,128)(2,1)S(1)} %maximum_select_fusion.4), channel_id=1, source_target_pairs={{0,8},{1,9},{2,10},{3,11},{4,12},{5,13},{6,14},{7,15},{8,0},{9,1},... | collective-permute-start | bytes 786440 | tf_op jit(solution)/shard_map/ppermute | solution.py:21
  19.0 22.6 %collective-permute-start.7 = (bf16[256,512]{1,0:T(8,128)(2,1)S(1)}, bf16[256,512]{1,0:T(8,128)(2,1)S(1)}, u32[]{:S(2)}, u32[]{:S(2)}) collective-permute-start(bf16[256,512]{1,0:T(8,128)(2,1)S(1)} %maximum_select_fusion.5), channel_id=1, source_target_pairs={{0,8},{1,9},{2,10},{3,11},{4,12},{5,13},{6,14},{7,15},{8,0},{9,1},... | collective-permute-start | bytes 786440 | tf_op jit(solution)/shard_map/ppermute | solution.py:21
  19.5 26.4 %collective-permute-start.3 = (bf16[128,2176]{1,0:T(8,128)(2,1)S(1)}, bf16[128,2176]{1,0:T(8,128)(2,1)S(1)}, u32[]{:S(2)}, u32[]{:S(2)}) collective-permute-start(bf16[128,2176]{1,0:T(8,128)(2,1)S(1)} %pad_maximum_fusion.12.refs_0_), channel_id=1, source_target_pairs={{0,16},{1,17},{2,18},{3,19},{4,20},{5,21},{6,22},{7,23},{8,24},{9,... | collective-permute-start | bytes 1671176 | tf_op jit(solution)/shard_map/ppermute | solution.py:21
  45.8 26.5 %collective-permute-start.8 = (bf16[256,2176]{1,0:T(8,128)(2,1)S(1)}, bf16[256,2176]{1,0:T(8,128)(2,1)S(1)}, u32[]{:S(2)}, u32[]{:S(2)}) collective-permute-start(bf16[256,2176]{1,0:T(8,128)(2,1)S(1)} %pad_maximum_fusion.6), channel_id=1, source_target_pairs={{0,2},{1,5},{2,0},{3,7},{4,6},{5,1},{6,4},{7,3},{8,10},{9,13},{10,... | collective-permute-start | bytes 3342344 | tf_op jit(solution)/shard_map/ppermute | solution.py:21
  46.4 27.2 %collective-permute-start.9 = (bf16[128,2176]{1,0:T(8,128)(2,1)S(1)}, bf16[128,2176]{1,0:T(8,128)(2,1)S(1)}, u32[]{:S(2)}, u32[]{:S(2)}) collective-permute-start(bf16[128,2176]{1,0:T(8,128)(2,1)S(1)} %collective-permute-done.3.refs_3_), channel_id=1, source_target_pairs={{0,4},{1,3},{2,6},{3,1},{4,0},{5,7},{6,2},{7,5},{8,12},{9,11},{10,... | collective-permute-start | bytes 1671176 | tf_op jit(solution)/shard_map/ppermute | solution.py:21
  47.8 25.5 %collective-permute-start.11 = (bf16[128,2048]{1,0:T(8,128)(2,1)S(1)}, bf16[128,2048]{1,0:T(8,128)(2,1)S(1)}, u32[]{:S(2)}, u32[]{:S(2)}) collective-permute-start(bf16[128,2048]{1,0:T(8,128)(2,1)S(1)} %constant_dynamic-update-slice_fusion.refs_0_), channel_id=1, source_target_pairs={{0,4},{1,3},{2,6},{3,1},{4,0},{5,7},{6,2},{7,5},{8,12},{9,11},{10,... | collective-permute-start | bytes 1572872 | tf_op jit(solution)/shard_map/ppermute | solution.py:21
  48.4 25.2 %collective-permute-start.10 = (bf16[128,2048]{1,0:T(8,128)(2,1)S(1)}, bf16[128,2048]{1,0:T(8,128)(2,1)S(1)}, u32[]{:S(2)}, u32[]{:S(2)}) collective-permute-start(bf16[128,2048]{1,0:T(8,128)(2,1)S(1)} %constant_dynamic-update-slice_fusion.refs_0_), channel_id=1, source_target_pairs={{0,16},{1,17},{2,18},{3,19},{4,20},{5,21},{6,22},{7,23},{8,24},{9,... | collective-permute-start | bytes 1572872 | tf_op jit(solution)/shard_map/ppermute | solution.py:21
  73.6 32.6 %collective-permute-start.13 = (bf16[512,2176]{1,0:T(8,128)(2,1)S(1)}, bf16[512,2176]{1,0:T(8,128)(2,1)S(1)}, u32[]{:S(2)}, u32[]{:S(2)}) collective-permute-start(bf16[512,2176]{1,0:T(8,128)(2,1)S(1)} %pad_maximum_fusion), channel_id=1, source_target_pairs={{0,1},{1,0},{2,3},{3,2},{4,5},{5,4},{6,7},{7,6},{8,9},{9,8},{10,11... | collective-permute-start | bytes 6684680 | tf_op jit(solution)/shard_map/ppermute | solution.py:21
  73.8 21.2 %collective-permute-start.12 = (bf16[256,2176]{1,0:T(8,128)(2,1)S(1)}, bf16[256,2176]{1,0:T(8,128)(2,1)S(1)}, u32[]{:S(2)}, u32[]{:S(2)}) collective-permute-start(bf16[256,2176]{1,0:T(8,128)(2,1)S(1)} %pad_maximum_fusion.7), channel_id=1, source_target_pairs={{0,2},{1,5},{2,0},{3,7},{4,6},{5,1},{6,4},{7,3},{8,10},{9,13},{10,... | collective-permute-start | bytes 3342344 | tf_op jit(solution)/shard_map/ppermute | solution.py:21
  74.3 31.9 %collective-permute-start.15 = (bf16[256,2048]{1,0:T(8,128)(2,1)S(1)}, bf16[256,2048]{1,0:T(8,128)(2,1)S(1)}, u32[]{:S(2)}, u32[]{:S(2)}) collective-permute-start(bf16[256,2048]{1,0:T(8,128)(2,1)S(1)} %pad_maximum_fusion.8), channel_id=1, source_target_pairs={{0,2},{1,5},{2,0},{3,7},{4,6},{5,1},{6,4},{7,3},{8,10},{9,13},{10,... | collective-permute-start | bytes 3145736 | tf_op jit(solution)/shard_map/ppermute | solution.py:21
  76.1 26.2 %collective-permute-start.14 = (bf16[512,512]{1,0:T(8,128)(2,1)}, bf16[512,512]{1,0:T(8,128)(2,1)}, u32[]{:S(2)}, u32[]{:S(2)}) collective-permute-start(bf16[512,512]{1,0:T(8,128)(2,1)} %constant_dynamic-update-slice_fusion.2.refs_0_), channel_id=1, source_target_pairs={{0,16},{1,17},{2,18},{3,19},{4,20},{5,21},{6,22},{7,23},{8,24},{9,... | collective-permute-start | bytes 1572872 | tf_op jit(solution)/shard_map/ppermute | solution.py:21
  76.1 26.2 %collective-permute-start.16 = (bf16[128,2048]{1,0:T(8,128)(2,1)S(1)}, bf16[128,2048]{1,0:T(8,128)(2,1)S(1)}, u32[]{:S(2)}, u32[]{:S(2)}) collective-permute-start(bf16[128,2048]{1,0:T(8,128)(2,1)S(1)} %collective-permute-done.10.refs_3_), channel_id=1, source_target_pairs={{0,4},{1,3},{2,6},{3,1},{4,0},{5,7},{6,2},{7,5},{8,12},{9,11},{10,... | collective-permute-start | bytes 1572872 | tf_op jit(solution)/shard_map/ppermute | solution.py:21
  106.2 34.5 %collective-permute-start.17 = (bf16[512,2176]{1,0:T(8,128)(2,1)}, bf16[512,2176]{1,0:T(8,128)(2,1)}, u32[]{:S(2)}, u32[]{:S(2)}) collective-permute-start(bf16[512,2176]{1,0:T(8,128)(2,1)} %pad_maximum_fusion.1), channel_id=1, source_target_pairs={{0,1},{1,0},{2,3},{3,2},{4,5},{5,4},{6,7},{7,6},{8,9},{9,8},{10,11... | collective-permute-start | bytes 6684680 | tf_op jit(solution)/shard_map/ppermute | solution.py:21
  106.6 34.2 %collective-permute-start.19 = (bf16[512,2048]{1,0:T(8,128)(2,1)S(1)}, bf16[512,2048]{1,0:T(8,128)(2,1)}, u32[]{:S(2)}, u32[]{:S(2)}) collective-permute-start(bf16[512,2048]{1,0:T(8,128)(2,1)S(1)} %pad_maximum_fusion.2), channel_id=1, source_target_pairs={{0,1},{1,0},{2,3},{3,2},{4,5},{5,4},{6,7},{7,6},{8,9},{9,8},{10,11... | collective-permute-start | bytes 6291464 | tf_op jit(solution)/shard_map/ppermute | solution.py:21
  108.3 29.7 %collective-permute-start.18 = (bf16[256,2048]{1,0:T(8,128)(2,1)}, bf16[256,2048]{1,0:T(8,128)(2,1)}, u32[]{:S(2)}, u32[]{:S(2)}) collective-permute-start(bf16[256,2048]{1,0:T(8,128)(2,1)} %pad_maximum_fusion.9), channel_id=1, source_target_pairs={{0,2},{1,5},{2,0},{3,7},{4,6},{5,1},{6,4},{7,3},{8,10},{9,13},{10,... | collective-permute-start | bytes 3145736 | tf_op jit(solution)/shard_map/ppermute | solution.py:21
  108.6 27.2 %collective-permute-start.20 = (bf16[512,512]{1,0:T(8,128)(2,1)}, bf16[512,512]{1,0:T(8,128)(2,1)}, u32[]{:S(2)}, u32[]{:S(2)}) collective-permute-start(bf16[512,512]{1,0:T(8,128)(2,1)} %constant_dynamic-update-slice_fusion.2.refs_0_), channel_id=1, source_target_pairs={{0,4},{1,3},{2,6},{3,1},{4,0},{5,7},{6,2},{7,5},{8,12},{9,11},{10,... | collective-permute-start | bytes 1572872 | tf_op jit(solution)/shard_map/ppermute | solution.py:21
  109.0 24.7 %collective-permute-start.21 = (bf16[512,512]{1,0:T(8,128)(2,1)}, bf16[512,512]{1,0:T(8,128)(2,1)}, u32[]{:S(2)}, u32[]{:S(2)}) collective-permute-start(bf16[512,512]{1,0:T(8,128)(2,1)} %collective-permute-done.14.refs_3_), channel_id=1, source_target_pairs={{0,4},{1,3},{2,6},{3,1},{4,0},{5,7},{6,2},{7,5},{8,12},{9,11},{10,... | collective-permute-start | bytes 1572872 | tf_op jit(solution)/shard_map/ppermute | solution.py:21
  140.8 42.5 %collective-permute-start.26 = (bf16[1024,512]{1,0:T(8,128)(2,1)}, bf16[1024,512]{1,0:T(8,128)(2,1)}, u32[]{:S(2)}, u32[]{:S(2)}) collective-permute-start(bf16[1024,512]{1,0:T(8,128)(2,1)} %pad_maximum_fusion.11), channel_id=1, source_target_pairs={{0,1},{1,0},{2,3},{3,2},{4,5},{5,4},{6,7},{7,6},{8,9},{9,8},{10,11... | collective-permute-start | bytes 3145736 | tf_op jit(solution)/shard_map/ppermute | solution.py:21
  140.8 27.9 %collective-permute-start.24 = (bf16[1024,512]{1,0:T(8,128)(2,1)}, bf16[1024,512]{1,0:T(8,128)(2,1)}, u32[]{:S(2)}, u32[]{:S(2)}) collective-permute-start(bf16[1024,512]{1,0:T(8,128)(2,1)} %pad_maximum_fusion.11), channel_id=1, source_target_pairs={{0,2},{1,5},{2,0},{3,7},{4,6},{5,1},{6,4},{7,3},{8,10},{9,13},{10,... | collective-permute-start | bytes 3145736 | tf_op jit(solution)/shard_map/ppermute | solution.py:21
  141.2 25.9 %collective-permute-start.23 = (bf16[1024,512]{1,0:T(8,128)(2,1)}, bf16[1024,512]{1,0:T(8,128)(2,1)S(1)}, u32[]{:S(2)}, u32[]{:S(2)}) collective-permute-start(bf16[1024,512]{1,0:T(8,128)(2,1)} %pad_maximum_fusion.10), channel_id=1, source_target_pairs={{0,2},{1,5},{2,0},{3,7},{4,6},{5,1},{6,4},{7,3},{8,10},{9,13},{10,... | collective-permute-start | bytes 3145736 | tf_op jit(solution)/shard_map/ppermute | solution.py:21
  142.9 25.8 %collective-permute-start.22 = (bf16[512,2048]{1,0:T(8,128)(2,1)}, bf16[512,2048]{1,0:T(8,128)(2,1)}, u32[]{:S(2)}, u32[]{:S(2)}) collective-permute-start(bf16[512,2048]{1,0:T(8,128)(2,1)} %pad_maximum_fusion.3), channel_id=1, source_target_pairs={{0,1},{1,0},{2,3},{3,2},{4,5},{5,4},{6,7},{7,6},{8,9},{9,8},{10,11... | collective-permute-start | bytes 6291464 | tf_op jit(solution)/shard_map/ppermute | solution.py:21
  153.7 38.5 %all-to-all-start = ((bf16[8,32,1024]{2,1,0:T(8,128)(2,1)}), bf16[8,32,1024]{2,1,0:T(8,128)(2,1)S(1)}, u32[]{:S(2)}, u32[]{:S(2)}) async-start(bf16[8,32,1024]{2,1,0:T(8,128)(2,1)} %bitcast.7), calls=%async_computation | async-start | bytes 1048576 | tf_op jit(solution)/shard_map/all_to_all | solution.py:716
  192.2 20.7 %all-to-all-start.1 = ((bf16[8,32,1024]{2,1,0:T(8,128)(2,1)}), bf16[8,32,1024]{2,1,0:T(8,128)(2,1)S(1)}, u32[]{:S(2)}, u32[]{:S(2)}) async-start(bf16[8,32,1024]{2,1,0:T(8,128)(2,1)} %bitcast.27), calls=%async_computation.1 | async-start | bytes 1048576 | tf_op jit(solution)/shard_map/all_to_all | solution.py:716
  230.1 18.5 %all-to-all-start.2 = ((bf16[8,32,1024]{2,1,0:T(8,128)(2,1)}), bf16[8,32,1024]{2,1,0:T(8,128)(2,1)S(1)}, u32[]{:S(2)}, u32[]{:S(2)}) async-start(bf16[8,32,1024]{2,1,0:T(8,128)(2,1)} %bitcast.28), calls=%async_computation.2 | async-start | bytes 1048576 | tf_op jit(solution)/shard_map/all_to_all | solution.py:716
  239.8 30.9 %collective-permute-start.31 = (bf16[256,3072]{1,0:T(8,128)(2,1)S(1)}, bf16[256,3072]{1,0:T(8,128)(2,1)}, u32[]{:S(2)}, u32[]{:S(2)}) collective-permute-start(bf16[256,3072]{1,0:T(8,128)(2,1)S(1)} %copy-done.38), channel_id=1, source_target_pairs={{0,1},{1,0},{2,3},{3,2},{4,5},{5,4},{6,7},{7,6},{8,9},{9,8},{10,11... | collective-permute-start | bytes 4718600 | tf_op jit(solution)/shard_map/ppermute | solution.py:21
  264.7 19.4 %collective-permute-start.35 = (bf16[256,1024]{1,0:T(8,128)(2,1)S(1)}, bf16[256,1024]{1,0:T(8,128)(2,1)S(1)}, u32[]{:S(2)}, u32[]{:S(2)}) collective-permute-start(bf16[256,1024]{1,0:T(8,128)(2,1)S(1)} %copy-done.40), channel_id=1, source_target_pairs={{0,2},{1,3},{2,0},{3,1},{4,6},{5,7},{6,4},{7,5},{8,10},{9,11},{10,... | collective-permute-start | bytes 1572872 | tf_op jit(solution)/shard_map/ppermute | solution.py:21
  284.2 17.9 %collective-permute-start.33 = (bf16[1024,512]{1,0:T(8,128)(2,1)}, bf16[1024,512]{1,0:T(8,128)(2,1)S(1)}, u32[]{:S(2)}, u32[]{:S(2)}) collective-permute-start(bf16[1024,512]{1,0:T(8,128)(2,1)} %get-tuple-element.147), channel_id=1, source_target_pairs={{0,2},{1,5},{2,0},{3,7},{4,6},{5,1},{6,4},{7,3},{8,10},{9,13},{10,... | collective-permute-start | bytes 3145736 | tf_op jit(solution)/shard_map/ppermute | solution.py:21
  298.9 33.9 %collective-permute-start.38 = (bf16[1024,2560]{1,0:T(8,128)(2,1)}, bf16[1024,2560]{1,0:T(8,128)(2,1)}, u32[]{:S(2)}, u32[]{:S(2)}) collective-permute-start(bf16[1024,2560]{1,0:T(8,128)(2,1)} %get-tuple-element.157), channel_id=1, source_target_pairs={{0,1},{1,0},{2,3},{3,2},{4,5},{5,4},{6,7},{7,6},{8,9},{9,8},{10,11... | collective-permute-start | bytes 15728648 | tf_op jit(solution)/shard_map/ppermute | solution.py:21
  301.7 31.2 %collective-permute-start.37 = (bf16[768,1024]{1,0:T(8,128)(2,1)S(1)}, bf16[768,1024]{1,0:T(8,128)(2,1)}, u32[]{:S(2)}, u32[]{:S(2)}) collective-permute-start(bf16[768,1024]{1,0:T(8,128)(2,1)S(1)} %pad_maximum_fusion.5), channel_id=1, source_target_pairs={{0,1},{1,0},{2,3},{3,2},{4,5},{5,4},{6,7},{7,6},{8,9},{9,8},{10,11... | collective-permute-start | bytes 4718600 | tf_op jit(solution)/shard_map/ppermute | solution.py:21
  303.4 26.1 %collective-permute-start.36 = (bf16[1024,512]{1,0:T(8,128)(2,1)}, bf16[1024,512]{1,0:T(8,128)(2,1)S(1)}, u32[]{:S(2)}, u32[]{:S(2)}) collective-permute-start(bf16[1024,512]{1,0:T(8,128)(2,1)} %add_convert_fusion.1), channel_id=1, source_target_pairs={{0,4},{1,3},{2,6},{3,1},{4,0},{5,7},{6,2},{7,5},{8,12},{9,11},{10,... | collective-permute-start | bytes 3145736 | tf_op jit(solution)/shard_map/ppermute | solution.py:21
  304.8 26.3 %collective-permute-start.34 = (bf16[1024,512]{1,0:T(8,128)(2,1)}, bf16[1024,512]{1,0:T(8,128)(2,1)S(1)}, u32[]{:S(2)}, u32[]{:S(2)}) collective-permute-start(bf16[1024,512]{1,0:T(8,128)(2,1)} %get-tuple-element.148), channel_id=1, source_target_pairs={{0,2},{1,5},{2,0},{3,7},{4,6},{5,1},{6,4},{7,3},{8,10},{9,13},{10,... | collective-permute-start | bytes 3145736 | tf_op jit(solution)/shard_map/ppermute | solution.py:21
  323.9 20.6 %collective-permute-start.39 = (bf16[64,4096]{1,0:T(8,128)(2,1)}, bf16[64,4096]{1,0:T(8,128)(2,1)}, u32[]{:S(2)}, u32[]{:S(2)}) collective-permute-start(bf16[64,4096]{1,0:T(8,128)(2,1)} %get-tuple-element.173), channel_id=1, source_target_pairs={{0,2},{1,3},{2,0},{3,1},{4,6},{5,7},{6,4},{7,5},{8,10},{9,11},{10,... | collective-permute-start | bytes 1572872 | tf_op jit(solution)/shard_map/ppermute | solution.py:21
  344.4 19.3 %collective-permute-start.41 = (bf16[1040,1536]{1,0:T(8,128)(2,1)}, bf16[1040,1536]{1,0:T(8,128)(2,1)}, u32[]{:S(2)}, u32[]{:S(2)}) collective-permute-start(bf16[1040,1536]{1,0:T(8,128)(2,1)} %get-tuple-element.171), channel_id=1, source_target_pairs={{0,1},{1,0},{2,3},{3,2},{4,5},{5,4},{6,7},{7,6},{8,9},{9,8},{10,11... | collective-permute-start | bytes 9584648 | tf_op jit(solution)/shard_map/ppermute | solution.py:21
  344.5 17.9 %collective-permute-start.40 = (bf16[256,2560]{1,0:T(8,128)(2,1)}, bf16[256,2560]{1,0:T(8,128)(2,1)S(1)}, u32[]{:S(2)}, u32[]{:S(2)}) collective-permute-start(bf16[256,2560]{1,0:T(8,128)(2,1)} %get-tuple-element.175), channel_id=1, source_target_pairs={{0,2},{1,5},{2,0},{3,7},{4,6},{5,1},{6,4},{7,3},{8,10},{9,13},{10,... | collective-permute-start | bytes 3932168 | tf_op jit(solution)/shard_map/ppermute | solution.py:21
  362.4 44.6 %collective-permute-start.43 = (bf16[256,2560]{1,0:T(8,128)(2,1)}, bf16[256,2560]{1,0:T(8,128)(2,1)}, u32[]{:S(2)}, u32[]{:S(2)}) collective-permute-start(bf16[256,2560]{1,0:T(8,128)(2,1)} %get-tuple-element.184), channel_id=1, source_target_pairs={{0,2},{1,5},{2,0},{3,7},{4,6},{5,1},{6,4},{7,3},{8,10},{9,13},{10,... | collective-permute-start | bytes 3932168 | tf_op jit(solution)/shard_map/ppermute | solution.py:21
  370.0 24.6 %collective-permute-start.42 = (bf16[512,512]{1,0:T(8,128)(2,1)S(1)}, bf16[512,512]{1,0:T(8,128)(2,1)S(1)}, u32[]{:S(2)}, u32[]{:S(2)}) collective-permute-start(bf16[512,512]{1,0:T(8,128)(2,1)S(1)} %slice.218), channel_id=1, source_target_pairs={{0,16},{1,17},{2,18},{3,19},{4,20},{5,21},{6,22},{7,23},{8,24},{9,... | collective-permute-start | bytes 1572872 | tf_op jit(solution)/shard_map/ppermute | solution.py:21
  370.1 33.2 %collective-permute-start.46 = (bf16[272,1536]{1,0:T(8,128)(2,1)}, bf16[272,1536]{1,0:T(8,128)(2,1)}, u32[]{:S(2)}, u32[]{:S(2)}) collective-permute-start(bf16[272,1536]{1,0:T(8,128)(2,1)} %get-tuple-element.187), channel_id=1, source_target_pairs={{0,2},{1,5},{2,0},{3,7},{4,6},{5,1},{6,4},{7,3},{8,10},{9,13},{10,... | collective-permute-start | bytes 2506760 | tf_op jit(solution)/shard_map/ppermute | solution.py:21
  372.6 34.4 %collective-permute-start.44 = (bf16[256,2560]{1,0:T(8,128)(2,1)}, bf16[256,2560]{1,0:T(8,128)(2,1)}, u32[]{:S(2)}, u32[]{:S(2)}) collective-permute-start(bf16[256,2560]{1,0:T(8,128)(2,1)} %add_convert_fusion), channel_id=1, source_target_pairs={{0,4},{1,3},{2,6},{3,1},{4,0},{5,7},{6,2},{7,5},{8,12},{9,11},{10,... | collective-permute-start | bytes 3932168 | tf_op jit(solution)/shard_map/ppermute | solution.py:21
  395.8 19.4 %all-to-all-start.3 = ((bf16[8,32,1024]{2,1,0:T(8,128)(2,1)}), bf16[8,32,1024]{2,1,0:T(8,128)(2,1)S(1)}, u32[]{:S(2)}, u32[]{:S(2)}) async-start(bf16[8,32,1024]{2,1,0:T(8,128)(2,1)} %bitcast.13), calls=%async_computation.3 | async-start | bytes 1048576 | tf_op jit(solution)/shard_map/all_to_all | solution.py:716
  406.4 37.3 %collective-permute-start.47 = (bf16[272,1536]{1,0:T(8,128)(2,1)}, bf16[272,1536]{1,0:T(8,128)(2,1)}, u32[]{:S(2)}, u32[]{:S(2)}) collective-permute-start(bf16[272,1536]{1,0:T(8,128)(2,1)} %fusion.1), channel_id=1, source_target_pairs={{0,4},{1,3},{2,6},{3,1},{4,0},{5,7},{6,2},{7,5},{8,12},{9,11},{10,... | collective-permute-start | bytes 2506760 | tf_op jit(solution)/shard_map/ppermute | solution.py:21
  409.1 36.8 %collective-permute-start.45 = (bf16[256,1536]{1,0:T(8,128)(2,1)}, bf16[256,1536]{1,0:T(8,128)(2,1)}, u32[]{:S(2)}, u32[]{:S(2)}) collective-permute-start(bf16[256,1536]{1,0:T(8,128)(2,1)} %get-tuple-element.186), channel_id=1, source_target_pairs={{0,2},{1,5},{2,0},{3,7},{4,6},{5,1},{6,4},{7,3},{8,10},{9,13},{10,... | collective-permute-start | bytes 2359304 | tf_op jit(solution)/shard_map/ppermute | solution.py:21
  412.0 17.1 %collective-permute-start.54 = (bf16[64,2560]{1,0:T(8,128)(2,1)}, bf16[64,2560]{1,0:T(8,128)(2,1)}, u32[]{:S(2)}, u32[]{:S(2)}) collective-permute-start(bf16[64,2560]{1,0:T(8,128)(2,1)} %get-tuple-element.199), channel_id=1, source_target_pairs={{0,24},{1,25},{2,26},{3,27},{4,28},{5,29},{6,30},{7,31},{8,16},{9,... | collective-permute-start | bytes 983048 | tf_op jit(solution)/shard_map/ppermute | solution.py:21
  413.0 29.4 %collective-permute-start.53 = (bf16[64,2560]{1,0:T(8,128)(2,1)}, bf16[64,2560]{1,0:T(8,128)(2,1)}, u32[]{:S(2)}, u32[]{:S(2)}) collective-permute-start(bf16[64,2560]{1,0:T(8,128)(2,1)} %get-tuple-element.200), channel_id=1, source_target_pairs={{0,16},{1,17},{2,18},{3,19},{4,20},{5,21},{6,22},{7,23},{8,24},{9,... | collective-permute-start | bytes 983048 | tf_op jit(solution)/shard_map/ppermute | solution.py:21
  425.9 48.5 %collective-permute-start.58 = (bf16[208,4096]{1,0:T(8,128)(2,1)S(1)}, bf16[208,4096]{1,0:T(8,128)(2,1)S(1)}, u32[]{:S(2)}, u32[]{:S(2)}) collective-permute-start(bf16[208,4096]{1,0:T(8,128)(2,1)S(1)} %copy-done.37), channel_id=1, source_target_pairs={{0,2},{1,3},{2,0},{3,1},{4,6},{5,7},{6,4},{7,5},{8,10},{9,11},{10,... | collective-permute-start | bytes 5111816 | tf_op jit(solution)/shard_map/ppermute | solution.py:21
  447.6 20.4 %collective-permute-start.49 = (bf16[80,1536]{1,0:T(8,128)(2,1)S(1)}, bf16[80,1536]{1,0:T(8,128)(2,1)S(1)}, u32[]{:S(2)}, u32[]{:S(2)}) collective-permute-start(bf16[80,1536]{1,0:T(8,128)(2,1)S(1)} %get-tuple-element.211), channel_id=1, source_target_pairs={{0,16},{1,17},{2,18},{3,19},{4,20},{5,21},{6,22},{7,23},{8,24},{9,... | collective-permute-start | bytes 737288 | tf_op jit(solution)/shard_map/ppermute | solution.py:21
  449.4 18.6 %collective-permute-start.50 = (bf16[80,1536]{1,0:T(8,128)(2,1)S(1)}, bf16[80,1536]{1,0:T(8,128)(2,1)S(1)}, u32[]{:S(2)}, u32[]{:S(2)}) collective-permute-start(bf16[80,1536]{1,0:T(8,128)(2,1)S(1)} %get-tuple-element.212), channel_id=1, source_target_pairs={{0,24},{1,25},{2,26},{3,27},{4,28},{5,29},{6,30},{7,31},{8,16},{9,... | collective-permute-start | bytes 737288 | tf_op jit(solution)/shard_map/ppermute | solution.py:21
  453.6 18.5 %collective-permute-start.56 = (bf16[256,512]{1,0:T(8,128)(2,1)S(1)}, bf16[256,512]{1,0:T(8,128)(2,1)S(1)}, u32[]{:S(2)}, u32[]{:S(2)}) collective-permute-start(bf16[256,512]{1,0:T(8,128)(2,1)S(1)} %slice.219), channel_id=1, source_target_pairs={{0,8},{1,9},{2,10},{3,11},{4,12},{5,13},{6,14},{7,15},{8,0},{9,1},... | collective-permute-start | bytes 786440 | tf_op jit(solution)/shard_map/ppermute | solution.py:21
  (58 other events, 657.6 us)

commit v2 on v1

--- a/solution.py
+++ b/solution.py
@@ -219,7 +219,7 @@
         )
         return 0
 
-    lax.fori_loop(0, HEADS // 2, pair, 0, unroll=True)
+    lax.fori_loop(0, HEADS // 2, pair, 0)
     hidden[...] = inputs + dot_nn(heads[...], weight[:, 3 * width : 4 * width])
     norm_two, _ = normed(hidden[...])
     ffn_in[...] = (norm_two * gains[1:2, :]).astype(BF16)

time: 488 us -> 483 us (0.990)
  Pallas kernels: 136 us -> 141 us
  waiting for transfers between devices: 221 us -> 216 us
    pallas_call x14, Pallas kernels: 136 us -> 141 us  [run_kernel(): pl.pallas_call(body, name=body_name(body), out_shape=list(outs), in_specs...]
    ppermute x59, waiting for transfers between devices: 198 us -> 193 us  [permuted(): lax.ppermute(values, ALL_AXES, [(d, target(d, n_dev)) for d in range(n_de...]
  transfers between devices with their start and end apart: 63 -> 63, of which waited for: 26 -> 26; matrix products, arithmetic and copies ran while one was open for 9% -> 9% of each run, Pallas kernels for 25% -> 26%
where the time goes in v2:
time: 483 us; the launch traced here: 476 us
  waiting for transfers between devices  216 us (45%)
  Pallas kernels  141 us (29%)
  starting transfers between devices  60.9 us (13%)
  other arithmetic  39.7 us (8%)
  local copies, waits for them, and re-layouts  14.6 us (3%)
    ppermute x59, waiting for transfers between devices, permuted(): lax.ppermute(values, ALL_AXES, [(d, target(d, n_dev)) for d in range(n_de...  193 us
    pallas_call x14, Pallas kernels, run_kernel(): pl.pallas_call(body, name=body_name(body), out_shape=list(outs), in_specs...  141 us
    ppermute x59, starting transfers between devices, permuted(): lax.ppermute(values, ALL_AXES, [(d, target(d, n_dev)) for d in range(n_de...  43 us
    all_to_all x4, waiting for transfers between devices, to_expert(): lax.all_to_all(picked.reshape(n_expert, per_dest, features), 'expert', sp...  23.3 us
    all_to_all x4, starting transfers between devices, to_expert(): lax.all_to_all(picked.reshape(n_expert, per_dest, features), 'expert', sp...  18 us
    concatenate x13, other arithmetic, on_device(): join = lambda *v: jnp.concatenate(v, axis=0)  13.2 us
  transfers between devices with their start and end apart: 63, of which 26 were waited for; matrix products, arithmetic and copies ran while one was open for 9% of the time, Pallas kernels for 26%

profile of v2, /device:TPU:0, one launch (start us, length us, event | category | flops | bytes accessed | tf_op | source)
XLA Modules:
  0.0 476.1 jit_solution(384715677530683715)
XLA Ops:
  5.7 2.7 collective-permute-start.1
  8.5 7.2 %collective-permute-done.1 = bf16[64,2176]{1,0:T(8,128)(2,1)S(1)} collective-permute-done((bf16[64,2176]{1,0:T(8,128)(2,1)S(1)}, bf16[64,2176]{1,0:T(8,128)(2,1)S(1)}, u32[]{:S(2)}, u32[]{:S(2)}) %collective-permute-start.1) | collective-permute-done | bytes 278560 | tf_op jit(solution)/shard_map/ppermute | solution.py:21
  19.5 2.7 collective-permute-start.3
  22.8 18.7 %collective-permute-done.7 = bf16[256,512]{1,0:T(8,128)(2,1)S(1)} collective-permute-done((bf16[256,512]{1,0:T(8,128)(2,1)S(1)}, bf16[256,512]{1,0:T(8,128)(2,1)S(1)}, u32[]{:S(2)}, u32[]{:S(2)}) %collective-permute-start.7) | collective-permute-done | bytes 262176 | tf_op jit(solution)/shard_map/ppermute | solution.py:21
  42.4 3.4 collective-permute-done.3.refs_3_
  48.4 23.9 %collective-permute-done.8.refs_2_ = bf16[256,2176]{1,0:T(8,128)(2,1)S(1)} collective-permute-done((bf16[256,2176]{1,0:T(8,128)(2,1)S(1)}, bf16[256,2176]{1,0:T(8,128)(2,1)S(1)}, u32[]{:S(2)}, u32[]{:S(2)}) %collective-permute-start.8) | collective-permute-done | bytes 1114144 | tf_op jit(solution)/shard_map/ppermute | solution.py:21
  76.4 18.6 %collective-permute-done.12.refs_5_ = bf16[256,2176]{1,0:T(8,128)(2,1)S(1)} collective-permute-done((bf16[256,2176]{1,0:T(8,128)(2,1)S(1)}, bf16[256,2176]{1,0:T(8,128)(2,1)S(1)}, u32[]{:S(2)}, u32[]{:S(2)}) %collective-permute-start.12) | collective-permute-done | bytes 1114144 | tf_op jit(solution)/shard_map/ppermute | solution.py:21
  96.7 5.6 %collective-permute-done.14.refs_3_ = bf16[512,512]{1,0:T(8,128)(2,1)} collective-permute-done((bf16[512,512]{1,0:T(8,128)(2,1)}, bf16[512,512]{1,0:T(8,128)(2,1)}, u32[]{:S(2)}, u32[]{:S(2)}) %collective-permute-start.14) | collective-permute-done | bytes 524320 | tf_op jit(solution)/shard_map/ppermute | solution.py:21
  102.3 3.9 collective-permute-done.15.refs_2_
  113.2 20.4 %collective-permute-done.21.refs_4_ = bf16[512,512]{1,0:T(8,128)(2,1)} collective-permute-done((bf16[512,512]{1,0:T(8,128)(2,1)}, bf16[512,512]{1,0:T(8,128)(2,1)}, u32[]{:S(2)}, u32[]{:S(2)}) %collective-permute-start.21) | collective-permute-done | bytes 524320 | tf_op jit(solution)/shard_map/ppermute | solution.py:21
  133.6 2.2 pad_maximum_fusion.11
  138.0 2.8 pad_maximum_fusion.3
  142.9 16.0 %attend_kernel.1 = (f32[256,1024]{1,0:T(8,128)}, bf16[256,1024]{1,0:T(8,128)(2,1)}, bf16[256,1024]{1,0:T(8,128)(2,1)}, bf16[256,3072]{1,0:T(8,128)(2,1)}, bf16[256,1024]{1,0:T(8,128)(2,1)}, /*index=5*/f32[8,1024]{1,0:T(8,128)}) custom-call(s32[4]{0:T(128)} %pad_add_fusion.pos, bf16[256,1024]{1,0:T(8,128)(2,1)} %tokens.3, bf16[128,2176]{1,0:T(8,128)(2,1)} %copy-done.21, ...), custom_call_target="tpu_custom_call" | custom-call | flops 80530636800 | bytes 409928160 | tf_op jit(solution)/shard_map/attend_kernel/pallas_call | solution.py:67
  158.9 5.2 %all-to-all-start = ((bf16[8,32,1024]{2,1,0:T(8,128)(2,1)}), bf16[8,32,1024]{2,1,0:T(8,128)(2,1)S(1)}, u32[]{:S(2)}, u32[]{:S(2)}) async-start(bf16[8,32,1024]{2,1,0:T(8,128)(2,1)} %bitcast.7), calls=%async_computation | async-start | bytes 1048576 | tf_op jit(solution)/shard_map/all_to_all | solution.py:716
  164.1 3.0 collective-permute-done.23.refs_2_
  169.2 10.7 %up_kernel.1 = (bf16[256,4096]{1,0:T(8,128)(2,1)}, f32[256,4096]{1,0:T(8,128)}) custom-call(s32[4]{0:T(128)} %pad_add_fusion.pos, bf16[256,1024]{1,0:T(8,128)(2,1)} %get-tuple-element.114.ffn_in.refs_8_, bf16[128,2048]{1,0:T(8,128)(2,1)} %copy-done.32, bf16[128,2048]{1,0:T(8,128)(2,1)} %copy-done.9, bf16[256,2048]{1,0:T(8,128)(2,1)} %copy-done.19, ...), custom_call_target="tpu_custom_call" | custom-call | flops 64424509440 | bytes 456131040 | tf_op jit(solution)/shard_map/up_kernel/pallas_call | solution.py:67
  181.6 7.2 %down_kernel.1 = (f32[256,1024]{1,0:T(8,128)}, bf16[256,1024]{1,0:T(8,128)(2,1)}) custom-call(s32[4]{0:T(128)} %pad_add_fusion.pos, bf16[256,4096]{1,0:T(8,128)(2,1)} %get-tuple-element.120.act.left, f32[256,1024]{1,0:T(8,128)} %get-tuple-element.121.hidden, bf16[256,256]{1,0:T(8,128)(2,1)} %fusion.6.pick, ...), custom_call_target="tpu_custom_call" | custom-call | flops 64424509440 | bytes 397148640 | tf_op jit(solution)/shard_map/down_kernel/pallas_call | solution.py:67
  188.8 5.4 %all-to-all-start.1 = ((bf16[8,32,1024]{2,1,0:T(8,128)(2,1)}), bf16[8,32,1024]{2,1,0:T(8,128)(2,1)S(1)}, u32[]{:S(2)}, u32[]{:S(2)}) async-start(bf16[8,32,1024]{2,1,0:T(8,128)(2,1)} %bitcast.27), calls=%async_computation.1 | async-start | bytes 1048576 | tf_op jit(solution)/shard_map/all_to_all | solution.py:716
  194.3 14.6 %all-to-all-done.1 = bf16[8,32,1024]{2,1,0:T(8,128)(2,1)S(1)} async-done(((bf16[8,32,1024]{2,1,0:T(8,128)(2,1)}), bf16[8,32,1024]{2,1,0:T(8,128)(2,1)S(1)}, u32[]{:S(2)}, u32[]{:S(2)}) %all-to-all-start.1) | async-done | bytes 524320 | tf_op jit(solution)/shard_map/all_to_all | solution.py:716
  209.7 16.5 %expert_kernel.1 = (bf16[256,1024]{1,0:T(8,128)(2,1)}, bf16[256,1024]{1,0:T(8,128)(2,1)}, bf16[256,1024]{1,0:T(8,128)(2,1)}, bf16[256,3072]{1,0:T(8,128)(2,1)}, ...) custom-call(s32[4]{0:T(128)} %pad_add_fusion.pos, ...), custom_call_target="tpu_custom_call" | custom-call | flops 257698037760 | bytes 740352512 | tf_op jit(solution)/shard_map/expert_kernel/pallas_call | solution.py:67
  226.2 3.9 all-to-all-start.2
  230.1 5.4 %copies_send_kernel.1 = bf16[528,4096]{1,0:T(8,128)(2,1)} custom-call(s32[4]{0:T(128)} %pad_add_fusion.pos, bf16[256,1024]{1,0:T(8,128)(2,1)} %get-tuple-element.131.left, bf16[256,4096]{1,0:T(8,128)(2,1)} %get-tuple-element.132.right, f32[8,1024]{1,0:T(8,128)} %get-tuple-element.133.vectors), custom_call_target="tpu_custom_call" | custom-call | flops 32212254720 | bytes 209388000 | tf_op jit(solution)/shard_map/copies_send_kernel/pallas_call | solution.py:67
  236.1 8.6 %all-to-all-done.2 = bf16[8,32,1024]{2,1,0:T(8,128)(2,1)S(1)} async-done(((bf16[8,32,1024]{2,1,0:T(8,128)(2,1)}), bf16[8,32,1024]{2,1,0:T(8,128)(2,1)S(1)}, u32[]{:S(2)}, u32[]{:S(2)}) %all-to-all-start.2) | async-done | bytes 524320 | tf_op jit(solution)/shard_map/all_to_all | solution.py:716
  245.5 6.3 %dense_grad_kernel.1 = (f32[256,1024]{1,0:T(8,128)}, bf16[256,1024]{1,0:T(8,128)(2,1)}, bf16[4096,512]{1,0:T(8,128)(2,1)}) custom-call(s32[4]{0:T(128)} %pad_add_fusion.pos, bf16[256,1024]{1,0:T(8,128)(2,1)} %bitcast.29, bf16[256,1024]{1,0:T(8,128)(2,1)} %cotangent.1, bf16[256,256]{1,0:T(8,128)(2,1)} %fusion.6.pick, ...), custom_call_target="tpu_custom_call" | custom-call | flops 64424509440 | bytes 271319520 | tf_op jit(solution)/shard_map/dense_grad_kernel/pallas_call | solution.py:67
  252.2 8.5 %pre_back_kernel.1.grad_pre = bf16[256,4096]{1,0:T(8,128)(2,1)} custom-call(s32[4]{0:T(128)} %pad_add_fusion.pos, bf16[256,1024]{1,0:T(8,128)(2,1)} %get-tuple-element.139.grad_low.right, f32[256,4096]{1,0:T(8,128)} %get-tuple-element.140.slope, bf16[512,512]{1,0:T(8,128)(2,1)} %constant_dynamic-update-slice_fusion.2.refs_0_, ...), custom_call_target="tpu_custom_call" | custom-call | flops 64424509440 | bytes 456131040 | tf_op jit(solution)/shard_map/pre_back_kernel/pallas_call | solution.py:67
  262.5 4.1 collective-permute-done.30.high
  266.7 7.1 %sum_keep_kernel.1 = (bf16[1024,512]{1,0:T(8,128)(2,1)}, bf16[1024,512]{1,0:T(8,128)(2,1)}, bf16[2048,512]{1,0:T(8,128)(2,1)}) custom-call(s32[4]{0:T(128)} %pad_add_fusion.pos, bf16[256,4096]{1,0:T(8,128)(2,1)} %get-tuple-element.120.act.left, bf16[256,1024]{1,0:T(8,128)(2,1)} %get-tuple-element.139.grad_low.right, ...), custom_call_target="tpu_custom_call" | custom-call | flops 64424509440 | bytes 330301920 | tf_op jit(solution)/shard_map/sum_keep_kernel/pallas_call | solution.py:67
  273.8 6.4 %copies_keep_kernel.1 = (bf16[64,4096]{1,0:T(8,128)(2,1)}, bf16[208,4096]{1,0:T(8,128)(2,1)}, bf16[256,4096]{1,0:T(8,128)(2,1)}, f32[8,1024]{1,0:T(8,128)}) custom-call(s32[4]{0:T(128)} %pad_add_fusion.pos, bf16[256,1024]{1,0:T(8,128)(2,1)} %get-tuple-element.131.left, bf16[256,4096]{1,0:T(8,128)(2,1)} %get-tuple-element.132.right, ...), custom_call_target="tpu_custom_call" | custom-call | flops 32212254720 | bytes 340132320 | tf_op jit(solution)/shard_map/copies_keep_kernel/pallas_call | solution.py:67
  281.0 13.9 %hidden_back_kernel.1 = (f32[256,1024]{1,0:T(8,128)}, bf16[256,1024]{1,0:T(8,128)(2,1)}, f32[8,1024]{1,0:T(8,128)}, bf16[1024,2560]{1,0:T(8,128)(2,1)}) custom-call(s32[4]{0:T(128)} %pad_add_fusion.pos, bf16[256,4096]{1,0:T(8,128)(2,1)} %pre_back_kernel.1.grad_pre, f32[256,1024]{1,0:T(8,128)} %get-tuple-element.121.hidden, ...), custom_call_target="tpu_custom_call" | custom-call | flops 112742891520 | bytes 615383552 | tf_op jit(solution)/shard_map/hidden_back_kernel/pallas_call | solution.py:67
  302.1 17.8 %attend_back_kernel.1 = (bf16[256,3072]{1,0:T(8,128)(2,1)}, f32[256,1024]{1,0:T(8,128)}, f32[8,1024]{1,0:T(8,128)}) custom-call(s32[4]{0:T(128)} %pad_add_fusion.pos, bf16[256,1024]{1,0:T(8,128)(2,1)} %get-tuple-element.160.grad_low, bf16[256,3072]{1,0:T(8,128)(2,1)} %get-tuple-element.161.qkv, bf16[256,1024]{1,0:T(8,128)(2,1)} %tokens.3, ...), custom_call_target="tpu_custom_call" | custom-call | flops 128849018880 | bytes 458097120 | tf_op jit(solution)/shard_map/attend_back_kernel/pallas_call | solution.py:67
  320.7 4.7 collective-permute-done.36
  328.9 11.6 %wide_keep_kernel.1 = (bf16[256,2560]{1,0:T(8,128)(2,1)}, bf16[256,2560]{1,0:T(8,128)(2,1)}, bf16[512,2560]{1,0:T(8,128)(2,1)}, bf16[1040,1536]{1,0:T(8,128)(2,1)}) custom-call(s32[4]{0:T(128)} %pad_add_fusion.pos, bf16[256,1024]{1,0:T(8,128)(2,1)} %get-tuple-element.114.ffn_in.refs_8_, bf16[256,1024]{1,0:T(8,128)(2,1)} %get-tuple-element.156.refs_9_.heads, ...), custom_call_target="tpu_custom_call" | custom-call | flops 80530636800 | bytes 585400832 | tf_op jit(solution)/shard_map/wide_keep_kernel/pallas_call | solution.py:67
  341.9 7.5 %copies_whole_kernel.1 = f32[1024,1024]{1,0:T(8,128)} custom-call(s32[4]{0:T(128)} %pad_add_fusion.pos, bf16[256,3072]{1,0:T(8,128)(2,1)} %get-tuple-element.143.kept, bf16[256,1024]{1,0:T(8,128)(2,1)} %copy-done.26, bf16[256,1024]{1,0:T(8,128)(2,1)} %copy-done.28, bf16[256,1024]{1,0:T(8,128)(2,1)} %copy-done.30, ...), custom_call_target="tpu_custom_call" | custom-call | flops 64424509440 | bytes 314573280 | tf_op jit(solution)/shard_map/copies_whole_kernel/pallas_call | solution.py:67
  349.4 9.0 %collective-permute-done.40 = bf16[256,2560]{1,0:T(8,128)(2,1)S(1)} collective-permute-done((bf16[256,2560]{1,0:T(8,128)(2,1)}, bf16[256,2560]{1,0:T(8,128)(2,1)S(1)}, u32[]{:S(2)}, u32[]{:S(2)}) %collective-permute-start.40) | collective-permute-done | bytes 1310752 | tf_op jit(solution)/shard_map/ppermute | solution.py:21
  359.7 6.2 %last_keep_kernel.1 = (bf16[272,1536]{1,0:T(8,128)(2,1)}, bf16[256,1536]{1,0:T(8,128)(2,1)}, bf16[512,1536]{1,0:T(8,128)(2,1)}, f32[8,1536]{1,0:T(8,128)}) custom-call(s32[4]{0:T(128)} %pad_add_fusion.pos, bf16[256,1024]{1,0:T(8,128)(2,1)} %get-tuple-element.168.attn_in.left, bf16[256,3072]{1,0:T(8,128)(2,1)} %get-tuple-element.163.grad_qkv.right, ...), custom_call_target="tpu_custom_call" | custom-call | flops 32212254720 | bytes 258048480 | tf_op jit(solution)/shard_map/last_keep_kernel/pallas_call | solution.py:67
  369.2 21.4 %collective-permute-done.42 = bf16[512,512]{1,0:T(8,128)(2,1)S(1)} collective-permute-done((bf16[512,512]{1,0:T(8,128)(2,1)S(1)}, bf16[512,512]{1,0:T(8,128)(2,1)S(1)}, u32[]{:S(2)}, u32[]{:S(2)}) %collective-permute-start.42) | collective-permute-done | bytes 524320 | tf_op jit(solution)/shard_map/ppermute | solution.py:21
  391.8 3.5 all-to-all-start.3
  395.3 4.0 collective-permute-done.46
  402.9 2.2 convert_add_fusion
  409.0 2.1 collective-permute-start.53
  413.3 8.8 %collective-permute-done.52 = bf16[64,2560]{1,0:T(8,128)(2,1)S(1)} collective-permute-done((bf16[64,2560]{1,0:T(8,128)(2,1)}, bf16[64,2560]{1,0:T(8,128)(2,1)S(1)}, u32[]{:S(2)}, u32[]{:S(2)}) %collective-permute-start.52) | collective-permute-done | bytes 327712 | tf_op jit(solution)/shard_map/ppermute | solution.py:21
  422.3 2.7 collective-permute-done.54
  425.0 13.3 %collective-permute-done.53 = bf16[64,2560]{1,0:T(8,128)(2,1)} collective-permute-done((bf16[64,2560]{1,0:T(8,128)(2,1)}, bf16[64,2560]{1,0:T(8,128)(2,1)}, u32[]{:S(2)}, u32[]{:S(2)}) %collective-permute-start.53) | collective-permute-done | bytes 327712 | tf_op jit(solution)/shard_map/ppermute | solution.py:21
  445.4 2.6 collective-permute-start.50
  449.6 6.5 %collective-permute-done.48 = bf16[80,1536]{1,0:T(8,128)(2,1)S(1)} collective-permute-done((bf16[80,1536]{1,0:T(8,128)(2,1)S(1)}, bf16[80,1536]{1,0:T(8,128)(2,1)S(1)}, u32[]{:S(2)}, u32[]{:S(2)}) %collective-permute-start.48) | collective-permute-done | bytes 245792 | tf_op jit(solution)/shard_map/ppermute | solution.py:21
  456.2 7.8 %collective-permute-done.49 = bf16[80,1536]{1,0:T(8,128)(2,1)S(1)} collective-permute-done((bf16[80,1536]{1,0:T(8,128)(2,1)S(1)}, bf16[80,1536]{1,0:T(8,128)(2,1)S(1)}, u32[]{:S(2)}, u32[]{:S(2)}) %collective-permute-start.49) | collective-permute-done | bytes 245792 | tf_op jit(solution)/shard_map/ppermute | solution.py:21
  464.8 3.2 collective-permute-done.56
  471.9 3.8 add_bitcast_fusion
  (258 shorter events, 80.6 us)
Async XLA Ops:
  15.7 26.6 %collective-permute-start.2 = (bf16[128,2176]{1,0:T(8,128)(2,1)S(1)}, bf16[128,2176]{1,0:T(8,128)(2,1)S(1)}, u32[]{:S(2)}, u32[]{:S(2)}) collective-permute-start(bf16[128,2176]{1,0:T(8,128)(2,1)S(1)} %pad_maximum_fusion.12.refs_0_), channel_id=1, source_target_pairs={{0,4},{1,3},{2,6},{3,1},{4,0},{5,7},{6,2},{7,5},{8,12},{9,11},{10,... | collective-permute-start | bytes 1671176 | tf_op jit(solution)/shard_map/ppermute | solution.py:21
  17.4 24.8 %collective-permute-start.5 = (bf16[64,2048]{1,0:T(8,128)(2,1)S(1)}, bf16[64,2048]{1,0:T(8,128)(2,1)S(1)}, u32[]{:S(2)}, u32[]{:S(2)}) collective-permute-start(bf16[64,2048]{1,0:T(8,128)(2,1)S(1)} %maximum_select_fusion.4), channel_id=1, source_target_pairs={{0,8},{1,9},{2,10},{3,11},{4,12},{5,13},{6,14},{7,15},{8,0},{9,1},... | collective-permute-start | bytes 786440 | tf_op jit(solution)/shard_map/ppermute | solution.py:21
  19.0 22.6 %collective-permute-start.7 = (bf16[256,512]{1,0:T(8,128)(2,1)S(1)}, bf16[256,512]{1,0:T(8,128)(2,1)S(1)}, u32[]{:S(2)}, u32[]{:S(2)}) collective-permute-start(bf16[256,512]{1,0:T(8,128)(2,1)S(1)} %maximum_select_fusion.5), channel_id=1, source_target_pairs={{0,8},{1,9},{2,10},{3,11},{4,12},{5,13},{6,14},{7,15},{8,0},{9,1},... | collective-permute-start | bytes 786440 | tf_op jit(solution)/shard_map/ppermute | solution.py:21
  19.5 26.4 %collective-permute-start.3 = (bf16[128,2176]{1,0:T(8,128)(2,1)S(1)}, bf16[128,2176]{1,0:T(8,128)(2,1)S(1)}, u32[]{:S(2)}, u32[]{:S(2)}) collective-permute-start(bf16[128,2176]{1,0:T(8,128)(2,1)S(1)} %pad_maximum_fusion.12.refs_0_), channel_id=1, source_target_pairs={{0,16},{1,17},{2,18},{3,19},{4,20},{5,21},{6,22},{7,23},{8,24},{9,... | collective-permute-start | bytes 1671176 | tf_op jit(solution)/shard_map/ppermute | solution.py:21
  45.8 26.5 %collective-permute-start.8 = (bf16[256,2176]{1,0:T(8,128)(2,1)S(1)}, bf16[256,2176]{1,0:T(8,128)(2,1)S(1)}, u32[]{:S(2)}, u32[]{:S(2)}) collective-permute-start(bf16[256,2176]{1,0:T(8,128)(2,1)S(1)} %pad_maximum_fusion.6), channel_id=1, source_target_pairs={{0,2},{1,5},{2,0},{3,7},{4,6},{5,1},{6,4},{7,3},{8,10},{9,13},{10,... | collective-permute-start | bytes 3342344 | tf_op jit(solution)/shard_map/ppermute | solution.py:21
  46.4 27.2 %collective-permute-start.9 = (bf16[128,2176]{1,0:T(8,128)(2,1)S(1)}, bf16[128,2176]{1,0:T(8,128)(2,1)S(1)}, u32[]{:S(2)}, u32[]{:S(2)}) collective-permute-start(bf16[128,2176]{1,0:T(8,128)(2,1)S(1)} %collective-permute-done.3.refs_3_), channel_id=1, source_target_pairs={{0,4},{1,3},{2,6},{3,1},{4,0},{5,7},{6,2},{7,5},{8,12},{9,11},{10,... | collective-permute-start | bytes 1671176 | tf_op jit(solution)/shard_map/ppermute | solution.py:21
  47.8 25.5 %collective-permute-start.11 = (bf16[128,2048]{1,0:T(8,128)(2,1)S(1)}, bf16[128,2048]{1,0:T(8,128)(2,1)S(1)}, u32[]{:S(2)}, u32[]{:S(2)}) collective-permute-start(bf16[128,2048]{1,0:T(8,128)(2,1)S(1)} %constant_dynamic-update-slice_fusion.refs_0_), channel_id=1, source_target_pairs={{0,4},{1,3},{2,6},{3,1},{4,0},{5,7},{6,2},{7,5},{8,12},{9,11},{10,... | collective-permute-start | bytes 1572872 | tf_op jit(solution)/shard_map/ppermute | solution.py:21
  48.4 25.2 %collective-permute-start.10 = (bf16[128,2048]{1,0:T(8,128)(2,1)S(1)}, bf16[128,2048]{1,0:T(8,128)(2,1)S(1)}, u32[]{:S(2)}, u32[]{:S(2)}) collective-permute-start(bf16[128,2048]{1,0:T(8,128)(2,1)S(1)} %constant_dynamic-update-slice_fusion.refs_0_), channel_id=1, source_target_pairs={{0,16},{1,17},{2,18},{3,19},{4,20},{5,21},{6,22},{7,23},{8,24},{9,... | collective-permute-start | bytes 1572872 | tf_op jit(solution)/shard_map/ppermute | solution.py:21
  73.6 32.6 %collective-permute-start.13 = (bf16[512,2176]{1,0:T(8,128)(2,1)S(1)}, bf16[512,2176]{1,0:T(8,128)(2,1)S(1)}, u32[]{:S(2)}, u32[]{:S(2)}) collective-permute-start(bf16[512,2176]{1,0:T(8,128)(2,1)S(1)} %pad_maximum_fusion), channel_id=1, source_target_pairs={{0,1},{1,0},{2,3},{3,2},{4,5},{5,4},{6,7},{7,6},{8,9},{9,8},{10,11... | collective-permute-start | bytes 6684680 | tf_op jit(solution)/shard_map/ppermute | solution.py:21
  73.8 21.2 %collective-permute-start.12 = (bf16[256,2176]{1,0:T(8,128)(2,1)S(1)}, bf16[256,2176]{1,0:T(8,128)(2,1)S(1)}, u32[]{:S(2)}, u32[]{:S(2)}) collective-permute-start(bf16[256,2176]{1,0:T(8,128)(2,1)S(1)} %pad_maximum_fusion.7), channel_id=1, source_target_pairs={{0,2},{1,5},{2,0},{3,7},{4,6},{5,1},{6,4},{7,3},{8,10},{9,13},{10,... | collective-permute-start | bytes 3342344 | tf_op jit(solution)/shard_map/ppermute | solution.py:21
  74.3 31.9 %collective-permute-start.15 = (bf16[256,2048]{1,0:T(8,128)(2,1)S(1)}, bf16[256,2048]{1,0:T(8,128)(2,1)S(1)}, u32[]{:S(2)}, u32[]{:S(2)}) collective-permute-start(bf16[256,2048]{1,0:T(8,128)(2,1)S(1)} %pad_maximum_fusion.8), channel_id=1, source_target_pairs={{0,2},{1,5},{2,0},{3,7},{4,6},{5,1},{6,4},{7,3},{8,10},{9,13},{10,... | collective-permute-start | bytes 3145736 | tf_op jit(solution)/shard_map/ppermute | solution.py:21
  76.1 26.2 %collective-permute-start.14 = (bf16[512,512]{1,0:T(8,128)(2,1)}, bf16[512,512]{1,0:T(8,128)(2,1)}, u32[]{:S(2)}, u32[]{:S(2)}) collective-permute-start(bf16[512,512]{1,0:T(8,128)(2,1)} %constant_dynamic-update-slice_fusion.2.refs_0_), channel_id=1, source_target_pairs={{0,16},{1,17},{2,18},{3,19},{4,20},{5,21},{6,22},{7,23},{8,24},{9,... | collective-permute-start | bytes 1572872 | tf_op jit(solution)/shard_map/ppermute | solution.py:21
  76.1 26.2 %collective-permute-start.16 = (bf16[128,2048]{1,0:T(8,128)(2,1)S(1)}, bf16[128,2048]{1,0:T(8,128)(2,1)S(1)}, u32[]{:S(2)}, u32[]{:S(2)}) collective-permute-start(bf16[128,2048]{1,0:T(8,128)(2,1)S(1)} %collective-permute-done.10.refs_3_), channel_id=1, source_target_pairs={{0,4},{1,3},{2,6},{3,1},{4,0},{5,7},{6,2},{7,5},{8,12},{9,11},{10,... | collective-permute-start | bytes 1572872 | tf_op jit(solution)/shard_map/ppermute | solution.py:21
  106.2 34.5 %collective-permute-start.17 = (bf16[512,2176]{1,0:T(8,128)(2,1)}, bf16[512,2176]{1,0:T(8,128)(2,1)}, u32[]{:S(2)}, u32[]{:S(2)}) collective-permute-start(bf16[512,2176]{1,0:T(8,128)(2,1)} %pad_maximum_fusion.1), channel_id=1, source_target_pairs={{0,1},{1,0},{2,3},{3,2},{4,5},{5,4},{6,7},{7,6},{8,9},{9,8},{10,11... | collective-permute-start | bytes 6684680 | tf_op jit(solution)/shard_map/ppermute | solution.py:21
  106.6 34.2 %collective-permute-start.19 = (bf16[512,2048]{1,0:T(8,128)(2,1)S(1)}, bf16[512,2048]{1,0:T(8,128)(2,1)}, u32[]{:S(2)}, u32[]{:S(2)}) collective-permute-start(bf16[512,2048]{1,0:T(8,128)(2,1)S(1)} %pad_maximum_fusion.2), channel_id=1, source_target_pairs={{0,1},{1,0},{2,3},{3,2},{4,5},{5,4},{6,7},{7,6},{8,9},{9,8},{10,11... | collective-permute-start | bytes 6291464 | tf_op jit(solution)/shard_map/ppermute | solution.py:21
  108.3 29.7 %collective-permute-start.18 = (bf16[256,2048]{1,0:T(8,128)(2,1)}, bf16[256,2048]{1,0:T(8,128)(2,1)}, u32[]{:S(2)}, u32[]{:S(2)}) collective-permute-start(bf16[256,2048]{1,0:T(8,128)(2,1)} %pad_maximum_fusion.9), channel_id=1, source_target_pairs={{0,2},{1,5},{2,0},{3,7},{4,6},{5,1},{6,4},{7,3},{8,10},{9,13},{10,... | collective-permute-start | bytes 3145736 | tf_op jit(solution)/shard_map/ppermute | solution.py:21
  108.6 27.2 %collective-permute-start.20 = (bf16[512,512]{1,0:T(8,128)(2,1)}, bf16[512,512]{1,0:T(8,128)(2,1)}, u32[]{:S(2)}, u32[]{:S(2)}) collective-permute-start(bf16[512,512]{1,0:T(8,128)(2,1)} %constant_dynamic-update-slice_fusion.2.refs_0_), channel_id=1, source_target_pairs={{0,4},{1,3},{2,6},{3,1},{4,0},{5,7},{6,2},{7,5},{8,12},{9,11},{10,... | collective-permute-start | bytes 1572872 | tf_op jit(solution)/shard_map/ppermute | solution.py:21
  109.0 24.7 %collective-permute-start.21 = (bf16[512,512]{1,0:T(8,128)(2,1)}, bf16[512,512]{1,0:T(8,128)(2,1)}, u32[]{:S(2)}, u32[]{:S(2)}) collective-permute-start(bf16[512,512]{1,0:T(8,128)(2,1)} %collective-permute-done.14.refs_3_), channel_id=1, source_target_pairs={{0,4},{1,3},{2,6},{3,1},{4,0},{5,7},{6,2},{7,5},{8,12},{9,11},{10,... | collective-permute-start | bytes 1572872 | tf_op jit(solution)/shard_map/ppermute | solution.py:21
  140.8 39.1 %collective-permute-start.26 = (bf16[1024,512]{1,0:T(8,128)(2,1)}, bf16[1024,512]{1,0:T(8,128)(2,1)}, u32[]{:S(2)}, u32[]{:S(2)}) collective-permute-start(bf16[1024,512]{1,0:T(8,128)(2,1)} %pad_maximum_fusion.11), channel_id=1, source_target_pairs={{0,1},{1,0},{2,3},{3,2},{4,5},{5,4},{6,7},{7,6},{8,9},{9,8},{10,11... | collective-permute-start | bytes 3145736 | tf_op jit(solution)/shard_map/ppermute | solution.py:21
  140.8 27.9 %collective-permute-start.24 = (bf16[1024,512]{1,0:T(8,128)(2,1)}, bf16[1024,512]{1,0:T(8,128)(2,1)}, u32[]{:S(2)}, u32[]{:S(2)}) collective-permute-start(bf16[1024,512]{1,0:T(8,128)(2,1)} %pad_maximum_fusion.11), channel_id=1, source_target_pairs={{0,2},{1,5},{2,0},{3,7},{4,6},{5,1},{6,4},{7,3},{8,10},{9,13},{10,... | collective-permute-start | bytes 3145736 | tf_op jit(solution)/shard_map/ppermute | solution.py:21
  141.2 25.9 %collective-permute-start.23 = (bf16[1024,512]{1,0:T(8,128)(2,1)}, bf16[1024,512]{1,0:T(8,128)(2,1)S(1)}, u32[]{:S(2)}, u32[]{:S(2)}) collective-permute-start(bf16[1024,512]{1,0:T(8,128)(2,1)} %pad_maximum_fusion.10), channel_id=1, source_target_pairs={{0,2},{1,5},{2,0},{3,7},{4,6},{5,1},{6,4},{7,3},{8,10},{9,13},{10,... | collective-permute-start | bytes 3145736 | tf_op jit(solution)/shard_map/ppermute | solution.py:21
  142.9 25.8 %collective-permute-start.22 = (bf16[512,2048]{1,0:T(8,128)(2,1)}, bf16[512,2048]{1,0:T(8,128)(2,1)}, u32[]{:S(2)}, u32[]{:S(2)}) collective-permute-start(bf16[512,2048]{1,0:T(8,128)(2,1)} %pad_maximum_fusion.3), channel_id=1, source_target_pairs={{0,1},{1,0},{2,3},{3,2},{4,5},{5,4},{6,7},{7,6},{8,9},{9,8},{10,11... | collective-permute-start | bytes 6291464 | tf_op jit(solution)/shard_map/ppermute | solution.py:21
  158.9 29.9 %all-to-all-start = ((bf16[8,32,1024]{2,1,0:T(8,128)(2,1)}), bf16[8,32,1024]{2,1,0:T(8,128)(2,1)S(1)}, u32[]{:S(2)}, u32[]{:S(2)}) async-start(bf16[8,32,1024]{2,1,0:T(8,128)(2,1)} %bitcast.7), calls=%async_computation | async-start | bytes 1048576 | tf_op jit(solution)/shard_map/all_to_all | solution.py:716
  188.8 20.1 %all-to-all-start.1 = ((bf16[8,32,1024]{2,1,0:T(8,128)(2,1)}), bf16[8,32,1024]{2,1,0:T(8,128)(2,1)S(1)}, u32[]{:S(2)}, u32[]{:S(2)}) async-start(bf16[8,32,1024]{2,1,0:T(8,128)(2,1)} %bitcast.27), calls=%async_computation.1 | async-start | bytes 1048576 | tf_op jit(solution)/shard_map/all_to_all | solution.py:716
  226.2 18.5 %all-to-all-start.2 = ((bf16[8,32,1024]{2,1,0:T(8,128)(2,1)}), bf16[8,32,1024]{2,1,0:T(8,128)(2,1)S(1)}, u32[]{:S(2)}, u32[]{:S(2)}) async-start(bf16[8,32,1024]{2,1,0:T(8,128)(2,1)} %bitcast.28), calls=%async_computation.2 | async-start | bytes 1048576 | tf_op jit(solution)/shard_map/all_to_all | solution.py:716
  235.8 30.9 %collective-permute-start.31 = (bf16[256,3072]{1,0:T(8,128)(2,1)S(1)}, bf16[256,3072]{1,0:T(8,128)(2,1)}, u32[]{:S(2)}, u32[]{:S(2)}) collective-permute-start(bf16[256,3072]{1,0:T(8,128)(2,1)S(1)} %copy-done.38), channel_id=1, source_target_pairs={{0,1},{1,0},{2,3},{3,2},{4,5},{5,4},{6,7},{7,6},{8,9},{9,8},{10,11... | collective-permute-start | bytes 4718600 | tf_op jit(solution)/shard_map/ppermute | solution.py:21
  260.7 19.4 %collective-permute-start.35 = (bf16[256,1024]{1,0:T(8,128)(2,1)S(1)}, bf16[256,1024]{1,0:T(8,128)(2,1)S(1)}, u32[]{:S(2)}, u32[]{:S(2)}) collective-permute-start(bf16[256,1024]{1,0:T(8,128)(2,1)S(1)} %copy-done.40), channel_id=1, source_target_pairs={{0,2},{1,3},{2,0},{3,1},{4,6},{5,7},{6,4},{7,5},{8,10},{9,11},{10,... | collective-permute-start | bytes 1572872 | tf_op jit(solution)/shard_map/ppermute | solution.py:21
  280.2 17.9 %collective-permute-start.33 = (bf16[1024,512]{1,0:T(8,128)(2,1)}, bf16[1024,512]{1,0:T(8,128)(2,1)S(1)}, u32[]{:S(2)}, u32[]{:S(2)}) collective-permute-start(bf16[1024,512]{1,0:T(8,128)(2,1)} %get-tuple-element.147), channel_id=1, source_target_pairs={{0,2},{1,5},{2,0},{3,7},{4,6},{5,1},{6,4},{7,3},{8,10},{9,13},{10,... | collective-permute-start | bytes 3145736 | tf_op jit(solution)/shard_map/ppermute | solution.py:21
  294.9 33.9 %collective-permute-start.38 = (bf16[1024,2560]{1,0:T(8,128)(2,1)}, bf16[1024,2560]{1,0:T(8,128)(2,1)}, u32[]{:S(2)}, u32[]{:S(2)}) collective-permute-start(bf16[1024,2560]{1,0:T(8,128)(2,1)} %get-tuple-element.157), channel_id=1, source_target_pairs={{0,1},{1,0},{2,3},{3,2},{4,5},{5,4},{6,7},{7,6},{8,9},{9,8},{10,11... | collective-permute-start | bytes 15728648 | tf_op jit(solution)/shard_map/ppermute | solution.py:21
  297.7 31.2 %collective-permute-start.37 = (bf16[768,1024]{1,0:T(8,128)(2,1)S(1)}, bf16[768,1024]{1,0:T(8,128)(2,1)}, u32[]{:S(2)}, u32[]{:S(2)}) collective-permute-start(bf16[768,1024]{1,0:T(8,128)(2,1)S(1)} %pad_maximum_fusion.5), channel_id=1, source_target_pairs={{0,1},{1,0},{2,3},{3,2},{4,5},{5,4},{6,7},{7,6},{8,9},{9,8},{10,11... | collective-permute-start | bytes 4718600 | tf_op jit(solution)/shard_map/ppermute | solution.py:21
  299.3 26.0 %collective-permute-start.36 = (bf16[1024,512]{1,0:T(8,128)(2,1)}, bf16[1024,512]{1,0:T(8,128)(2,1)S(1)}, u32[]{:S(2)}, u32[]{:S(2)}) collective-permute-start(bf16[1024,512]{1,0:T(8,128)(2,1)} %add_convert_fusion.1), channel_id=1, source_target_pairs={{0,4},{1,3},{2,6},{3,1},{4,0},{5,7},{6,2},{7,5},{8,12},{9,11},{10,... | collective-permute-start | bytes 3145736 | tf_op jit(solution)/shard_map/ppermute | solution.py:21
  300.8 26.3 %collective-permute-start.34 = (bf16[1024,512]{1,0:T(8,128)(2,1)}, bf16[1024,512]{1,0:T(8,128)(2,1)S(1)}, u32[]{:S(2)}, u32[]{:S(2)}) collective-permute-start(bf16[1024,512]{1,0:T(8,128)(2,1)} %get-tuple-element.148), channel_id=1, source_target_pairs={{0,2},{1,5},{2,0},{3,7},{4,6},{5,1},{6,4},{7,3},{8,10},{9,13},{10,... | collective-permute-start | bytes 3145736 | tf_op jit(solution)/shard_map/ppermute | solution.py:21
  319.9 20.6 %collective-permute-start.39 = (bf16[64,4096]{1,0:T(8,128)(2,1)}, bf16[64,4096]{1,0:T(8,128)(2,1)}, u32[]{:S(2)}, u32[]{:S(2)}) collective-permute-start(bf16[64,4096]{1,0:T(8,128)(2,1)} %get-tuple-element.173), channel_id=1, source_target_pairs={{0,2},{1,3},{2,0},{3,1},{4,6},{5,7},{6,4},{7,5},{8,10},{9,11},{10,... | collective-permute-start | bytes 1572872 | tf_op jit(solution)/shard_map/ppermute | solution.py:21
  340.4 19.3 %collective-permute-start.41 = (bf16[1040,1536]{1,0:T(8,128)(2,1)}, bf16[1040,1536]{1,0:T(8,128)(2,1)}, u32[]{:S(2)}, u32[]{:S(2)}) collective-permute-start(bf16[1040,1536]{1,0:T(8,128)(2,1)} %get-tuple-element.171), channel_id=1, source_target_pairs={{0,1},{1,0},{2,3},{3,2},{4,5},{5,4},{6,7},{7,6},{8,9},{9,8},{10,11... | collective-permute-start | bytes 9584648 | tf_op jit(solution)/shard_map/ppermute | solution.py:21
  340.5 17.9 %collective-permute-start.40 = (bf16[256,2560]{1,0:T(8,128)(2,1)}, bf16[256,2560]{1,0:T(8,128)(2,1)S(1)}, u32[]{:S(2)}, u32[]{:S(2)}) collective-permute-start(bf16[256,2560]{1,0:T(8,128)(2,1)} %get-tuple-element.175), channel_id=1, source_target_pairs={{0,2},{1,5},{2,0},{3,7},{4,6},{5,1},{6,4},{7,3},{8,10},{9,13},{10,... | collective-permute-start | bytes 3932168 | tf_op jit(solution)/shard_map/ppermute | solution.py:21
  358.4 44.5 %collective-permute-start.43 = (bf16[256,2560]{1,0:T(8,128)(2,1)}, bf16[256,2560]{1,0:T(8,128)(2,1)}, u32[]{:S(2)}, u32[]{:S(2)}) collective-permute-start(bf16[256,2560]{1,0:T(8,128)(2,1)} %get-tuple-element.184), channel_id=1, source_target_pairs={{0,2},{1,5},{2,0},{3,7},{4,6},{5,1},{6,4},{7,3},{8,10},{9,13},{10,... | collective-permute-start | bytes 3932168 | tf_op jit(solution)/shard_map/ppermute | solution.py:21
  366.0 24.6 %collective-permute-start.42 = (bf16[512,512]{1,0:T(8,128)(2,1)S(1)}, bf16[512,512]{1,0:T(8,128)(2,1)S(1)}, u32[]{:S(2)}, u32[]{:S(2)}) collective-permute-start(bf16[512,512]{1,0:T(8,128)(2,1)S(1)} %slice.218), channel_id=1, source_target_pairs={{0,16},{1,17},{2,18},{3,19},{4,20},{5,21},{6,22},{7,23},{8,24},{9,... | collective-permute-start | bytes 1572872 | tf_op jit(solution)/shard_map/ppermute | solution.py:21
  366.1 33.2 %collective-permute-start.46 = (bf16[272,1536]{1,0:T(8,128)(2,1)}, bf16[272,1536]{1,0:T(8,128)(2,1)}, u32[]{:S(2)}, u32[]{:S(2)}) collective-permute-start(bf16[272,1536]{1,0:T(8,128)(2,1)} %get-tuple-element.187), channel_id=1, source_target_pairs={{0,2},{1,5},{2,0},{3,7},{4,6},{5,1},{6,4},{7,3},{8,10},{9,13},{10,... | collective-permute-start | bytes 2506760 | tf_op jit(solution)/shard_map/ppermute | solution.py:21
  368.6 34.4 %collective-permute-start.44 = (bf16[256,2560]{1,0:T(8,128)(2,1)}, bf16[256,2560]{1,0:T(8,128)(2,1)}, u32[]{:S(2)}, u32[]{:S(2)}) collective-permute-start(bf16[256,2560]{1,0:T(8,128)(2,1)} %add_convert_fusion), channel_id=1, source_target_pairs={{0,4},{1,3},{2,6},{3,1},{4,0},{5,7},{6,2},{7,5},{8,12},{9,11},{10,... | collective-permute-start | bytes 3932168 | tf_op jit(solution)/shard_map/ppermute | solution.py:21
  391.8 19.3 %all-to-all-start.3 = ((bf16[8,32,1024]{2,1,0:T(8,128)(2,1)}), bf16[8,32,1024]{2,1,0:T(8,128)(2,1)S(1)}, u32[]{:S(2)}, u32[]{:S(2)}) async-start(bf16[8,32,1024]{2,1,0:T(8,128)(2,1)} %bitcast.13), calls=%async_computation.3 | async-start | bytes 1048576 | tf_op jit(solution)/shard_map/all_to_all | solution.py:716
  402.4 37.3 %collective-permute-start.47 = (bf16[272,1536]{1,0:T(8,128)(2,1)}, bf16[272,1536]{1,0:T(8,128)(2,1)}, u32[]{:S(2)}, u32[]{:S(2)}) collective-permute-start(bf16[272,1536]{1,0:T(8,128)(2,1)} %fusion.1), channel_id=1, source_target_pairs={{0,4},{1,3},{2,6},{3,1},{4,0},{5,7},{6,2},{7,5},{8,12},{9,11},{10,... | collective-permute-start | bytes 2506760 | tf_op jit(solution)/shard_map/ppermute | solution.py:21
  405.1 36.9 %collective-permute-start.45 = (bf16[256,1536]{1,0:T(8,128)(2,1)}, bf16[256,1536]{1,0:T(8,128)(2,1)}, u32[]{:S(2)}, u32[]{:S(2)}) collective-permute-start(bf16[256,1536]{1,0:T(8,128)(2,1)} %get-tuple-element.186), channel_id=1, source_target_pairs={{0,2},{1,5},{2,0},{3,7},{4,6},{5,1},{6,4},{7,3},{8,10},{9,13},{10,... | collective-permute-start | bytes 2359304 | tf_op jit(solution)/shard_map/ppermute | solution.py:21
  408.1 17.0 %collective-permute-start.54 = (bf16[64,2560]{1,0:T(8,128)(2,1)}, bf16[64,2560]{1,0:T(8,128)(2,1)}, u32[]{:S(2)}, u32[]{:S(2)}) collective-permute-start(bf16[64,2560]{1,0:T(8,128)(2,1)} %get-tuple-element.199), channel_id=1, source_target_pairs={{0,24},{1,25},{2,26},{3,27},{4,28},{5,29},{6,30},{7,31},{8,16},{9,... | collective-permute-start | bytes 983048 | tf_op jit(solution)/shard_map/ppermute | solution.py:21
  409.0 29.4 %collective-permute-start.53 = (bf16[64,2560]{1,0:T(8,128)(2,1)}, bf16[64,2560]{1,0:T(8,128)(2,1)}, u32[]{:S(2)}, u32[]{:S(2)}) collective-permute-start(bf16[64,2560]{1,0:T(8,128)(2,1)} %get-tuple-element.200), channel_id=1, source_target_pairs={{0,16},{1,17},{2,18},{3,19},{4,20},{5,21},{6,22},{7,23},{8,24},{9,... | collective-permute-start | bytes 983048 | tf_op jit(solution)/shard_map/ppermute | solution.py:21
  422.0 48.4 %collective-permute-start.58 = (bf16[208,4096]{1,0:T(8,128)(2,1)S(1)}, bf16[208,4096]{1,0:T(8,128)(2,1)S(1)}, u32[]{:S(2)}, u32[]{:S(2)}) collective-permute-start(bf16[208,4096]{1,0:T(8,128)(2,1)S(1)} %copy-done.37), channel_id=1, source_target_pairs={{0,2},{1,3},{2,0},{3,1},{4,6},{5,7},{6,4},{7,5},{8,10},{9,11},{10,... | collective-permute-start | bytes 5111816 | tf_op jit(solution)/shard_map/ppermute | solution.py:21
  443.6 20.4 %collective-permute-start.49 = (bf16[80,1536]{1,0:T(8,128)(2,1)S(1)}, bf16[80,1536]{1,0:T(8,128)(2,1)S(1)}, u32[]{:S(2)}, u32[]{:S(2)}) collective-permute-start(bf16[80,1536]{1,0:T(8,128)(2,1)S(1)} %get-tuple-element.211), channel_id=1, source_target_pairs={{0,16},{1,17},{2,18},{3,19},{4,20},{5,21},{6,22},{7,23},{8,24},{9,... | collective-permute-start | bytes 737288 | tf_op jit(solution)/shard_map/ppermute | solution.py:21
  445.4 18.6 %collective-permute-start.50 = (bf16[80,1536]{1,0:T(8,128)(2,1)S(1)}, bf16[80,1536]{1,0:T(8,128)(2,1)S(1)}, u32[]{:S(2)}, u32[]{:S(2)}) collective-permute-start(bf16[80,1536]{1,0:T(8,128)(2,1)S(1)} %get-tuple-element.212), channel_id=1, source_target_pairs={{0,24},{1,25},{2,26},{3,27},{4,28},{5,29},{6,30},{7,31},{8,16},{9,... | collective-permute-start | bytes 737288 | tf_op jit(solution)/shard_map/ppermute | solution.py:21
  449.6 18.5 %collective-permute-start.56 = (bf16[256,512]{1,0:T(8,128)(2,1)S(1)}, bf16[256,512]{1,0:T(8,128)(2,1)S(1)}, u32[]{:S(2)}, u32[]{:S(2)}) collective-permute-start(bf16[256,512]{1,0:T(8,128)(2,1)S(1)} %slice.219), channel_id=1, source_target_pairs={{0,8},{1,9},{2,10},{3,11},{4,12},{5,13},{6,14},{7,15},{8,0},{9,1},... | collective-permute-start | bytes 786440 | tf_op jit(solution)/shard_map/ppermute | solution.py:21
  (58 other events, 654.2 us)

commit v3 on v2

--- a/solution.py
+++ b/solution.py
@@ -652,8 +652,7 @@
     for step in range(1, n_planes):
         send = total[step * block : (step + 1) * block].astype(BF16)
         if vector is not None:
-            low = jnp.pad(vector, ((0, VECTOR_ROWS - vector.shape[0]), (0, 0))).astype(BF16)
-            send = jnp.concatenate([send, low], axis=0)
+            send = jnp.concatenate([send, vector.astype(BF16)], axis=0)
         got = swap_plane(send, step).astype(F32)
         result = result + got[:block]
         if vector is not None:
@@ -665,9 +664,8 @@
     half = kept.shape[0] // 2
     send = (kept[half:].astype(F32) + got_far[:half].astype(F32)).astype(BF16)
     if vector is not None:
-        vector = vector + got_far[half : half + vector.shape[0]].astype(F32)
-        low = jnp.pad(vector, ((0, VECTOR_ROWS - vector.shape[0]), (0, 0))).astype(BF16)
-        send = jnp.concatenate([send, low], axis=0)
+        vector = vector[:2] + got_far[half : half + 2].astype(F32)
+        send = jnp.concatenate([send, vector.astype(BF16)], axis=0)
     got = swap_first(after(send, *gate) if gate else send).astype(F32)
     if vector is not None:
         vector = vector + got[half : half + vector.shape[0]]

time: 483 us -> 480 us (level)
  no operation moved by 1% of the time
where the time goes in v3:
time: 480 us; the launch traced here: 473 us
  waiting for transfers between devices  213 us (44%)
  Pallas kernels  141 us (29%)
  starting transfers between devices  61.1 us (13%)
  other arithmetic  39.7 us (8%)
  local copies, waits for them, and re-layouts  14.6 us (3%)
    ppermute x59, waiting for transfers between devices, permuted(): lax.ppermute(values, ALL_AXES, [(d, target(d, n_dev)) for d in range(n_de...  190 us
    pallas_call x14, Pallas kernels, run_kernel(): pl.pallas_call(body, name=body_name(body), out_shape=list(outs), in_specs...  141 us
    ppermute x59, starting transfers between devices, permuted(): lax.ppermute(values, ALL_AXES, [(d, target(d, n_dev)) for d in range(n_de...  43.2 us
    all_to_all x4, waiting for transfers between devices, to_expert(): lax.all_to_all(picked.reshape(n_expert, per_dest, features), 'expert', sp...  23.3 us
    all_to_all x4, starting transfers between devices, to_expert(): lax.all_to_all(picked.reshape(n_expert, per_dest, features), 'expert', sp...  18 us
    concatenate x13, other arithmetic, on_device(): join = lambda *v: jnp.concatenate(v, axis=0)  13.2 us
  transfers between devices with their start and end apart: 63, of which 26 were waited for; matrix products, arithmetic and copies ran while one was open for 9% of the time, Pallas kernels for 26%

profile of v3, /device:TPU:0, one launch (start us, length us, event | category | flops | bytes accessed | tf_op | source)
XLA Modules:
  0.0 473.3 jit_solution(12433161927155913649)
XLA Ops:
  5.7 2.7 collective-permute-start.1
  8.5 7.2 %collective-permute-done.1 = bf16[64,2176]{1,0:T(8,128)(2,1)S(1)} collective-permute-done((bf16[64,2176]{1,0:T(8,128)(2,1)S(1)}, bf16[64,2176]{1,0:T(8,128)(2,1)S(1)}, u32[]{:S(2)}, u32[]{:S(2)}) %collective-permute-start.1) | collective-permute-done | bytes 278560 | tf_op jit(solution)/shard_map/ppermute | solution.py:21
  19.5 2.7 collective-permute-start.3
  22.8 18.7 %collective-permute-done.7 = bf16[256,512]{1,0:T(8,128)(2,1)S(1)} collective-permute-done((bf16[256,512]{1,0:T(8,128)(2,1)S(1)}, bf16[256,512]{1,0:T(8,128)(2,1)S(1)}, u32[]{:S(2)}, u32[]{:S(2)}) %collective-permute-start.7) | collective-permute-done | bytes 262176 | tf_op jit(solution)/shard_map/ppermute | solution.py:21
  42.4 3.4 collective-permute-done.3.refs_3_
  48.4 23.9 %collective-permute-done.8.refs_2_ = bf16[256,2176]{1,0:T(8,128)(2,1)S(1)} collective-permute-done((bf16[256,2176]{1,0:T(8,128)(2,1)S(1)}, bf16[256,2176]{1,0:T(8,128)(2,1)S(1)}, u32[]{:S(2)}, u32[]{:S(2)}) %collective-permute-start.8) | collective-permute-done | bytes 1114144 | tf_op jit(solution)/shard_map/ppermute | solution.py:21
  76.4 18.6 %collective-permute-done.12.refs_5_ = bf16[256,2176]{1,0:T(8,128)(2,1)S(1)} collective-permute-done((bf16[256,2176]{1,0:T(8,128)(2,1)S(1)}, bf16[256,2176]{1,0:T(8,128)(2,1)S(1)}, u32[]{:S(2)}, u32[]{:S(2)}) %collective-permute-start.12) | collective-permute-done | bytes 1114144 | tf_op jit(solution)/shard_map/ppermute | solution.py:21
  96.7 5.6 %collective-permute-done.14.refs_3_ = bf16[512,512]{1,0:T(8,128)(2,1)} collective-permute-done((bf16[512,512]{1,0:T(8,128)(2,1)}, bf16[512,512]{1,0:T(8,128)(2,1)}, u32[]{:S(2)}, u32[]{:S(2)}) %collective-permute-start.14) | collective-permute-done | bytes 524320 | tf_op jit(solution)/shard_map/ppermute | solution.py:21
  102.3 3.9 collective-permute-done.15.refs_2_
  113.2 20.4 %collective-permute-done.21.refs_4_ = bf16[512,512]{1,0:T(8,128)(2,1)} collective-permute-done((bf16[512,512]{1,0:T(8,128)(2,1)}, bf16[512,512]{1,0:T(8,128)(2,1)}, u32[]{:S(2)}, u32[]{:S(2)}) %collective-permute-start.21) | collective-permute-done | bytes 524320 | tf_op jit(solution)/shard_map/ppermute | solution.py:21
  133.6 2.2 pad_maximum_fusion.11
  135.9 2.1 pad_maximum_fusion.10
  138.0 2.8 pad_maximum_fusion.3
  142.9 16.0 %attend_kernel.1 = (f32[256,1024]{1,0:T(8,128)}, bf16[256,1024]{1,0:T(8,128)(2,1)}, bf16[256,1024]{1,0:T(8,128)(2,1)}, bf16[256,3072]{1,0:T(8,128)(2,1)}, bf16[256,1024]{1,0:T(8,128)(2,1)}, /*index=5*/f32[8,1024]{1,0:T(8,128)}) custom-call(s32[4]{0:T(128)} %pad_add_fusion.pos, bf16[256,1024]{1,0:T(8,128)(2,1)} %tokens.3, bf16[128,2176]{1,0:T(8,128)(2,1)} %copy-done.21, ...), custom_call_target="tpu_custom_call" | custom-call | flops 80530636800 | bytes 409928160 | tf_op jit(solution)/shard_map/attend_kernel/pallas_call | solution.py:67
  158.9 5.2 %all-to-all-start = ((bf16[8,32,1024]{2,1,0:T(8,128)(2,1)}), bf16[8,32,1024]{2,1,0:T(8,128)(2,1)S(1)}, u32[]{:S(2)}, u32[]{:S(2)}) async-start(bf16[8,32,1024]{2,1,0:T(8,128)(2,1)} %bitcast.7), calls=%async_computation | async-start | bytes 1048576 | tf_op jit(solution)/shard_map/all_to_all | solution.py:714
  164.1 3.0 collective-permute-done.23.refs_2_
  169.2 10.7 %up_kernel.1 = (bf16[256,4096]{1,0:T(8,128)(2,1)}, f32[256,4096]{1,0:T(8,128)}) custom-call(s32[4]{0:T(128)} %pad_add_fusion.pos, bf16[256,1024]{1,0:T(8,128)(2,1)} %get-tuple-element.114.ffn_in.refs_8_, bf16[128,2048]{1,0:T(8,128)(2,1)} %copy-done.31, bf16[128,2048]{1,0:T(8,128)(2,1)} %copy-done.9, bf16[256,2048]{1,0:T(8,128)(2,1)} %copy-done.19, ...), custom_call_target="tpu_custom_call" | custom-call | flops 64424509440 | bytes 456131040 | tf_op jit(solution)/shard_map/up_kernel/pallas_call | solution.py:67
  181.6 7.2 %down_kernel.1 = (f32[256,1024]{1,0:T(8,128)}, bf16[256,1024]{1,0:T(8,128)(2,1)}) custom-call(s32[4]{0:T(128)} %pad_add_fusion.pos, bf16[256,4096]{1,0:T(8,128)(2,1)} %get-tuple-element.120.act.left, f32[256,1024]{1,0:T(8,128)} %get-tuple-element.121.hidden, bf16[256,256]{1,0:T(8,128)(2,1)} %fusion.3.pick, ...), custom_call_target="tpu_custom_call" | custom-call | flops 64424509440 | bytes 397148640 | tf_op jit(solution)/shard_map/down_kernel/pallas_call | solution.py:67
  188.8 5.4 %all-to-all-start.1 = ((bf16[8,32,1024]{2,1,0:T(8,128)(2,1)}), bf16[8,32,1024]{2,1,0:T(8,128)(2,1)S(1)}, u32[]{:S(2)}, u32[]{:S(2)}) async-start(bf16[8,32,1024]{2,1,0:T(8,128)(2,1)} %bitcast.27), calls=%async_computation.1 | async-start | bytes 1048576 | tf_op jit(solution)/shard_map/all_to_all | solution.py:714
  194.3 14.6 %all-to-all-done.1 = bf16[8,32,1024]{2,1,0:T(8,128)(2,1)S(1)} async-done(((bf16[8,32,1024]{2,1,0:T(8,128)(2,1)}), bf16[8,32,1024]{2,1,0:T(8,128)(2,1)S(1)}, u32[]{:S(2)}, u32[]{:S(2)}) %all-to-all-start.1) | async-done | bytes 524320 | tf_op jit(solution)/shard_map/all_to_all | solution.py:714
  209.7 16.5 %expert_kernel.1 = (bf16[256,1024]{1,0:T(8,128)(2,1)}, bf16[256,1024]{1,0:T(8,128)(2,1)}, bf16[256,1024]{1,0:T(8,128)(2,1)}, bf16[256,3072]{1,0:T(8,128)(2,1)}, ...) custom-call(s32[4]{0:T(128)} %pad_add_fusion.pos, ...), custom_call_target="tpu_custom_call" | custom-call | flops 257698037760 | bytes 740352512 | tf_op jit(solution)/shard_map/expert_kernel/pallas_call | solution.py:67
  226.2 3.9 all-to-all-start.2
  230.1 5.4 %copies_send_kernel.1 = bf16[528,4096]{1,0:T(8,128)(2,1)} custom-call(s32[4]{0:T(128)} %pad_add_fusion.pos, bf16[256,1024]{1,0:T(8,128)(2,1)} %get-tuple-element.131.left, bf16[256,4096]{1,0:T(8,128)(2,1)} %get-tuple-element.132.right, f32[8,1024]{1,0:T(8,128)} %get-tuple-element.133.vectors), custom_call_target="tpu_custom_call" | custom-call | flops 32212254720 | bytes 209388000 | tf_op jit(solution)/shard_map/copies_send_kernel/pallas_call | solution.py:67
  236.1 8.6 %all-to-all-done.2 = bf16[8,32,1024]{2,1,0:T(8,128)(2,1)S(1)} async-done(((bf16[8,32,1024]{2,1,0:T(8,128)(2,1)}), bf16[8,32,1024]{2,1,0:T(8,128)(2,1)S(1)}, u32[]{:S(2)}, u32[]{:S(2)}) %all-to-all-start.2) | async-done | bytes 524320 | tf_op jit(solution)/shard_map/all_to_all | solution.py:714
  245.5 6.3 %dense_grad_kernel.1 = (f32[256,1024]{1,0:T(8,128)}, bf16[256,1024]{1,0:T(8,128)(2,1)}, bf16[4096,512]{1,0:T(8,128)(2,1)}) custom-call(s32[4]{0:T(128)} %pad_add_fusion.pos, bf16[256,1024]{1,0:T(8,128)(2,1)} %bitcast.29, bf16[256,1024]{1,0:T(8,128)(2,1)} %cotangent.1, bf16[256,256]{1,0:T(8,128)(2,1)} %fusion.3.pick, ...), custom_call_target="tpu_custom_call" | custom-call | flops 64424509440 | bytes 271319520 | tf_op jit(solution)/shard_map/dense_grad_kernel/pallas_call | solution.py:67
  252.2 8.5 %pre_back_kernel.1.grad_pre = bf16[256,4096]{1,0:T(8,128)(2,1)} custom-call(s32[4]{0:T(128)} %pad_add_fusion.pos, bf16[256,1024]{1,0:T(8,128)(2,1)} %get-tuple-element.139.grad_low.right, f32[256,4096]{1,0:T(8,128)} %get-tuple-element.140.slope, bf16[512,512]{1,0:T(8,128)(2,1)} %constant_dynamic-update-slice_fusion.2.refs_0_, ...), custom_call_target="tpu_custom_call" | custom-call | flops 64424509440 | bytes 456131040 | tf_op jit(solution)/shard_map/pre_back_kernel/pallas_call | solution.py:67
  262.5 4.1 collective-permute-done.30.high
  266.7 7.1 %sum_keep_kernel.1 = (bf16[1024,512]{1,0:T(8,128)(2,1)}, bf16[1024,512]{1,0:T(8,128)(2,1)}, bf16[2048,512]{1,0:T(8,128)(2,1)}) custom-call(s32[4]{0:T(128)} %pad_add_fusion.pos, bf16[256,4096]{1,0:T(8,128)(2,1)} %get-tuple-element.120.act.left, bf16[256,1024]{1,0:T(8,128)(2,1)} %get-tuple-element.139.grad_low.right, ...), custom_call_target="tpu_custom_call" | custom-call | flops 64424509440 | bytes 330301920 | tf_op jit(solution)/shard_map/sum_keep_kernel/pallas_call | solution.py:67
  273.8 6.4 %copies_keep_kernel.1 = (bf16[64,4096]{1,0:T(8,128)(2,1)}, bf16[208,4096]{1,0:T(8,128)(2,1)}, bf16[256,4096]{1,0:T(8,128)(2,1)}, f32[8,1024]{1,0:T(8,128)}) custom-call(s32[4]{0:T(128)} %pad_add_fusion.pos, bf16[256,1024]{1,0:T(8,128)(2,1)} %get-tuple-element.131.left, bf16[256,4096]{1,0:T(8,128)(2,1)} %get-tuple-element.132.right, ...), custom_call_target="tpu_custom_call" | custom-call | flops 32212254720 | bytes 340132320 | tf_op jit(solution)/shard_map/copies_keep_kernel/pallas_call | solution.py:67
  281.0 13.9 %hidden_back_kernel.1 = (f32[256,1024]{1,0:T(8,128)}, bf16[256,1024]{1,0:T(8,128)(2,1)}, f32[8,1024]{1,0:T(8,128)}, bf16[1024,2560]{1,0:T(8,128)(2,1)}) custom-call(s32[4]{0:T(128)} %pad_add_fusion.pos, bf16[256,4096]{1,0:T(8,128)(2,1)} %pre_back_kernel.1.grad_pre, f32[256,1024]{1,0:T(8,128)} %get-tuple-element.121.hidden, ...), custom_call_target="tpu_custom_call" | custom-call | flops 112742891520 | bytes 615383552 | tf_op jit(solution)/shard_map/hidden_back_kernel/pallas_call | solution.py:67
  302.1 17.8 %attend_back_kernel.1 = (bf16[256,3072]{1,0:T(8,128)(2,1)}, f32[256,1024]{1,0:T(8,128)}, f32[8,1024]{1,0:T(8,128)}) custom-call(s32[4]{0:T(128)} %pad_add_fusion.pos, bf16[256,1024]{1,0:T(8,128)(2,1)} %get-tuple-element.160.grad_low, bf16[256,3072]{1,0:T(8,128)(2,1)} %get-tuple-element.161.qkv, bf16[256,1024]{1,0:T(8,128)(2,1)} %tokens.3, ...), custom_call_target="tpu_custom_call" | custom-call | flops 128849018880 | bytes 458097120 | tf_op jit(solution)/shard_map/attend_back_kernel/pallas_call | solution.py:67
  320.7 4.7 collective-permute-done.36
  328.9 11.6 %wide_keep_kernel.1 = (bf16[256,2560]{1,0:T(8,128)(2,1)}, bf16[256,2560]{1,0:T(8,128)(2,1)}, bf16[512,2560]{1,0:T(8,128)(2,1)}, bf16[1040,1536]{1,0:T(8,128)(2,1)}) custom-call(s32[4]{0:T(128)} %pad_add_fusion.pos, bf16[256,1024]{1,0:T(8,128)(2,1)} %get-tuple-element.114.ffn_in.refs_8_, bf16[256,1024]{1,0:T(8,128)(2,1)} %get-tuple-element.156.refs_9_.heads, ...), custom_call_target="tpu_custom_call" | custom-call | flops 80530636800 | bytes 585400832 | tf_op jit(solution)/shard_map/wide_keep_kernel/pallas_call | solution.py:67
  341.9 7.5 %copies_whole_kernel.1 = f32[1024,1024]{1,0:T(8,128)} custom-call(s32[4]{0:T(128)} %pad_add_fusion.pos, bf16[256,3072]{1,0:T(8,128)(2,1)} %get-tuple-element.143.kept, bf16[256,1024]{1,0:T(8,128)(2,1)} %copy-done.26, bf16[256,1024]{1,0:T(8,128)(2,1)} %copy-done.28, bf16[256,1024]{1,0:T(8,128)(2,1)} %copy-done.30, ...), custom_call_target="tpu_custom_call" | custom-call | flops 64424509440 | bytes 314573280 | tf_op jit(solution)/shard_map/copies_whole_kernel/pallas_call | solution.py:67
  349.4 9.0 %collective-permute-done.40 = bf16[256,2560]{1,0:T(8,128)(2,1)S(1)} collective-permute-done((bf16[256,2560]{1,0:T(8,128)(2,1)}, bf16[256,2560]{1,0:T(8,128)(2,1)S(1)}, u32[]{:S(2)}, u32[]{:S(2)}) %collective-permute-start.40) | collective-permute-done | bytes 1310752 | tf_op jit(solution)/shard_map/ppermute | solution.py:21
  359.7 6.2 %last_keep_kernel.1 = (bf16[272,1536]{1,0:T(8,128)(2,1)}, bf16[256,1536]{1,0:T(8,128)(2,1)}, bf16[512,1536]{1,0:T(8,128)(2,1)}, f32[8,1536]{1,0:T(8,128)}) custom-call(s32[4]{0:T(128)} %pad_add_fusion.pos, bf16[256,1024]{1,0:T(8,128)(2,1)} %get-tuple-element.168.attn_in.left, bf16[256,3072]{1,0:T(8,128)(2,1)} %get-tuple-element.163.grad_qkv.right, ...), custom_call_target="tpu_custom_call" | custom-call | flops 32212254720 | bytes 258048480 | tf_op jit(solution)/shard_map/last_keep_kernel/pallas_call | solution.py:67
  369.2 21.4 %collective-permute-done.42 = bf16[512,512]{1,0:T(8,128)(2,1)S(1)} collective-permute-done((bf16[512,512]{1,0:T(8,128)(2,1)S(1)}, bf16[512,512]{1,0:T(8,128)(2,1)S(1)}, u32[]{:S(2)}, u32[]{:S(2)}) %collective-permute-start.42) | collective-permute-done | bytes 524320 | tf_op jit(solution)/shard_map/ppermute | solution.py:21
  391.8 3.5 all-to-all-start.3
  395.3 4.0 collective-permute-done.46
  402.9 2.2 convert_add_fusion
  408.9 2.1 collective-permute-start.53
  413.3 10.3 %collective-permute-done.47 = bf16[258,1536]{1,0:T(8,128)(2,1)} collective-permute-done((bf16[258,1536]{1,0:T(8,128)(2,1)}, bf16[258,1536]{1,0:T(8,128)(2,1)}, u32[]{:S(2)}, u32[]{:S(2)}) %collective-permute-start.47) | collective-permute-done | bytes 792608 | tf_op jit(solution)/shard_map/ppermute | solution.py:21
  426.3 12.1 %collective-permute-done.53 = bf16[64,2560]{1,0:T(8,128)(2,1)} collective-permute-done((bf16[64,2560]{1,0:T(8,128)(2,1)}, bf16[64,2560]{1,0:T(8,128)(2,1)}, u32[]{:S(2)}, u32[]{:S(2)}) %collective-permute-start.53) | collective-permute-done | bytes 327712 | tf_op jit(solution)/shard_map/ppermute | solution.py:21
  444.5 2.6 collective-permute-start.50
  448.8 5.8 %collective-permute-done.48 = bf16[66,1536]{1,0:T(8,128)(2,1)S(1)} collective-permute-done((bf16[66,1536]{1,0:T(8,128)(2,1)S(1)}, bf16[66,1536]{1,0:T(8,128)(2,1)S(1)}, u32[]{:S(2)}, u32[]{:S(2)}) %collective-permute-start.48) | collective-permute-done | bytes 202784 | tf_op jit(solution)/shard_map/ppermute | solution.py:21
  454.6 7.0 %collective-permute-done.49 = bf16[66,1536]{1,0:T(8,128)(2,1)S(1)} collective-permute-done((bf16[66,1536]{1,0:T(8,128)(2,1)S(1)}, bf16[66,1536]{1,0:T(8,128)(2,1)S(1)}, u32[]{:S(2)}, u32[]{:S(2)}) %collective-permute-start.49) | collective-permute-done | bytes 202784 | tf_op jit(solution)/shard_map/ppermute | solution.py:21
  462.4 2.9 collective-permute-done.56
  469.1 3.8 add_bitcast_fusion
  (258 shorter events, 80.1 us)
Async XLA Ops:
  15.7 26.6 %collective-permute-start.2 = (bf16[128,2176]{1,0:T(8,128)(2,1)S(1)}, bf16[128,2176]{1,0:T(8,128)(2,1)S(1)}, u32[]{:S(2)}, u32[]{:S(2)}) collective-permute-start(bf16[128,2176]{1,0:T(8,128)(2,1)S(1)} %pad_maximum_fusion.13.refs_0_), channel_id=1, source_target_pairs={{0,4},{1,3},{2,6},{3,1},{4,0},{5,7},{6,2},{7,5},{8,12},{9,11},{10,... | collective-permute-start | bytes 1671176 | tf_op jit(solution)/shard_map/ppermute | solution.py:21
  17.4 24.8 %collective-permute-start.5 = (bf16[64,2048]{1,0:T(8,128)(2,1)S(1)}, bf16[64,2048]{1,0:T(8,128)(2,1)S(1)}, u32[]{:S(2)}, u32[]{:S(2)}) collective-permute-start(bf16[64,2048]{1,0:T(8,128)(2,1)S(1)} %maximum_select_fusion.4), channel_id=1, source_target_pairs={{0,8},{1,9},{2,10},{3,11},{4,12},{5,13},{6,14},{7,15},{8,0},{9,1},... | collective-permute-start | bytes 786440 | tf_op jit(solution)/shard_map/ppermute | solution.py:21
  19.0 22.6 %collective-permute-start.7 = (bf16[256,512]{1,0:T(8,128)(2,1)S(1)}, bf16[256,512]{1,0:T(8,128)(2,1)S(1)}, u32[]{:S(2)}, u32[]{:S(2)}) collective-permute-start(bf16[256,512]{1,0:T(8,128)(2,1)S(1)} %maximum_select_fusion.5), channel_id=1, source_target_pairs={{0,8},{1,9},{2,10},{3,11},{4,12},{5,13},{6,14},{7,15},{8,0},{9,1},... | collective-permute-start | bytes 786440 | tf_op jit(solution)/shard_map/ppermute | solution.py:21
  19.5 26.4 %collective-permute-start.3 = (bf16[128,2176]{1,0:T(8,128)(2,1)S(1)}, bf16[128,2176]{1,0:T(8,128)(2,1)S(1)}, u32[]{:S(2)}, u32[]{:S(2)}) collective-permute-start(bf16[128,2176]{1,0:T(8,128)(2,1)S(1)} %pad_maximum_fusion.13.refs_0_), channel_id=1, source_target_pairs={{0,16},{1,17},{2,18},{3,19},{4,20},{5,21},{6,22},{7,23},{8,24},{9,... | collective-permute-start | bytes 1671176 | tf_op jit(solution)/shard_map/ppermute | solution.py:21
  45.8 26.5 %collective-permute-start.8 = (bf16[256,2176]{1,0:T(8,128)(2,1)S(1)}, bf16[256,2176]{1,0:T(8,128)(2,1)S(1)}, u32[]{:S(2)}, u32[]{:S(2)}) collective-permute-start(bf16[256,2176]{1,0:T(8,128)(2,1)S(1)} %pad_maximum_fusion.6), channel_id=1, source_target_pairs={{0,2},{1,5},{2,0},{3,7},{4,6},{5,1},{6,4},{7,3},{8,10},{9,13},{10,... | collective-permute-start | bytes 3342344 | tf_op jit(solution)/shard_map/ppermute | solution.py:21
  46.4 27.2 %collective-permute-start.9 = (bf16[128,2176]{1,0:T(8,128)(2,1)S(1)}, bf16[128,2176]{1,0:T(8,128)(2,1)S(1)}, u32[]{:S(2)}, u32[]{:S(2)}) collective-permute-start(bf16[128,2176]{1,0:T(8,128)(2,1)S(1)} %collective-permute-done.3.refs_3_), channel_id=1, source_target_pairs={{0,4},{1,3},{2,6},{3,1},{4,0},{5,7},{6,2},{7,5},{8,12},{9,11},{10,... | collective-permute-start | bytes 1671176 | tf_op jit(solution)/shard_map/ppermute | solution.py:21
  47.8 25.5 %collective-permute-start.11 = (bf16[128,2048]{1,0:T(8,128)(2,1)S(1)}, bf16[128,2048]{1,0:T(8,128)(2,1)S(1)}, u32[]{:S(2)}, u32[]{:S(2)}) collective-permute-start(bf16[128,2048]{1,0:T(8,128)(2,1)S(1)} %constant_dynamic-update-slice_fusion.refs_0_), channel_id=1, source_target_pairs={{0,4},{1,3},{2,6},{3,1},{4,0},{5,7},{6,2},{7,5},{8,12},{9,11},{10,... | collective-permute-start | bytes 1572872 | tf_op jit(solution)/shard_map/ppermute | solution.py:21
  48.4 25.2 %collective-permute-start.10 = (bf16[128,2048]{1,0:T(8,128)(2,1)S(1)}, bf16[128,2048]{1,0:T(8,128)(2,1)S(1)}, u32[]{:S(2)}, u32[]{:S(2)}) collective-permute-start(bf16[128,2048]{1,0:T(8,128)(2,1)S(1)} %constant_dynamic-update-slice_fusion.refs_0_), channel_id=1, source_target_pairs={{0,16},{1,17},{2,18},{3,19},{4,20},{5,21},{6,22},{7,23},{8,24},{9,... | collective-permute-start | bytes 1572872 | tf_op jit(solution)/shard_map/ppermute | solution.py:21
  73.6 32.6 %collective-permute-start.13 = (bf16[512,2176]{1,0:T(8,128)(2,1)S(1)}, bf16[512,2176]{1,0:T(8,128)(2,1)S(1)}, u32[]{:S(2)}, u32[]{:S(2)}) collective-permute-start(bf16[512,2176]{1,0:T(8,128)(2,1)S(1)} %pad_maximum_fusion), channel_id=1, source_target_pairs={{0,1},{1,0},{2,3},{3,2},{4,5},{5,4},{6,7},{7,6},{8,9},{9,8},{10,11... | collective-permute-start | bytes 6684680 | tf_op jit(solution)/shard_map/ppermute | solution.py:21
  73.8 21.2 %collective-permute-start.12 = (bf16[256,2176]{1,0:T(8,128)(2,1)S(1)}, bf16[256,2176]{1,0:T(8,128)(2,1)S(1)}, u32[]{:S(2)}, u32[]{:S(2)}) collective-permute-start(bf16[256,2176]{1,0:T(8,128)(2,1)S(1)} %pad_maximum_fusion.7), channel_id=1, source_target_pairs={{0,2},{1,5},{2,0},{3,7},{4,6},{5,1},{6,4},{7,3},{8,10},{9,13},{10,... | collective-permute-start | bytes 3342344 | tf_op jit(solution)/shard_map/ppermute | solution.py:21
  74.3 31.9 %collective-permute-start.15 = (bf16[256,2048]{1,0:T(8,128)(2,1)S(1)}, bf16[256,2048]{1,0:T(8,128)(2,1)S(1)}, u32[]{:S(2)}, u32[]{:S(2)}) collective-permute-start(bf16[256,2048]{1,0:T(8,128)(2,1)S(1)} %pad_maximum_fusion.8), channel_id=1, source_target_pairs={{0,2},{1,5},{2,0},{3,7},{4,6},{5,1},{6,4},{7,3},{8,10},{9,13},{10,... | collective-permute-start | bytes 3145736 | tf_op jit(solution)/shard_map/ppermute | solution.py:21
  76.1 26.2 %collective-permute-start.14 = (bf16[512,512]{1,0:T(8,128)(2,1)}, bf16[512,512]{1,0:T(8,128)(2,1)}, u32[]{:S(2)}, u32[]{:S(2)}) collective-permute-start(bf16[512,512]{1,0:T(8,128)(2,1)} %constant_dynamic-update-slice_fusion.2.refs_0_), channel_id=1, source_target_pairs={{0,16},{1,17},{2,18},{3,19},{4,20},{5,21},{6,22},{7,23},{8,24},{9,... | collective-permute-start | bytes 1572872 | tf_op jit(solution)/shard_map/ppermute | solution.py:21
  76.1 26.2 %collective-permute-start.16 = (bf16[128,2048]{1,0:T(8,128)(2,1)S(1)}, bf16[128,2048]{1,0:T(8,128)(2,1)S(1)}, u32[]{:S(2)}, u32[]{:S(2)}) collective-permute-start(bf16[128,2048]{1,0:T(8,128)(2,1)S(1)} %collective-permute-done.10.refs_3_), channel_id=1, source_target_pairs={{0,4},{1,3},{2,6},{3,1},{4,0},{5,7},{6,2},{7,5},{8,12},{9,11},{10,... | collective-permute-start | bytes 1572872 | tf_op jit(solution)/shard_map/ppermute | solution.py:21
  106.2 34.5 %collective-permute-start.17 = (bf16[512,2176]{1,0:T(8,128)(2,1)}, bf16[512,2176]{1,0:T(8,128)(2,1)}, u32[]{:S(2)}, u32[]{:S(2)}) collective-permute-start(bf16[512,2176]{1,0:T(8,128)(2,1)} %pad_maximum_fusion.1), channel_id=1, source_target_pairs={{0,1},{1,0},{2,3},{3,2},{4,5},{5,4},{6,7},{7,6},{8,9},{9,8},{10,11... | collective-permute-start | bytes 6684680 | tf_op jit(solution)/shard_map/ppermute | solution.py:21
  106.6 34.2 %collective-permute-start.19 = (bf16[512,2048]{1,0:T(8,128)(2,1)S(1)}, bf16[512,2048]{1,0:T(8,128)(2,1)}, u32[]{:S(2)}, u32[]{:S(2)}) collective-permute-start(bf16[512,2048]{1,0:T(8,128)(2,1)S(1)} %pad_maximum_fusion.2), channel_id=1, source_target_pairs={{0,1},{1,0},{2,3},{3,2},{4,5},{5,4},{6,7},{7,6},{8,9},{9,8},{10,11... | collective-permute-start | bytes 6291464 | tf_op jit(solution)/shard_map/ppermute | solution.py:21
  108.3 29.7 %collective-permute-start.18 = (bf16[256,2048]{1,0:T(8,128)(2,1)}, bf16[256,2048]{1,0:T(8,128)(2,1)}, u32[]{:S(2)}, u32[]{:S(2)}) collective-permute-start(bf16[256,2048]{1,0:T(8,128)(2,1)} %pad_maximum_fusion.9), channel_id=1, source_target_pairs={{0,2},{1,5},{2,0},{3,7},{4,6},{5,1},{6,4},{7,3},{8,10},{9,13},{10,... | collective-permute-start | bytes 3145736 | tf_op jit(solution)/shard_map/ppermute | solution.py:21
  108.6 27.2 %collective-permute-start.20 = (bf16[512,512]{1,0:T(8,128)(2,1)}, bf16[512,512]{1,0:T(8,128)(2,1)}, u32[]{:S(2)}, u32[]{:S(2)}) collective-permute-start(bf16[512,512]{1,0:T(8,128)(2,1)} %constant_dynamic-update-slice_fusion.2.refs_0_), channel_id=1, source_target_pairs={{0,4},{1,3},{2,6},{3,1},{4,0},{5,7},{6,2},{7,5},{8,12},{9,11},{10,... | collective-permute-start | bytes 1572872 | tf_op jit(solution)/shard_map/ppermute | solution.py:21
  109.0 24.7 %collective-permute-start.21 = (bf16[512,512]{1,0:T(8,128)(2,1)}, bf16[512,512]{1,0:T(8,128)(2,1)}, u32[]{:S(2)}, u32[]{:S(2)}) collective-permute-start(bf16[512,512]{1,0:T(8,128)(2,1)} %collective-permute-done.14.refs_3_), channel_id=1, source_target_pairs={{0,4},{1,3},{2,6},{3,1},{4,0},{5,7},{6,2},{7,5},{8,12},{9,11},{10,... | collective-permute-start | bytes 1572872 | tf_op jit(solution)/shard_map/ppermute | solution.py:21
  140.8 39.1 %collective-permute-start.26 = (bf16[1024,512]{1,0:T(8,128)(2,1)}, bf16[1024,512]{1,0:T(8,128)(2,1)}, u32[]{:S(2)}, u32[]{:S(2)}) collective-permute-start(bf16[1024,512]{1,0:T(8,128)(2,1)} %pad_maximum_fusion.11), channel_id=1, source_target_pairs={{0,1},{1,0},{2,3},{3,2},{4,5},{5,4},{6,7},{7,6},{8,9},{9,8},{10,11... | collective-permute-start | bytes 3145736 | tf_op jit(solution)/shard_map/ppermute | solution.py:21
  140.8 27.9 %collective-permute-start.24 = (bf16[1024,512]{1,0:T(8,128)(2,1)}, bf16[1024,512]{1,0:T(8,128)(2,1)}, u32[]{:S(2)}, u32[]{:S(2)}) collective-permute-start(bf16[1024,512]{1,0:T(8,128)(2,1)} %pad_maximum_fusion.11), channel_id=1, source_target_pairs={{0,2},{1,5},{2,0},{3,7},{4,6},{5,1},{6,4},{7,3},{8,10},{9,13},{10,... | collective-permute-start | bytes 3145736 | tf_op jit(solution)/shard_map/ppermute | solution.py:21
  141.2 25.9 %collective-permute-start.23 = (bf16[1024,512]{1,0:T(8,128)(2,1)}, bf16[1024,512]{1,0:T(8,128)(2,1)S(1)}, u32[]{:S(2)}, u32[]{:S(2)}) collective-permute-start(bf16[1024,512]{1,0:T(8,128)(2,1)} %pad_maximum_fusion.10), channel_id=1, source_target_pairs={{0,2},{1,5},{2,0},{3,7},{4,6},{5,1},{6,4},{7,3},{8,10},{9,13},{10,... | collective-permute-start | bytes 3145736 | tf_op jit(solution)/shard_map/ppermute | solution.py:21
  142.9 25.8 %collective-permute-start.22 = (bf16[512,2048]{1,0:T(8,128)(2,1)}, bf16[512,2048]{1,0:T(8,128)(2,1)}, u32[]{:S(2)}, u32[]{:S(2)}) collective-permute-start(bf16[512,2048]{1,0:T(8,128)(2,1)} %pad_maximum_fusion.3), channel_id=1, source_target_pairs={{0,1},{1,0},{2,3},{3,2},{4,5},{5,4},{6,7},{7,6},{8,9},{9,8},{10,11... | collective-permute-start | bytes 6291464 | tf_op jit(solution)/shard_map/ppermute | solution.py:21
  158.9 29.9 %all-to-all-start = ((bf16[8,32,1024]{2,1,0:T(8,128)(2,1)}), bf16[8,32,1024]{2,1,0:T(8,128)(2,1)S(1)}, u32[]{:S(2)}, u32[]{:S(2)}) async-start(bf16[8,32,1024]{2,1,0:T(8,128)(2,1)} %bitcast.7), calls=%async_computation | async-start | bytes 1048576 | tf_op jit(solution)/shard_map/all_to_all | solution.py:714
  188.8 20.1 %all-to-all-start.1 = ((bf16[8,32,1024]{2,1,0:T(8,128)(2,1)}), bf16[8,32,1024]{2,1,0:T(8,128)(2,1)S(1)}, u32[]{:S(2)}, u32[]{:S(2)}) async-start(bf16[8,32,1024]{2,1,0:T(8,128)(2,1)} %bitcast.27), calls=%async_computation.1 | async-start | bytes 1048576 | tf_op jit(solution)/shard_map/all_to_all | solution.py:714
  226.2 18.5 %all-to-all-start.2 = ((bf16[8,32,1024]{2,1,0:T(8,128)(2,1)}), bf16[8,32,1024]{2,1,0:T(8,128)(2,1)S(1)}, u32[]{:S(2)}, u32[]{:S(2)}) async-start(bf16[8,32,1024]{2,1,0:T(8,128)(2,1)} %bitcast.28), calls=%async_computation.2 | async-start | bytes 1048576 | tf_op jit(solution)/shard_map/all_to_all | solution.py:714
  235.8 30.9 %collective-permute-start.31 = (bf16[256,3072]{1,0:T(8,128)(2,1)S(1)}, bf16[256,3072]{1,0:T(8,128)(2,1)}, u32[]{:S(2)}, u32[]{:S(2)}) collective-permute-start(bf16[256,3072]{1,0:T(8,128)(2,1)S(1)} %copy-done.38), channel_id=1, source_target_pairs={{0,1},{1,0},{2,3},{3,2},{4,5},{5,4},{6,7},{7,6},{8,9},{9,8},{10,11... | collective-permute-start | bytes 4718600 | tf_op jit(solution)/shard_map/ppermute | solution.py:21
  260.7 19.4 %collective-permute-start.35 = (bf16[256,1024]{1,0:T(8,128)(2,1)S(1)}, bf16[256,1024]{1,0:T(8,128)(2,1)S(1)}, u32[]{:S(2)}, u32[]{:S(2)}) collective-permute-start(bf16[256,1024]{1,0:T(8,128)(2,1)S(1)} %copy-done.40), channel_id=1, source_target_pairs={{0,2},{1,3},{2,0},{3,1},{4,6},{5,7},{6,4},{7,5},{8,10},{9,11},{10,... | collective-permute-start | bytes 1572872 | tf_op jit(solution)/shard_map/ppermute | solution.py:21
  280.2 17.9 %collective-permute-start.33 = (bf16[1024,512]{1,0:T(8,128)(2,1)}, bf16[1024,512]{1,0:T(8,128)(2,1)S(1)}, u32[]{:S(2)}, u32[]{:S(2)}) collective-permute-start(bf16[1024,512]{1,0:T(8,128)(2,1)} %get-tuple-element.147), channel_id=1, source_target_pairs={{0,2},{1,5},{2,0},{3,7},{4,6},{5,1},{6,4},{7,3},{8,10},{9,13},{10,... | collective-permute-start | bytes 3145736 | tf_op jit(solution)/shard_map/ppermute | solution.py:21
  294.9 33.9 %collective-permute-start.38 = (bf16[1024,2560]{1,0:T(8,128)(2,1)}, bf16[1024,2560]{1,0:T(8,128)(2,1)}, u32[]{:S(2)}, u32[]{:S(2)}) collective-permute-start(bf16[1024,2560]{1,0:T(8,128)(2,1)} %get-tuple-element.157), channel_id=1, source_target_pairs={{0,1},{1,0},{2,3},{3,2},{4,5},{5,4},{6,7},{7,6},{8,9},{9,8},{10,11... | collective-permute-start | bytes 15728648 | tf_op jit(solution)/shard_map/ppermute | solution.py:21
  297.7 31.2 %collective-permute-start.37 = (bf16[768,1024]{1,0:T(8,128)(2,1)S(1)}, bf16[768,1024]{1,0:T(8,128)(2,1)}, u32[]{:S(2)}, u32[]{:S(2)}) collective-permute-start(bf16[768,1024]{1,0:T(8,128)(2,1)S(1)} %pad_maximum_fusion.5), channel_id=1, source_target_pairs={{0,1},{1,0},{2,3},{3,2},{4,5},{5,4},{6,7},{7,6},{8,9},{9,8},{10,11... | collective-permute-start | bytes 4718600 | tf_op jit(solution)/shard_map/ppermute | solution.py:21
  299.3 26.0 %collective-permute-start.36 = (bf16[1024,512]{1,0:T(8,128)(2,1)}, bf16[1024,512]{1,0:T(8,128)(2,1)S(1)}, u32[]{:S(2)}, u32[]{:S(2)}) collective-permute-start(bf16[1024,512]{1,0:T(8,128)(2,1)} %add_convert_fusion.1), channel_id=1, source_target_pairs={{0,4},{1,3},{2,6},{3,1},{4,0},{5,7},{6,2},{7,5},{8,12},{9,11},{10,... | collective-permute-start | bytes 3145736 | tf_op jit(solution)/shard_map/ppermute | solution.py:21
  300.8 26.3 %collective-permute-start.34 = (bf16[1024,512]{1,0:T(8,128)(2,1)}, bf16[1024,512]{1,0:T(8,128)(2,1)S(1)}, u32[]{:S(2)}, u32[]{:S(2)}) collective-permute-start(bf16[1024,512]{1,0:T(8,128)(2,1)} %get-tuple-element.148), channel_id=1, source_target_pairs={{0,2},{1,5},{2,0},{3,7},{4,6},{5,1},{6,4},{7,3},{8,10},{9,13},{10,... | collective-permute-start | bytes 3145736 | tf_op jit(solution)/shard_map/ppermute | solution.py:21
  319.9 20.6 %collective-permute-start.39 = (bf16[64,4096]{1,0:T(8,128)(2,1)}, bf16[64,4096]{1,0:T(8,128)(2,1)}, u32[]{:S(2)}, u32[]{:S(2)}) collective-permute-start(bf16[64,4096]{1,0:T(8,128)(2,1)} %get-tuple-element.173), channel_id=1, source_target_pairs={{0,2},{1,3},{2,0},{3,1},{4,6},{5,7},{6,4},{7,5},{8,10},{9,11},{10,... | collective-permute-start | bytes 1572872 | tf_op jit(solution)/shard_map/ppermute | solution.py:21
  340.4 19.3 %collective-permute-start.41 = (bf16[1040,1536]{1,0:T(8,128)(2,1)}, bf16[1040,1536]{1,0:T(8,128)(2,1)}, u32[]{:S(2)}, u32[]{:S(2)}) collective-permute-start(bf16[1040,1536]{1,0:T(8,128)(2,1)} %get-tuple-element.171), channel_id=1, source_target_pairs={{0,1},{1,0},{2,3},{3,2},{4,5},{5,4},{6,7},{7,6},{8,9},{9,8},{10,11... | collective-permute-start | bytes 9584648 | tf_op jit(solution)/shard_map/ppermute | solution.py:21
  340.5 17.9 %collective-permute-start.40 = (bf16[256,2560]{1,0:T(8,128)(2,1)}, bf16[256,2560]{1,0:T(8,128)(2,1)S(1)}, u32[]{:S(2)}, u32[]{:S(2)}) collective-permute-start(bf16[256,2560]{1,0:T(8,128)(2,1)} %get-tuple-element.175), channel_id=1, source_target_pairs={{0,2},{1,5},{2,0},{3,7},{4,6},{5,1},{6,4},{7,3},{8,10},{9,13},{10,... | collective-permute-start | bytes 3932168 | tf_op jit(solution)/shard_map/ppermute | solution.py:21
  358.4 44.5 %collective-permute-start.43 = (bf16[256,2560]{1,0:T(8,128)(2,1)}, bf16[256,2560]{1,0:T(8,128)(2,1)}, u32[]{:S(2)}, u32[]{:S(2)}) collective-permute-start(bf16[256,2560]{1,0:T(8,128)(2,1)} %get-tuple-element.184), channel_id=1, source_target_pairs={{0,2},{1,5},{2,0},{3,7},{4,6},{5,1},{6,4},{7,3},{8,10},{9,13},{10,... | collective-permute-start | bytes 3932168 | tf_op jit(solution)/shard_map/ppermute | solution.py:21
  366.0 24.6 %collective-permute-start.42 = (bf16[512,512]{1,0:T(8,128)(2,1)S(1)}, bf16[512,512]{1,0:T(8,128)(2,1)S(1)}, u32[]{:S(2)}, u32[]{:S(2)}) collective-permute-start(bf16[512,512]{1,0:T(8,128)(2,1)S(1)} %slice.230), channel_id=1, source_target_pairs={{0,16},{1,17},{2,18},{3,19},{4,20},{5,21},{6,22},{7,23},{8,24},{9,... | collective-permute-start | bytes 1572872 | tf_op jit(solution)/shard_map/ppermute | solution.py:21
  366.1 33.2 %collective-permute-start.46 = (bf16[272,1536]{1,0:T(8,128)(2,1)}, bf16[272,1536]{1,0:T(8,128)(2,1)}, u32[]{:S(2)}, u32[]{:S(2)}) collective-permute-start(bf16[272,1536]{1,0:T(8,128)(2,1)} %get-tuple-element.187), channel_id=1, source_target_pairs={{0,2},{1,5},{2,0},{3,7},{4,6},{5,1},{6,4},{7,3},{8,10},{9,13},{10,... | collective-permute-start | bytes 2506760 | tf_op jit(solution)/shard_map/ppermute | solution.py:21
  368.6 34.3 %collective-permute-start.44 = (bf16[256,2560]{1,0:T(8,128)(2,1)}, bf16[256,2560]{1,0:T(8,128)(2,1)}, u32[]{:S(2)}, u32[]{:S(2)}) collective-permute-start(bf16[256,2560]{1,0:T(8,128)(2,1)} %add_convert_fusion), channel_id=1, source_target_pairs={{0,4},{1,3},{2,6},{3,1},{4,0},{5,7},{6,2},{7,5},{8,12},{9,11},{10,... | collective-permute-start | bytes 3932168 | tf_op jit(solution)/shard_map/ppermute | solution.py:21
  391.8 19.3 %all-to-all-start.3 = ((bf16[8,32,1024]{2,1,0:T(8,128)(2,1)}), bf16[8,32,1024]{2,1,0:T(8,128)(2,1)S(1)}, u32[]{:S(2)}, u32[]{:S(2)}) async-start(bf16[8,32,1024]{2,1,0:T(8,128)(2,1)} %bitcast.13), calls=%async_computation.3 | async-start | bytes 1048576 | tf_op jit(solution)/shard_map/all_to_all | solution.py:714
  402.3 21.2 %collective-permute-start.47 = (bf16[258,1536]{1,0:T(8,128)(2,1)}, bf16[258,1536]{1,0:T(8,128)(2,1)}, u32[]{:S(2)}, u32[]{:S(2)}) collective-permute-start(bf16[258,1536]{1,0:T(8,128)(2,1)} %pad_maximum_fusion.12), channel_id=1, source_target_pairs={{0,4},{1,3},{2,6},{3,1},{4,0},{5,7},{6,2},{7,5},{8,12},{9,11},{10,... | collective-permute-start | bytes 2377736 | tf_op jit(solution)/shard_map/ppermute | solution.py:21
  405.1 36.0 %collective-permute-start.45 = (bf16[256,1536]{1,0:T(8,128)(2,1)}, bf16[256,1536]{1,0:T(8,128)(2,1)}, u32[]{:S(2)}, u32[]{:S(2)}) collective-permute-start(bf16[256,1536]{1,0:T(8,128)(2,1)} %get-tuple-element.186), channel_id=1, source_target_pairs={{0,2},{1,5},{2,0},{3,7},{4,6},{5,1},{6,4},{7,3},{8,10},{9,13},{10,... | collective-permute-start | bytes 2359304 | tf_op jit(solution)/shard_map/ppermute | solution.py:21
  407.5 18.7 %collective-permute-start.52 = (bf16[64,2560]{1,0:T(8,128)(2,1)}, bf16[64,2560]{1,0:T(8,128)(2,1)S(1)}, u32[]{:S(2)}, u32[]{:S(2)}) collective-permute-start(bf16[64,2560]{1,0:T(8,128)(2,1)} %get-tuple-element.198), channel_id=1, source_target_pairs={{0,8},{1,9},{2,10},{3,11},{4,12},{5,13},{6,14},{7,15},{8,0},{9,1},... | collective-permute-start | bytes 983048 | tf_op jit(solution)/shard_map/ppermute | solution.py:21
  408.0 18.2 %collective-permute-start.54 = (bf16[64,2560]{1,0:T(8,128)(2,1)}, bf16[64,2560]{1,0:T(8,128)(2,1)}, u32[]{:S(2)}, u32[]{:S(2)}) collective-permute-start(bf16[64,2560]{1,0:T(8,128)(2,1)} %get-tuple-element.199), channel_id=1, source_target_pairs={{0,24},{1,25},{2,26},{3,27},{4,28},{5,29},{6,30},{7,31},{8,16},{9,... | collective-permute-start | bytes 983048 | tf_op jit(solution)/shard_map/ppermute | solution.py:21
  408.9 29.4 %collective-permute-start.53 = (bf16[64,2560]{1,0:T(8,128)(2,1)}, bf16[64,2560]{1,0:T(8,128)(2,1)}, u32[]{:S(2)}, u32[]{:S(2)}) collective-permute-start(bf16[64,2560]{1,0:T(8,128)(2,1)} %get-tuple-element.200), channel_id=1, source_target_pairs={{0,16},{1,17},{2,18},{3,19},{4,20},{5,21},{6,22},{7,23},{8,24},{9,... | collective-permute-start | bytes 983048 | tf_op jit(solution)/shard_map/ppermute | solution.py:21
  423.6 44.1 %collective-permute-start.58 = (bf16[208,4096]{1,0:T(8,128)(2,1)S(1)}, bf16[208,4096]{1,0:T(8,128)(2,1)S(1)}, u32[]{:S(2)}, u32[]{:S(2)}) collective-permute-start(bf16[208,4096]{1,0:T(8,128)(2,1)S(1)} %copy-done.37), channel_id=1, source_target_pairs={{0,2},{1,3},{2,0},{3,1},{4,6},{5,7},{6,4},{7,5},{8,10},{9,11},{10,... | collective-permute-start | bytes 5111816 | tf_op jit(solution)/shard_map/ppermute | solution.py:21
  442.7 18.8 %collective-permute-start.49 = (bf16[66,1536]{1,0:T(8,128)(2,1)S(1)}, bf16[66,1536]{1,0:T(8,128)(2,1)S(1)}, u32[]{:S(2)}, u32[]{:S(2)}) collective-permute-start(bf16[66,1536]{1,0:T(8,128)(2,1)S(1)} %get-tuple-element.211), channel_id=1, source_target_pairs={{0,16},{1,17},{2,18},{3,19},{4,20},{5,21},{6,22},{7,23},{8,24},{9,... | collective-permute-start | bytes 608264 | tf_op jit(solution)/shard_map/ppermute | solution.py:21
  444.5 17.1 %collective-permute-start.50 = (bf16[66,1536]{1,0:T(8,128)(2,1)S(1)}, bf16[66,1536]{1,0:T(8,128)(2,1)S(1)}, u32[]{:S(2)}, u32[]{:S(2)}) collective-permute-start(bf16[66,1536]{1,0:T(8,128)(2,1)S(1)} %get-tuple-element.212), channel_id=1, source_target_pairs={{0,24},{1,25},{2,26},{3,27},{4,28},{5,29},{6,30},{7,31},{8,16},{9,... | collective-permute-start | bytes 608264 | tf_op jit(solution)/shard_map/ppermute | solution.py:21
  (58 other events, 669.2 us)
